TPU v7x, 32 devices: a whole 2x2x4 slice. The times are simulated.
32 devices in a mesh: col: 4 (over x, core), af: 8 (over z, y).
Axes of the slice: x: 2, y: 2, z: 4, core: 2. Of those that a mesh axis runs over, the one named last changes fastest.
Arguments:
- coarse_state: float32 [3, 8, 128, 1024], P(None, None, 'af', 'col'), may hold values from 0.1 to 2
- coarse_kappa: float32 [8, 128, 1024], P(None, 'af', 'col'), may hold values from 0.25 to 1
- coarse_rate: float32 [8, 128, 1024], P(None, 'af', 'col'), may hold values from 0.5 to 6
- fine_state: float32 [128, 3, 32, 1024], P(('col', 'af')), may hold values from 0.1 to 2
- fine_kappa: float32 [128, 32, 1024], P(('col', 'af')), may hold values from 0.25 to 1
- fine_rate: float32 [128, 32, 1024], P(('col', 'af')), may hold values from 0.5 to 6
- boxes: int32 [128, 2], replicated, may hold values from 0 to 127, as said below
- cover: int32 [16, 128], replicated, may hold values from -1 to 127, as said below
Outputs:
- coarse_out: float32 [3, 8, 128, 1024], P(None, None, 'af', 'col')
- fine_out: float32 [128, 3, 32, 1024], P(('col', 'af'))
Inputs may be any that keep to these rules, and one draw needn't show every extreme that they name: `boxes`: A patch's block spans all 8 planes; it lies in the 32 block rows of one col index, never in the first or last of them nor in the slab's first or last block column, and no two patches share a face. The patches whose blocks lie in one col index's rows are the rows of the fine arrays held by that col index, in no particular order. The 2 block columns of one af index hold at most 10 patches, and in every col index some af index holds exactly that many. cover[bx, by] is the patch whose block is (bx, by), or -1 where none is; it agrees with boxes, and every patch appears once.
All inputs are finite; a program needn't handle non-finite values.
Results may differ from a plain program's by a relative error of at most 0.0003.
Values sent between devices are 32-bit elements; how exact they have to be, the bound alone decides.
No kernel may reach another device: no remote copies, remote signals or barrier semaphores. Data moves between devices by JAX's collectives and lax.ppermute only.
A program may use at most 192 MiB of HBM per device.

v0:
```python
import functools

import jax
import jax.numpy as jnp
from jax import lax
from jax.experimental import pallas as pl
from jax.experimental.pallas import tpu as pltpu
from jax.sharding import PartitionSpec as P

NZC = 8
RATIO = 4
BLK = 8
SPECIES = 3
EDGE = BLK * RATIO
FZ = NZC * RATIO
LANES = 128
TILES = EDGE * EDGE // LANES
ZTILES = FZ // 8
STRIDE = 48
PAD = 8
FACES = 4
PLANES = SPECIES * NZC
STRIP_ROWS = 2 * PLANES
AVG_ROWS = PLANES * BLK
KINDS = 9
FIELD_ROWS = SPECIES * TILES * STRIDE
COEFF_ROWS = KINDS * TILES * FZ
UPWARD_ROWS = TILES * STRIDE
EDGE_ROWS = PLANES + NZC
HALO_START = STRIP_ROWS + EDGE_ROWS

DT_COARSE = 1.0 / 28.0
DIFFUSE = (1.0, 0.7, 0.45)
SIGNS = (-1.0, -1.0, 1.0)
FINE_SCALE = RATIO * RATIO * DT_COARSE / RATIO
DT_FINE = DT_COARSE / RATIO


def lane_ids(shape):
    return lax.broadcasted_iota(jnp.int32, shape, len(shape) - 1)


def roll_lanes(values, shift):
    width = values.shape[-1]
    shift = shift % width
    return values if shift == 0 else pltpu.roll(values, shift, values.ndim - 1)


def split_pair(values):
    high = values.astype(jnp.bfloat16)
    low = (values - high.astype(jnp.float32)).astype(jnp.bfloat16)
    return high, low


def face(scale, one, other):
    summed = one + other
    inverse = pl.reciprocal(summed, approx=True)
    inverse = inverse * (2.0 - summed * inverse)
    return (2.0 * scale) * (one * other) * inverse


def start_all(copies):
    for copy in copies:
        copy.start()


def selector(place_ref, column, cells_y):
    wanted = jnp.where(place_ref[0:8, :] == column, place_ref[8:16, :], -1)
    row = lax.broadcasted_iota(jnp.int32, wanted.shape, 0)
    return jnp.concatenate(
        [jnp.where(row + 8 * at == wanted, 1.0, 0.0) for at in range(cells_y // 8)], axis=0
    ).astype(jnp.bfloat16)


def strips_kernel(
    boxes_hbm,
    state_hbm,
    kappa_hbm,
    rate_hbm,
    new_hbm,
    send_ref,
    place_ref,
    xlo_ref,
    xhi_ref,
    ylo_ref,
    yhi_ref,
    boxes_ref,
    state_ref,
    kappa_ref,
    rate_ref,
    new_ref,
    padded,
    fresh,
    sems,
    *,
    cells_x,
    cells_y,
    group,
    slots,
):
    pairs = (
        (boxes_hbm, boxes_ref),
        (kappa_hbm, kappa_ref),
        (state_hbm, state_ref),
        (rate_hbm, rate_ref),
    )
    copies = [
        pltpu.make_async_copy(source, target, sems.at[index])
        for index, (source, target) in enumerate(pairs)
    ]
    start_all(copies)

    patches = boxes_ref.shape[1]
    lanes = group * BLK
    base_patch = lax.axis_index("col") * group
    member = lax.broadcasted_iota(jnp.int32, (patches, lanes), 0) - base_patch
    spread = jnp.where(member == lane_ids((patches, lanes)) // BLK, 1.0, 0.0).astype(jnp.bfloat16)
    first_col = lax.axis_index("af") * (cells_x // BLK)
    first_cell = lax.axis_index("col") * cells_y
    copies[0].wait()
    boxes = boxes_ref[...].astype(jnp.float32)
    stacked = jnp.concatenate(
        [jnp.broadcast_to(boxes[row : row + 1], (8, patches)) for row in range(2)], axis=0
    )
    found = jnp.dot(
        stacked.astype(jnp.bfloat16), spread, preferred_element_type=jnp.float32
    ).astype(jnp.int32)
    place_ref[0:8, :] = found[0:8] - first_col
    place_ref[8:16, :] = found[8:16] * BLK - first_cell + lane_ids((8, lanes)) % BLK

    halves = cells_y // LANES
    span = cells_x + 2 * PAD
    nothing = jnp.zeros((PAD, LANES), jnp.float32)

    def base(field, half, z):
        return ((field * halves + half) * NZC + z) * span

    for copy in copies[1:]:
        copy.wait()
    for field in range(SPECIES + 1):
        for half in range(halves):
            cols = pl.ds(half * LANES, LANES)
            for z in range(NZC):
                if field < SPECIES:
                    start = (field * NZC + z) * cells_x
                    plane = state_ref[start : start + cells_x, cols]
                else:
                    plane = kappa_ref[z * cells_x : (z + 1) * cells_x, cols]
                at = base(field, half, z)
                padded[at : at + PAD, :] = nothing
                padded[at + PAD : at + PAD + cells_x, :] = plane
                padded[at + PAD + cells_x : at + span, :] = nothing

    lane = lane_ids((cells_x, LANES))
    row_id = lax.broadcasted_iota(jnp.int32, (cells_x, LANES), 0)

    low = jnp.zeros((cells_x, LANES), jnp.float32)
    high = jnp.zeros((cells_x, LANES), jnp.float32)
    for plane in range(PLANES + NZC):
        field, z = divmod(plane, NZC)
        at = base(field, 0, z) + PAD
        first = padded[at : at + cells_x, :]
        at = base(field, halves - 1, z) + PAD
        last = padded[at : at + cells_x, :]
        low = jnp.where(lane == plane, roll_lanes(first, plane), low)
        high = jnp.where(lane == plane, roll_lanes(last, plane + 1), high)
    ylo_ref[...] = low
    yhi_ref[...] = high

    def load(field, half, z, shift):
        at = base(field, half, z) + PAD + shift
        return padded[at : at + cells_x, :]

    def neighbours(field, half, z):
        here = load(field, half, z, 0)
        after = roll_lanes(here, -1)
        if half + 1 < halves:
            after = jnp.where(
                lane == LANES - 1, roll_lanes(load(field, half + 1, z, 0), -1), after
            )
        before = roll_lanes(here, 1)
        if half > 0:
            before = jnp.where(lane == 0, roll_lanes(load(field, half - 1, z, 0), 1), before)
        found = [after, before, load(field, half, z, 1), load(field, half, z, -1)]
        if z + 1 < NZC:
            found.append(load(field, half, z + 1, 0))
        if z > 0:
            found.append(load(field, half, z - 1, 0))
        return found

    for z in range(NZC):
        for half in range(halves):
            cols = pl.ds(half * LANES, LANES)
            conduct = load(SPECIES, half, z, 0)
            coeffs = [face(DT_COARSE, conduct, other) for other in neighbours(SPECIES, half, z)]
            if half == halves - 1:
                coeffs[0] = jnp.where(lane == LANES - 1, 0.0, coeffs[0])
            if half == 0:
                coeffs[1] = jnp.where(lane == 0, 0.0, coeffs[1])
            coeffs[2] = jnp.where(row_id == cells_x - 1, 0.0, coeffs[2])
            coeffs[3] = jnp.where(row_id == 0, 0.0, coeffs[3])
            centers = [load(field, half, z, 0) for field in range(SPECIES)]
            forward = (DT_COARSE * rate_ref[z * cells_x : (z + 1) * cells_x, cols]) * (
                centers[0] * centers[1] - centers[2]
            )
            for field in range(SPECIES):
                center = centers[field]
                flux = None
                for coeff, other in zip(coeffs, neighbours(field, half, z)):
                    term = coeff * (other - center)
                    flux = term if flux is None else flux + term
                start = (field * NZC + z) * cells_x
                result = center + DIFFUSE[field] * flux + SIGNS[field] * forward
                new_ref[start : start + cells_x, cols] = result
                start = ((field * halves + half) * NZC + z) * cells_x
                fresh[start : start + cells_x, :] = result

    keep_new = pltpu.make_async_copy(new_ref, new_hbm, sems.at[0])
    keep_new.start()

    def old_row(field, half, row):
        return padded[pl.ds(base(field, half, 0) + PAD + row, NZC, stride=span), :]

    def edge_at(row):
        return jnp.concatenate(
            [
                jnp.concatenate([old_row(field, half, row) for field in range(SPECIES + 1)], axis=0)
                for half in range(halves)
            ],
            axis=1,
        )

    def rows_at(row):
        columns = []
        for half in range(halves):
            pieces = [old_row(field, half, row) for field in range(SPECIES)]
            for field in range(SPECIES):
                start = (field * halves + half) * NZC * cells_x
                pieces.append(fresh[pl.ds(start + row, NZC, stride=cells_x), :])
            columns.append(jnp.concatenate(pieces, axis=0))
        return jnp.concatenate(columns, axis=1)

    block_cols = cells_x // BLK
    spot = lane_ids((STRIP_ROWS, cells_y)) % BLK
    lower_y = []
    upper_y = []
    for column in range(block_cols):
        below = jnp.zeros((STRIP_ROWS, cells_y), jnp.float32)
        above = jnp.zeros((STRIP_ROWS, cells_y), jnp.float32)
        for x in range(BLK):
            strip = rows_at(column * BLK + x)
            below = jnp.where(spot == x, roll_lanes(strip, x + 1), below)
            above = jnp.where(spot == x, roll_lanes(strip, x - BLK), above)
        lower_y.append(below)
        upper_y.append(above)

    first_row = edge_at(0)
    last_row = edge_at(cells_x - 1)
    xlo_ref[...] = first_row
    xhi_ref[...] = last_row
    place = lane_ids((EDGE_ROWS, cells_y)) % BLK

    def corners(row, at):
        below = jnp.where(place == at, roll_lanes(row, at + 1), 0.0)
        return jnp.where(place == at + 1, roll_lanes(row, at + 1 - BLK), below)

    extra_members = {
        -1: [(1, first_row), (2, corners(first_row, 2))],
        0: [(0, first_row), (2, corners(first_row, 0))],
        block_cols - 1: [
            (0, last_row),
            (2, corners(last_row, 0)),
            (3, jnp.ones((EDGE_ROWS, cells_y), jnp.float32)),
        ],
        block_cols: [(1, last_row), (2, corners(last_row, 2))],
    }

    faces = [None] * (2 * FACES)

    def add(index, part):
        faces[index] = part if faces[index] is None else faces[index] + part

    for column in range(-1, block_cols + 1):
        members = []
        if column >= 1:
            members.append((0, rows_at(column * BLK - 1)))
        if column < block_cols - 1:
            members.append((1, rows_at(column * BLK + BLK)))
        if 0 <= column < block_cols:
            members.append((2, lower_y[column]))
            members.append((3, upper_y[column]))
        for index, rows in extra_members.get(column, []):
            members.append((FACES + index, rows))
        operands = []
        for _, rows in members:
            operands.extend(split_pair(rows))
        moved = jnp.dot(
            jnp.concatenate(operands, axis=0),
            selector(place_ref, column, cells_y),
            preferred_element_type=jnp.float32,
        )
        at = 0
        for index, rows in members:
            size = rows.shape[0]
            add(index, moved[at : at + size] + moved[at + size : at + 2 * size])
            at += 2 * size

    width = slots * BLK
    me = lax.axis_index("af")
    for target in range(group // slots):
        first = target * width
        tile = first // LANES * LANES
        for start, size, kind in ((0, STRIP_ROWS, 0), (STRIP_ROWS, EDGE_ROWS, FACES)):
            part = lane_ids((size, LANES)) // width
            chunk = jnp.zeros((size, LANES), jnp.float32)
            for index in range(FACES):
                piece = faces[kind + index][:, tile : tile + LANES]
                chunk = jnp.where(
                    part == index, roll_lanes(piece, index * width - (first - tile)), chunk
                )
            send_ref[target, start : start + size, :] = chunk
        halo = jnp.where(me < target, last_row, first_row)
        for half in range(halves):
            start = HALO_START + half * EDGE_ROWS
            send_ref[target, start : start + EDGE_ROWS, :] = halo[
                :, half * LANES : (half + 1) * LANES
            ]
    keep_new.wait()


def ghost_table(tile):
    lane = lane_ids((BLK, LANES))
    pos = lax.broadcasted_iota(jnp.int32, (BLK, LANES), 0)
    x = tile * (LANES // EDGE) + lane // EDGE
    y = lane % EDGE
    along_y = y // RATIO == pos
    along_x = x // RATIO == pos
    seen = (
        (x == 0) & along_y,
        (x == EDGE - 1) & along_y,
        (y == 0) & along_x,
        (y == EDGE - 1) & along_x,
    )
    nothing = jnp.zeros((LANES // FACES - BLK, LANES), jnp.float32)
    rows = []
    for where in seen:
        rows.extend([jnp.where(where, 1.0, 0.0), nothing])
    return jnp.concatenate(rows + rows, axis=0).astype(jnp.bfloat16)


def plane_table():
    shape = (2 * SPECIES * FZ, STRIP_ROWS)
    rows = lax.broadcasted_iota(jnp.int32, shape, 0)
    return jnp.where(rows // RATIO == lane_ids(shape), 1.0, 0.0).astype(jnp.bfloat16)


def mean_table():
    shape = (2 * LANES, LANES)
    rows = lax.broadcasted_iota(jnp.int32, shape, 0)
    same = rows % EDGE // RATIO == lane_ids(shape) % BLK
    return jnp.where(same, 1.0 / RATIO**3, 0.0).astype(jnp.bfloat16)


def complete_strips(gathered):
    width = LANES // FACES
    beside = [
        gathered[STRIP_ROWS + field * NZC : STRIP_ROWS + (field + 1) * NZC]
        for field in range(SPECIES + 1)
    ]
    lane = lane_ids((NZC, LANES))
    part = lane // width
    pos = lane % BLK
    flag = jnp.where(part == FACES - 1, beside[0], 0.0)
    flag = flag + roll_lanes(flag, width)
    upper = flag + roll_lanes(flag, 2 * width) > 0.5
    conduct = jnp.maximum(beside[SPECIES], 0.125)
    block = face(DT_COARSE, conduct, roll_lanes(conduct, -width))
    corner = face(DT_COARSE, conduct, roll_lanes(conduct, -2))
    nothing = jnp.zeros((NZC, LANES), jnp.float32)
    added = []
    for field in range(SPECIES):
        values = beside[field]
        across = DIFFUSE[field] * block * (values - roll_lanes(values, -width))
        along = DIFFUSE[field] * corner * (roll_lanes(values, -2) - values)
        share = jnp.where((part == 0) & ~upper, across, nothing)
        share = jnp.where((part == 1) & upper, roll_lanes(across, width), share)
        for index in range(2):
            home = 2 + index
            for at, chosen in ((0, ~upper), (BLK - 1, upper)):
                moved = roll_lanes(along, index * width + at - index)
                share = jnp.where((part == home) & (pos == at) & chosen, moved, share)
        added.append(share)
    new = gathered[PLANES:STRIP_ROWS] + jnp.concatenate(added, axis=0)
    return gathered[:PLANES], new


def aligned(start, size):
    return pl.ds(pl.multiple_of(start, 8), size)


def padded_at(block, ztile):
    return block * STRIDE + PAD + 8 * ztile


def advance(source, target, coeffs, upward, slot, from_rows, to_rows, ztile, ghosts):
    lane = lane_ids((8, LANES))

    def value(field, tile, shift):
        return source[pl.ds(from_rows + padded_at(field * TILES + tile, ztile) + shift, 8), :]

    def get(kind, tile):
        return coeffs[
            aligned(slot * COEFF_ROWS + (kind * TILES + tile) * FZ + 8 * ztile, 8), :
        ]

    centers = [value(field, 0, 0) for field in range(SPECIES)]
    down = [roll_lanes(center, -EDGE) for center in centers]
    up = [roll_lanes(center, EDGE) for center in centers]
    up_before = list(up)
    for tile in range(TILES):
        if tile + 1 < TILES:
            centers_after = [value(field, tile + 1, 0) for field in range(SPECIES)]
            down_after = [roll_lanes(center, -EDGE) for center in centers_after]
        next_x, prev_x, next_y, prev_y, rate = [get(kind, tile) for kind in range(5)]
        base = slot * UPWARD_ROWS + padded_at(tile, ztile)
        next_z = upward[pl.ds(base, 8), :]
        prev_z = upward[pl.ds(base - 1, 8), :]
        forward = rate * (centers[0] * centers[1] - centers[2])
        for field in range(SPECIES):
            center = centers[field]
            ahead, behind = down[field], up[field]
            if tile + 1 < TILES:
                ahead = jnp.where(lane < LANES - EDGE, ahead, down_after[field])
            if tile > 0:
                behind = jnp.where(lane >= EDGE, behind, up_before[field])
            flux = (next_x * ahead + prev_x * behind) + (
                next_y * roll_lanes(center, -1) + prev_y * roll_lanes(center, 1)
            )
            flux = flux + (next_z * value(field, tile, 1) + prev_z * value(field, tile, -1))
            share = ghosts(field, tile)
            if share is not None:
                flux = flux + share
            if DIFFUSE[field] != 1.0:
                flux = DIFFUSE[field] * flux
            result = get(5 + field, tile) * center + flux
            result = result - forward if SIGNS[field] < 0 else result + forward
            target[aligned(to_rows + padded_at(field * TILES + tile, ztile), 8), :] = result
        if tile + 1 < TILES:
            up_before = up
            centers, down = centers_after, down_after
            up = [roll_lanes(center, EDGE) for center in centers]


def clear_pads(ref):
    edge = jnp.zeros((PAD, LANES), jnp.float32)

    def body(block, carry):
        ref[aligned(block * STRIDE, PAD), :] = edge
        ref[aligned(block * STRIDE + PAD + FZ, PAD), :] = edge
        return carry

    lax.fori_loop(0, ref.shape[0] // STRIDE, body, 0)


def prepare_kernel(
    after_ref,
    state_hbm,
    kappa_hbm,
    rate_hbm,
    ylo_ref,
    yhi_ref,
    fields_hbm,
    coeffs_hbm,
    upward_hbm,
    ylo_out,
    yhi_out,
    fields_ref,
    coeffs,
    upward,
    state_ref,
    kappa_ref,
    rate_ref,
    first,
    conduct,
    sems,
    out_sems,
    *,
    slots,
):
    def loads(slot):
        return [
            pltpu.make_async_copy(source.at[slot], target.at[slot], sems.at[order, slot])
            for order, (source, target) in enumerate(
                ((kappa_hbm, kappa_ref), (rate_hbm, rate_ref), (state_hbm, state_ref))
            )
        ]

    for slot in range(slots):
        start_all(loads(slot))
    ylo_out[...] = ylo_ref[...]
    yhi_out[...] = yhi_ref[...]

    def stores(slot):
        return [
            pltpu.make_async_copy(
                source.at[aligned(slot * size, size)],
                target.at[aligned(slot * size, size)],
                out_sems.at[order, slot],
            )
            for order, (source, target, size) in enumerate(
                (
                    (fields_ref, fields_hbm, FIELD_ROWS),
                    (coeffs, coeffs_hbm, COEFF_ROWS),
                    (upward, upward_hbm, UPWARD_ROWS),
                )
            )
        ]

    for ref in (fields_ref, upward, first, conduct):
        clear_pads(ref)

    lane = lane_ids((8, LANES))
    column = lane % EDGE
    side_y = jnp.where((column == 0) | (column == EDGE - 1), 1.0, 0.0)

    def one_patch(slot, carry):
        for copy in loads(slot):
            copy.wait()

        for tile in range(TILES):
            cols = pl.ds(tile * LANES, LANES)
            for field in range(SPECIES):
                row = padded_at(field * TILES + tile, 0)
                first[row : row + FZ, :] = state_ref[slot, field, :, cols]
            row = padded_at(tile, 0)
            conduct[row : row + FZ, :] = kappa_ref[slot, :, cols]

        def keep(kind, tile, ztile, values):
            coeffs[
                aligned(slot * COEFF_ROWS + (kind * TILES + tile) * FZ + 8 * ztile, 8), :
            ] = values

        for ztile in range(ZTILES):

            def here(tile, shift):
                return conduct[pl.ds(padded_at(tile, ztile) + shift, 8), :]

            center = here(0, 0)
            turned = roll_lanes(center, -EDGE)
            back_before = None
            for tile in range(TILES):
                other = turned
                if tile + 1 < TILES:
                    center_after = here(tile + 1, 0)
                    turned_after = roll_lanes(center_after, -EDGE)
                    other = jnp.where(lane < LANES - EDGE, turned, turned_after)
                next_x = face(FINE_SCALE, center, other)
                if tile == TILES - 1:
                    next_x = jnp.where(lane < LANES - EDGE, next_x, 0.0)
                back = roll_lanes(next_x, EDGE)
                prev_x = jnp.where(lane >= EDGE, back, 0.0 if tile == 0 else back_before)
                next_y = jnp.where(
                    column < EDGE - 1, face(FINE_SCALE, center, roll_lanes(center, -1)), 0.0
                )
                prev_y = roll_lanes(next_y, 1)
                next_z = face(FINE_SCALE, center, here(tile, 1))
                prev_z = face(FINE_SCALE, center, here(tile, -1))
                sides = side_y
                if tile == 0:
                    sides = sides + jnp.where(lane < EDGE, 1.0, 0.0)
                if tile == TILES - 1:
                    sides = sides + jnp.where(lane >= LANES - EDGE, 1.0, 0.0)
                scale = FINE_SCALE * center
                total = (next_x + prev_x) + (next_y + prev_y) + (next_z + prev_z) + sides * scale
                upward[aligned(slot * UPWARD_ROWS + padded_at(tile, ztile), 8), :] = next_z
                keep(0, tile, ztile, next_x)
                keep(1, tile, ztile, prev_x)
                keep(2, tile, ztile, next_y)
                keep(3, tile, ztile, prev_y)
                rate = rate_ref[slot, pl.ds(8 * ztile, 8), pl.ds(tile * LANES, LANES)]
                keep(4, tile, ztile, DT_FINE * rate)
                for field in range(SPECIES):
                    keep(5 + field, tile, ztile, 1.0 - DIFFUSE[field] * total)
                keep(8, tile, ztile, scale)
                back_before = back
                if tile + 1 < TILES:
                    center, turned = center_after, turned_after

        for ztile in range(ZTILES):
            advance(
                first,
                fields_ref,
                coeffs,
                upward,
                slot,
                0,
                slot * FIELD_ROWS,
                ztile,
                lambda field, tile: None,
            )
        start_all(stores(slot))
        return carry

    lax.fori_loop(0, slots, one_patch, 0)
    for slot in range(slots):
        for copy in stores(slot):
            copy.wait()


def finish_kernel(
    strips_hbm,
    fields_hbm,
    coeffs_hbm,
    upward_hbm,
    yl_ref,
    yr_ref,
    out_hbm,
    avg_hbm,
    strips_ref,
    fields_ref,
    coeffs,
    upward,
    ghost_ref,
    plane_ref,
    mean_ref,
    avg_ref,
    first,
    second,
    share,
    drift,
    staged,
    sems,
    in_sems,
    strips_sem,
    avg_sems,
    *,
    slots,
):
    arrive = pltpu.make_async_copy(strips_hbm.at[:, pl.ds(0, HALO_START)], strips_ref, strips_sem)
    arrive.start()

    def loads(slot):
        return [
            pltpu.make_async_copy(
                source.at[aligned(slot * size, size)],
                target.at[aligned(slot * size, size)],
                in_sems.at[order, slot],
            )
            for order, (source, target, size) in enumerate(
                (
                    (fields_hbm, fields_ref, FIELD_ROWS),
                    (coeffs_hbm, coeffs, COEFF_ROWS),
                    (upward_hbm, upward, UPWARD_ROWS),
                )
            )
        ]

    start_all(loads(0))
    sources = strips_ref.shape[0]
    clear_pads(first)
    clear_pads(second)
    for tile in range(TILES):
        ghost_ref[:, tile * LANES : (tile + 1) * LANES] = ghost_table(tile)
    plane_ref[...] = plane_table()
    mean_ref[...] = mean_table()
    arrive.wait()

    gathered = strips_ref[0]
    for source in range(1, sources):
        gathered = gathered + strips_ref[source]
    old, new = complete_strips(gathered)
    gathered = jnp.concatenate([old, (new - old) * (1.0 / RATIO)], axis=0)
    quarter = AVG_ROWS // FACES
    group_of = lane_ids((quarter, LANES)) // BLK

    def send_out(slot):
        return pltpu.make_async_copy(staged.at[slot], out_hbm.at[slot], sems.at[slot])

    def one_patch(slot, carry):
        for copy in loads(slot):
            copy.wait()

        @pl.when(slot + 1 < slots)
        def _():
            start_all(loads(slot + 1))

        turned = pltpu.roll(gathered, (LANES - slot * BLK) % LANES, 1)
        stretched = jnp.dot(
            plane_ref[...],
            jnp.concatenate(split_pair(turned), axis=1),
            preferred_element_type=jnp.float32,
        ).astype(jnp.bfloat16)
        base = slot * FIELD_ROWS
        scales = slot * COEFF_ROWS
        for tile in range(TILES):
            ghosts = jnp.dot(
                stretched,
                ghost_ref[:, tile * LANES : (tile + 1) * LANES],
                preferred_element_type=jnp.float32,
            )
            scale = coeffs[aligned(scales + (8 * TILES + tile) * FZ, FZ), :]
            for field in range(SPECIES):
                row = (field * TILES + tile) * FZ
                old = scale * ghosts[field * FZ : (field + 1) * FZ]
                step = scale * ghosts[(SPECIES + field) * FZ : (SPECIES + field + 1) * FZ]
                drift[row : row + FZ, :] = step
                share[row : row + FZ, :] = old + step
                row = padded_at(field * TILES + tile, 0)
                second[row : row + FZ, :] = (
                    fields_ref[aligned(base + row, FZ), :] + DIFFUSE[field] * old
                )

        for step in range(1, RATIO):
            source, target = (second, first) if step % 2 else (first, second)
            for ztile in range(ZTILES):

                def ghosts(field, tile):
                    spot = pl.ds((field * TILES + tile) * FZ + 8 * ztile, 8)
                    value = share[spot, :]
                    if step + 1 < RATIO:
                        share[spot, :] = value + drift[spot, :]
                    return value

                advance(source, target, coeffs, upward, slot, 0, 0, ztile, ghosts)

        for tile in range(TILES):
            for field in range(SPECIES):
                row = padded_at(field * TILES + tile, 0)
                staged[slot, field, :, pl.ds(tile * LANES, LANES)] = first[row : row + FZ, :]
        send_out(slot).start()

        sums = []
        for field in range(SPECIES):
            for plane in range(NZC):
                start = field * TILES * STRIDE + PAD + RATIO * plane
                part = first[pl.ds(start, TILES, stride=STRIDE), :]
                for z in range(1, RATIO):
                    part = part + first[pl.ds(start + z, TILES, stride=STRIDE), :]
                sums.append(part)
        means = jnp.dot(
            jnp.concatenate(split_pair(jnp.concatenate(sums, axis=0)), axis=1),
            mean_ref[...],
            preferred_element_type=jnp.float32,
        )
        chunk = avg_ref[...]
        for part in range(FACES):
            chunk = jnp.where(
                group_of == part * slots + slot,
                means[part * quarter : (part + 1) * quarter],
                chunk,
            )
        avg_ref[...] = chunk
        return carry

    avg_ref[...] = jnp.zeros((quarter, LANES), jnp.float32)
    lax.fori_loop(0, slots, one_patch, 0)
    copies = [
        pltpu.make_async_copy(avg_ref, avg_hbm.at[target], avg_sems.at[target])
        for target in range(sources)
    ]
    start_all(copies)
    for copy in copies:
        copy.wait()
    for slot in range(slots):
        send_out(slot).wait()


def place_kernel(
    place_ref,
    avg_ref,
    new_hbm,
    strips_hbm,
    xlo_ref,
    xhi_ref,
    ylo_ref,
    yhi_ref,
    yl_ref,
    yr_ref,
    out_ref,
    new_ref,
    halo_ref,
    sems,
    *,
    cells_x,
    cells_y,
    group,
    slots,
):
    me = lax.axis_index("af")
    last = strips_hbm.shape[0] - 1
    rows = pl.ds(HALO_START, halo_ref.shape[1])
    fetches = [
        pltpu.make_async_copy(
            strips_hbm.at[jnp.maximum(me - 1, 0), rows], halo_ref.at[0], sems.at[0]
        ),
        pltpu.make_async_copy(
            strips_hbm.at[jnp.minimum(me + 1, last), rows], halo_ref.at[1], sems.at[1]
        ),
        pltpu.make_async_copy(new_hbm, new_ref, sems.at[2]),
    ]
    start_all(fetches)

    def edge_share(own_ref, other_ref):
        own = own_ref[...]
        other = other_ref[...]
        coeff = face(DT_COARSE, jnp.maximum(own, 0.125), other)
        lane = lane_ids(own.shape)
        spread = jnp.zeros_like(own)
        for field in range(SPECIES):
            moved = roll_lanes(coeff, (field - SPECIES) * NZC)
            spread = jnp.where(lane // NZC == field, DIFFUSE[field] * moved, spread)
        return spread * (other - own)

    lower = edge_share(ylo_ref, yl_ref)
    upper = edge_share(yhi_ref, yr_ref)

    width = slots * BLK
    quarter = AVG_ROWS // FACES
    per_tile = LANES // width
    part = lane_ids((quarter, LANES)) // width
    columns = []
    for tile in range(group * BLK // LANES):
        rows = []
        for index in range(FACES):
            merged = jnp.zeros((quarter, LANES), jnp.float32)
            for place in range(per_tile):
                piece = roll_lanes(avg_ref[tile * per_tile + place], (place - index) * width)
                merged = jnp.where(part == place, piece, merged)
            rows.append(merged)
        columns.append(jnp.concatenate(rows, axis=0))
    high, low = split_pair(jnp.concatenate(columns, axis=1))
    ones = jnp.ones((16, high.shape[1]), jnp.bfloat16)
    stacked = jnp.concatenate([high, low, ones], axis=0)

    for copy in fetches:
        copy.wait()
    lane = lane_ids((BLK, LANES))
    row_id = lax.broadcasted_iota(jnp.int32, (BLK, LANES), 0)
    halves = cells_y // LANES

    def side_share(own_ref, side, exists):
        shares = []
        for half in range(halves):
            own = own_ref[:, half * LANES : (half + 1) * LANES]
            other = halo_ref[side, half * EDGE_ROWS : (half + 1) * EDGE_ROWS]
            coeff = face(DT_COARSE, own[PLANES:], other[PLANES:])
            coeff = jnp.where(exists, coeff, 0.0)
            shares.append(
                jnp.concatenate(
                    [
                        (DIFFUSE[field] * coeff)
                        * (
                            other[field * NZC : (field + 1) * NZC]
                            - own[field * NZC : (field + 1) * NZC]
                        )
                        for field in range(SPECIES)
                    ],
                    axis=0,
                )
            )
        return shares

    before = side_share(xlo_ref, 0, me > 0)
    after = side_share(xhi_ref, 1, me < last)
    block_cols = cells_x // BLK
    for column in range(block_cols):
        placed = lax.dot_general(
            stacked,
            selector(place_ref, column, cells_y),
            (((1,), (1,)), ((), ())),
            preferred_element_type=jnp.float32,
        )
        covered = placed[2 * AVG_ROWS : 2 * AVG_ROWS + 8] > 0.5
        for plane in range(PLANES):
            values = (
                placed[plane * BLK : (plane + 1) * BLK]
                + placed[AVG_ROWS + plane * BLK : AVG_ROWS + (plane + 1) * BLK]
            )
            row = plane * cells_x + column * BLK
            edge_rows = slice(column * BLK, (column + 1) * BLK)
            for half in range(halves):
                cols = slice(half * LANES, (half + 1) * LANES)
                coarse = new_ref[row : row + BLK, cols]
                if column == 0:
                    share = before[half][plane : plane + 1]
                    coarse = coarse + jnp.where(row_id == 0, share, 0.0)
                if column == block_cols - 1:
                    share = after[half][plane : plane + 1]
                    coarse = coarse + jnp.where(row_id == BLK - 1, share, 0.0)
                if half == 0:
                    share = roll_lanes(lower[edge_rows], -plane)
                    coarse = coarse + jnp.where(lane == 0, share, 0.0)
                if half == halves - 1:
                    share = roll_lanes(upper[edge_rows], LANES - 1 - plane)
                    coarse = coarse + jnp.where(lane == LANES - 1, share, 0.0)
                out_ref[row : row + BLK, cols] = jnp.where(
                    covered[:, cols], values[:, cols], coarse
                )


VMEM = pl.BlockSpec(memory_space=pltpu.VMEM)
HBM = pl.BlockSpec(memory_space=pltpu.HBM)
PARAMS = pltpu.CompilerParams(vmem_limit_bytes=40 * 1024 * 1024)


def f32(*shape):
    return jax.ShapeDtypeStruct(shape, jnp.float32)


def hbm32(*shape):
    return pltpu.HBM(shape, jnp.float32)


def pinned(*arrays):
    return [pltpu.with_memory_space_constraint(array, pltpu.HBM) for array in arrays]


def shifted(values, axis, step):
    count = lax.axis_size(axis)
    pairs = [(i, i + step) for i in range(count) if 0 <= i + step < count]
    return lax.ppermute(values, axis, pairs)


def exchange(chunks):
    return lax.all_to_all(chunks, "af", split_axis=0, concat_axis=0, tiled=True)


def per_device(
    coarse_state, coarse_kappa, coarse_rate, fine_state, fine_kappa, fine_rate, boxes, cover
):
    af_count = lax.axis_size("af")
    slots = fine_state.shape[0]
    cells_x, cells_y = coarse_state.shape[2:]
    group = af_count * slots
    lanes = group * BLK
    halves = cells_y // LANES
    rows = PLANES * cells_x
    plain = NZC * cells_x
    sizes = dict(cells_x=cells_x, cells_y=cells_y, group=group)

    span = cells_x + 2 * PAD
    chunk_rows = HALO_START + halves * EDGE_ROWS
    new, send, place, xlo, xhi, ylo, yhi = pl.pallas_call(
        functools.partial(strips_kernel, slots=slots, **sizes),
        out_shape=[
            hbm32(rows, cells_y),
            f32(af_count, chunk_rows, LANES),
            jax.ShapeDtypeStruct((16, lanes), jnp.int32),
        ]
        + [f32(EDGE_ROWS, cells_y)] * 2
        + [f32(cells_x, LANES)] * 2,
        in_specs=[HBM] * 4,
        out_specs=[HBM] + [VMEM] * 6,
        scratch_shapes=[
            pltpu.VMEM((2, boxes.shape[0]), jnp.int32),
            pltpu.VMEM((rows, cells_y), jnp.float32),
            pltpu.VMEM((plain, cells_y), jnp.float32),
            pltpu.VMEM((plain, cells_y), jnp.float32),
            pltpu.VMEM((rows, cells_y), jnp.float32),
            pltpu.VMEM(((SPECIES + 1) * halves * NZC * span, LANES), jnp.float32),
            pltpu.VMEM((rows * halves, LANES), jnp.float32),
            pltpu.SemaphoreType.DMA((4,)),
        ],
        compiler_params=PARAMS,
        name="strips",
    )(
        *pinned(
            boxes.T,
            coarse_state.reshape(rows, cells_y),
            coarse_kappa.reshape(plain, cells_y),
            coarse_rate.reshape(plain, cells_y),
        )
    )

    strips = exchange(send)

    kept = [hbm32(slots * size, LANES) for size in (FIELD_ROWS, COEFF_ROWS, UPWARD_ROWS)]
    kept_scratch = [pltpu.VMEM((slots * size, LANES), jnp.float32)
        for size in (FIELD_ROWS, COEFF_ROWS, UPWARD_ROWS)]
    fields, coeffs, upward, ylo_sent, yhi_sent = pl.pallas_call(
        functools.partial(prepare_kernel, slots=slots),
        out_shape=kept + [f32(cells_x, LANES)] * 2,
        in_specs=[HBM] * 4 + [VMEM] * 2,
        out_specs=[HBM] * 3 + [VMEM] * 2,
        scratch_shapes=kept_scratch
        + [
            pltpu.VMEM(fine_state.shape, jnp.float32),
            pltpu.VMEM(fine_kappa.shape, jnp.float32),
            pltpu.VMEM(fine_rate.shape, jnp.float32),
            pltpu.VMEM((FIELD_ROWS, LANES), jnp.float32),
            pltpu.VMEM((UPWARD_ROWS, LANES), jnp.float32),
            pltpu.SemaphoreType.DMA((3, slots)),
            pltpu.SemaphoreType.DMA((3, slots)),
        ],
        compiler_params=PARAMS,
        name="prepare",
    )(*pinned(new, fine_state, fine_kappa, fine_rate), ylo, yhi)
    yl = shifted(yhi_sent, "col", 1)
    yr = shifted(ylo_sent, "col", -1)

    chunk = (AVG_ROWS // FACES, LANES)
    fine_out, averages = pl.pallas_call(
        functools.partial(finish_kernel, slots=slots),
        out_shape=[hbm32(*fine_state.shape), hbm32(af_count, *chunk)],
        in_specs=[HBM] * 4 + [VMEM] * 2,
        out_specs=[HBM, HBM],
        scratch_shapes=[pltpu.VMEM((af_count, HALO_START, LANES), jnp.float32)]
        + kept_scratch
        + [
            pltpu.VMEM((2 * LANES, EDGE * EDGE), jnp.bfloat16),
            pltpu.VMEM((2 * SPECIES * FZ, STRIP_ROWS), jnp.bfloat16),
            pltpu.VMEM((2 * LANES, LANES), jnp.bfloat16),
            pltpu.VMEM(chunk, jnp.float32),
            pltpu.VMEM((FIELD_ROWS, LANES), jnp.float32),
            pltpu.VMEM((FIELD_ROWS, LANES), jnp.float32),
            pltpu.VMEM((SPECIES * TILES * FZ, LANES), jnp.float32),
            pltpu.VMEM((SPECIES * TILES * FZ, LANES), jnp.float32),
            pltpu.VMEM(fine_state.shape, jnp.float32),
            pltpu.SemaphoreType.DMA((slots,)),
            pltpu.SemaphoreType.DMA((3, slots)),
            pltpu.SemaphoreType.DMA,
            pltpu.SemaphoreType.DMA((af_count,)),
        ],
        compiler_params=PARAMS,
        name="finish",
    )(*pinned(strips, fields, coeffs, upward), yl, yr)

    arrived = exchange(averages)

    placed = pl.pallas_call(
        functools.partial(place_kernel, slots=slots, **sizes),
        out_shape=f32(rows, cells_y),
        in_specs=[VMEM] * 2 + [HBM] * 2 + [VMEM] * 6,
        out_specs=VMEM,
        scratch_shapes=[
            pltpu.VMEM((rows, cells_y), jnp.float32),
            pltpu.VMEM((2, halves * EDGE_ROWS, LANES), jnp.float32),
            pltpu.SemaphoreType.DMA((3,)),
        ],
        compiler_params=PARAMS,
        name="place",
    )(place, arrived, *pinned(new, strips), xlo, xhi, ylo, yhi, yl, yr)
    return (placed.reshape(coarse_state.shape), fine_out)


def solution(mesh):
    return jax.shard_map(
        per_device,
        mesh=mesh,
        in_specs=(
            P(None, None, "af", "col"),
            P(None, "af", "col"),
            P(None, "af", "col"),
            P(("col", "af"), None, None, None),
            P(("col", "af"), None, None),
            P(("col", "af"), None, None),
            P(),
            P(),
        ),
        out_specs=(P(None, None, "af", "col"), P(("col", "af"), None, None, None)),
        check_vma=False,
    )
```

profile of v0, /device:TPU:0, one launch (start us, length us, event | category | flops | bytes accessed | tf_op | source)
XLA Modules:
  0.0 53.4 jit_solution(1456044798805741011)
XLA Ops:
  0.6 3.9 %strips.1 = (f32[384,256]{1,0:T(8,128)}, f32[8,144,128]{2,1,0:T(8,128)}, s32[16,256]{1,0:T(8,128)S(1)}, f32[32,256]{1,0:T(8,128)S(1)}, f32[32,256]{1,0:T(8,128)S...) custom-call(s32[2,128]{1,0:T(2,128)} %bitcast.9, f32[384,256]{1,0:T(8,128)} %bitcast.5, f32[128,256]{1,0:T(8,128)} %bitcast.7, ...), custom_call_target="tpu_custom_call" | custom-call | tf_op jit(solution)/shard_map/strips/pallas_call | solution.py:943
  4.6 7.3 %all-to-all-start = ((f32[8,144,128]{2,1,0:T(8,128)}), f32[8,144,128]{2,1,0:T(8,128)S(1)}, u32[]{:S(2)}, u32[]{:S(2)}) async-start(f32[8,144,128]{2,1,0:T(8,128)} %get-tuple-element.17), calls=%async_computation | async-start | bytes 1179648 | tf_op jit(solution)/shard_map/all_to_all | solution.py:925
  11.9 6.6 %prepare.1 = (f32[4608,128]{1,0:T(8,128)}, f32[9216,128]{1,0:T(8,128)}, f32[1536,128]{1,0:T(8,128)}, f32[16,128]{1,0:T(8,128)S(1)}, f32[16,128]{1,0:T(8,128)S(1)}) custom-call(f32[384,256]{1,0:T(8,128)} %get-tuple-element.18.after_ref.new_hbm, f32[4,3,32,1024]{3,2,1,0:T(8,128)} %state_hbm.1, f32[4,32,1024]{2,1,0:T(8,128)} %kappa_hbm.1, ...), custom_call_target="tpu_custom_call" | custom-call | tf_op jit(solution)/shard_map/prepare/pallas_call | solution.py:980
  18.4 1.5 %collective-permute-start = (f32[16,128]{1,0:T(8,128)S(1)}, f32[16,128]{1,0:T(8,128)S(1)}, u32[]{:S(2)}, u32[]{:S(2)}) collective-permute-start(f32[16,128]{1,0:T(8,128)S(1)} %get-tuple-element.24), channel_id=1, source_target_pairs={{0,8},{8,16},{16,24},{1,9},{9,17},{17,25},{2,10},{10,18},{18,26},{... | collective-permute-start | bytes 24584 | tf_op jit(solution)/shard_map/ppermute | solution.py:921
  19.9 1.3 %collective-permute-start.1 = (f32[16,128]{1,0:T(8,128)S(1)}, f32[16,128]{1,0:T(8,128)S(1)}, u32[]{:S(2)}, u32[]{:S(2)}) collective-permute-start(f32[16,128]{1,0:T(8,128)S(1)} %get-tuple-element.25), channel_id=1, source_target_pairs={{8,0},{16,8},{24,16},{9,1},{17,9},{25,17},{10,2},{18,10},{26,18},{... | collective-permute-start | bytes 24584 | tf_op jit(solution)/shard_map/ppermute | solution.py:921
  21.2 0.0 collective-permute-done.yl_ref
  21.2 3.3 %collective-permute-done.1.yr_ref = f32[16,128]{1,0:T(8,128)S(1)} collective-permute-done((f32[16,128]{1,0:T(8,128)S(1)}, f32[16,128]{1,0:T(8,128)S(1)}, u32[]{:S(2)}, u32[]{:S(2)}) %collective-permute-start.1) | collective-permute-done | bytes 8224 | tf_op jit(solution)/shard_map/ppermute | solution.py:921
  24.5 3.2 %all-to-all-done.strips_hbm = f32[8,144,128]{2,1,0:T(8,128)S(1)} async-done(((f32[8,144,128]{2,1,0:T(8,128)}), f32[8,144,128]{2,1,0:T(8,128)S(1)}, u32[]{:S(2)}, u32[]{:S(2)}) %all-to-all-start) | async-done | bytes 589856 | tf_op jit(solution)/shard_map/all_to_all | solution.py:925
  27.8 0.0 copy-start
  27.8 0.9 %copy-done = f32[8,144,128]{2,1,0:T(8,128)} copy-done((f32[8,144,128]{2,1,0:T(8,128)}, f32[8,144,128]{2,1,0:T(8,128)S(1)}, u32[]{:S(2)}) %copy-start) | copy-done | bytes 589848
  28.6 10.0 %finish.1 = (f32[4,3,32,1024]{3,2,1,0:T(8,128)}, f32[8,48,128]{2,1,0:T(8,128)}) custom-call(f32[8,144,128]{2,1,0:T(8,128)} %copy-done, f32[4608,128]{1,0:T(8,128)} %get-tuple-element.21.fields_hbm, f32[9216,128]{1,0:T(8,128)} %get-tuple-element.22.coeffs_hbm, f32[1536,128]{1,0:T(8,128)} %get-tuple-element.23.upward_hbm, ...), custom_call_target="tpu_custom_call" | custom-call | tf_op jit(solution)/shard_map/finish/pallas_call | solution.py:1002
  38.6 12.5 %all_to_all.10.avg_ref = f32[8,48,128]{2,1,0:T(8,128)S(1)} all-to-all(f32[8,48,128]{2,1,0:T(8,128)} %get-tuple-element.26), channel_id=1, replica_groups=mesh['col'=4,'af'=8] {'af'}, dimensions={0} | all-to-all | bytes 393216 | tf_op jit(solution)/shard_map/all_to_all | solution.py:925
  51.1 2.3 %place.1 = f32[384,256]{1,0:T(8,128)} custom-call(s32[16,256]{1,0:T(8,128)S(1)} %get-tuple-element.16.place_ref, f32[8,48,128]{2,1,0:T(8,128)S(1)} %all_to_all.10.avg_ref, f32[384,256]{1,0:T(8,128)} %get-tuple-element.18.after_ref.new_hbm, f32[8,144,128]{2,1,0:T(8,128)} %copy-done, f32[32,256]{1,0:T(8,128)S(1)} %get-tuple-element.27.xlo_ref, ...), custom_call_target="tpu_custom_call" | custom-call | tf_op jit(solution)/shard_map/place/pallas_call | solution.py:1030
Async XLA Ops:
  4.6 23.2 %all-to-all-start = ((f32[8,144,128]{2,1,0:T(8,128)}), f32[8,144,128]{2,1,0:T(8,128)S(1)}, u32[]{:S(2)}, u32[]{:S(2)}) async-start(f32[8,144,128]{2,1,0:T(8,128)} %get-tuple-element.17), calls=%async_computation | async-start | bytes 1179648 | tf_op jit(solution)/shard_map/all_to_all | solution.py:925
  18.4 2.8 %collective-permute-start = (f32[16,128]{1,0:T(8,128)S(1)}, f32[16,128]{1,0:T(8,128)S(1)}, u32[]{:S(2)}, u32[]{:S(2)}) collective-permute-start(f32[16,128]{1,0:T(8,128)S(1)} %get-tuple-element.24), channel_id=1, source_target_pairs={{0,8},{8,16},{16,24},{1,9},{9,17},{17,25},{2,10},{10,18},{18,26},{... | collective-permute-start | bytes 24584 | tf_op jit(solution)/shard_map/ppermute | solution.py:921
  19.9 4.6 %collective-permute-start.1 = (f32[16,128]{1,0:T(8,128)S(1)}, f32[16,128]{1,0:T(8,128)S(1)}, u32[]{:S(2)}, u32[]{:S(2)}) collective-permute-start(f32[16,128]{1,0:T(8,128)S(1)} %get-tuple-element.25), channel_id=1, source_target_pairs={{8,0},{16,8},{24,16},{9,1},{17,9},{25,17},{10,2},{18,10},{26,18},{... | collective-permute-start | bytes 24584 | tf_op jit(solution)/shard_map/ppermute | solution.py:921
  27.8 0.9 %copy-start = (f32[8,144,128]{2,1,0:T(8,128)}, f32[8,144,128]{2,1,0:T(8,128)S(1)}, u32[]{:S(2)}) copy-start(f32[8,144,128]{2,1,0:T(8,128)S(1)} %all-to-all-done.strips_hbm) | copy-start | bytes 1769476
where the time goes:
time: 53.9 us; the launch traced here: 53.4 us
  Pallas kernels  22.8 us (42%)
  blocking collectives  12.5 us (23%)
  starting transfers between devices  10 us (19%)
  waiting for transfers between devices  6.53 us (12%)
  local copies, waits for them, and re-layouts  0.87 us (2%)
  between operations  0.68 us (1%)
    all_to_all x1, blocking collectives, exchange(): return lax.all_to_all(chunks, 'af', split_axis=0, concat_axis=0, tiled=True)  12.5 us
    pallas_call x1, Pallas kernels, per_device(): pl.pallas_call(functools.partial(finish_kernel, slots=slots), out_shape=[...  10 us
    all_to_all x1, starting transfers between devices, exchange(): return lax.all_to_all(chunks, 'af', split_axis=0, concat_axis=0, tiled=True)  7.29 us
    pallas_call x1, Pallas kernels, per_device(): pl.pallas_call(functools.partial(prepare_kernel, slots=slots), out_shape=...  6.57 us
    pallas_call x1, Pallas kernels, per_device(): pl.pallas_call(functools.partial(strips_kernel, slots=slots, **sizes), ou...  3.92 us
    ppermute x2, waiting for transfers between devices, shifted(): return lax.ppermute(values, axis, pairs)  3.31 us
    all_to_all x1, waiting for transfers between devices, exchange(): return lax.all_to_all(chunks, 'af', split_axis=0, concat_axis=0, tiled=True)  3.22 us
    ppermute x2, starting transfers between devices, shifted(): return lax.ppermute(values, axis, pairs)  2.76 us
  transfers between devices with their start and end apart: 3, of which 2 were waited for; matrix products, arithmetic and copies ran while one was open for 0% of the time, Pallas kernels for 12%

commit v1 on v0

--- a/solution.py
+++ b/solution.py
@@ -27,7 +27,8 @@
 COEFF_ROWS = KINDS * TILES * FZ
 UPWARD_ROWS = TILES * STRIDE
 EDGE_ROWS = PLANES + NZC
-HALO_START = STRIP_ROWS + EDGE_ROWS
+BESIDE_ROWS = 2 * NZC
+HALO_START = STRIP_ROWS + BESIDE_ROWS
 
 DT_COARSE = 1.0 / 28.0
 DIFFUSE = (1.0, 0.7, 0.45)
@@ -258,24 +259,42 @@
     last_row = edge_at(cells_x - 1)
     xlo_ref[...] = first_row
     xhi_ref[...] = last_row
-    place = lane_ids((EDGE_ROWS, cells_y)) % BLK
-
-    def corners(row, at):
-        below = jnp.where(place == at, roll_lanes(row, at + 1), 0.0)
-        return jnp.where(place == at + 1, roll_lanes(row, at + 1 - BLK), below)
+    place = lane_ids((NZC, cells_y)) % BLK
+    ones = jnp.ones((NZC, cells_y), jnp.float32)
+
+    def field_of(row, field):
+        return row[field * NZC : (field + 1) * NZC]
+
+    def corners(row, fields, first_at):
+        found = jnp.zeros((NZC, cells_y), jnp.float32)
+        for order, field in enumerate(fields):
+            at = first_at + 2 * order
+            values = field_of(row, field)
+            found = jnp.where(place == at, roll_lanes(values, at + 1), found)
+            found = jnp.where(place == at + 1, roll_lanes(values, at + 1 - BLK), found)
+        return found
+
+    every = range(SPECIES)
+
+    def near(row):
+        own = [(field, field_of(row, field)) for field in range(SPECIES + 1)]
+        return own + [(5, corners(row, [SPECIES], 0))]
+
+    def far(row):
+        return [
+            (4, field_of(row, SPECIES)),
+            (5, corners(row, every, 2)),
+            (6, corners(row, [SPECIES], 0)),
+        ]
 
     extra_members = {
-        -1: [(1, first_row), (2, corners(first_row, 2))],
-        0: [(0, first_row), (2, corners(first_row, 0))],
-        block_cols - 1: [
-            (0, last_row),
-            (2, corners(last_row, 0)),
-            (3, jnp.ones((EDGE_ROWS, cells_y), jnp.float32)),
-        ],
-        block_cols: [(1, last_row), (2, corners(last_row, 2))],
+        -1: far(first_row),
+        0: near(first_row),
+        block_cols - 1: near(last_row) + [(7, ones)],
+        block_cols: far(last_row),
     }
 
-    faces = [None] * (2 * FACES)
+    faces = [None] * (3 * FACES)
 
     def add(index, part):
         faces[index] = part if faces[index] is None else faces[index] + part
@@ -310,7 +329,11 @@
     for target in range(group // slots):
         first = target * width
         tile = first // LANES * LANES
-        for start, size, kind in ((0, STRIP_ROWS, 0), (STRIP_ROWS, EDGE_ROWS, FACES)):
+        for start, size, kind in (
+            (0, STRIP_ROWS, 0),
+            (STRIP_ROWS, NZC, FACES),
+            (STRIP_ROWS + NZC, NZC, 2 * FACES),
+        ):
             part = lane_ids((size, LANES)) // width
             chunk = jnp.zeros((size, LANES), jnp.float32)
             for index in range(FACES):
@@ -363,32 +386,37 @@
 
 def complete_strips(gathered):
     width = LANES // FACES
-    beside = [
-        gathered[STRIP_ROWS + field * NZC : STRIP_ROWS + (field + 1) * NZC]
-        for field in range(SPECIES + 1)
-    ]
+    own = gathered[STRIP_ROWS : STRIP_ROWS + NZC]
+    beside = gathered[STRIP_ROWS + NZC : STRIP_ROWS + 2 * NZC]
     lane = lane_ids((NZC, LANES))
     part = lane // width
     pos = lane % BLK
-    flag = jnp.where(part == FACES - 1, beside[0], 0.0)
+    flag = jnp.where(part == FACES - 1, beside, 0.0)
     flag = flag + roll_lanes(flag, width)
     upper = flag + roll_lanes(flag, 2 * width) > 0.5
-    conduct = jnp.maximum(beside[SPECIES], 0.125)
-    block = face(DT_COARSE, conduct, roll_lanes(conduct, -width))
-    corner = face(DT_COARSE, conduct, roll_lanes(conduct, -2))
-    nothing = jnp.zeros((NZC, LANES), jnp.float32)
+
+    def coefficient(one, other):
+        return face(DT_COARSE, jnp.maximum(one, 0.125), jnp.maximum(other, 0.125))
+
+    block = coefficient(roll_lanes(own, width), beside)
+    corner = coefficient(beside, roll_lanes(beside, -width))
     added = []
     for field in range(SPECIES):
-        values = beside[field]
-        across = DIFFUSE[field] * block * (values - roll_lanes(values, -width))
-        along = DIFFUSE[field] * corner * (roll_lanes(values, -2) - values)
-        share = jnp.where((part == 0) & ~upper, across, nothing)
+        old = gathered[field * NZC : (field + 1) * NZC]
+        there = jnp.where(upper, roll_lanes(old, -width), old)
+        across = DIFFUSE[field] * block * (roll_lanes(own, -field * width) - there)
+        below = jnp.where(upper, roll_lanes(old, -width - (BLK - 1)), roll_lanes(old, -width))
+        above = jnp.where(
+            upper, roll_lanes(old, -2 * width - (BLK - 2)), roll_lanes(old, 1 - 2 * width)
+        )
+        here = jnp.where(pos == 0, below, above)
+        along = DIFFUSE[field] * corner * (roll_lanes(beside, -2 - 2 * field) - here)
+        share = jnp.where((part == 0) & ~upper, across, 0.0)
         share = jnp.where((part == 1) & upper, roll_lanes(across, width), share)
         for index in range(2):
-            home = 2 + index
             for at, chosen in ((0, ~upper), (BLK - 1, upper)):
-                moved = roll_lanes(along, index * width + at - index)
-                share = jnp.where((part == home) & (pos == at) & chosen, moved, share)
+                moved = roll_lanes(along, (1 + index) * width + at - index)
+                share = jnp.where((part == 2 + index) & (pos == at) & chosen, moved, share)
         added.append(share)
     new = gathered[PLANES:STRIP_ROWS] + jnp.concatenate(added, axis=0)
     return gathered[:PLANES], new
@@ -406,7 +434,8 @@
     lane = lane_ids((8, LANES))
 
     def value(field, tile, shift):
-        return source[pl.ds(from_rows + padded_at(field * TILES + tile, ztile) + shift, 8), :]
+        start = from_rows + padded_at(field * TILES + tile, ztile) + shift
+        return source[aligned(start, 8) if shift == 0 else pl.ds(start, 8), :]
 
     def get(kind, tile):
         return coeffs[
@@ -423,7 +452,7 @@
             down_after = [roll_lanes(center, -EDGE) for center in centers_after]
         next_x, prev_x, next_y, prev_y, rate = [get(kind, tile) for kind in range(5)]
         base = slot * UPWARD_ROWS + padded_at(tile, ztile)
-        next_z = upward[pl.ds(base, 8), :]
+        next_z = upward[aligned(base, 8), :]
         prev_z = upward[pl.ds(base - 1, 8), :]
         forward = rate * (centers[0] * centers[1] - centers[2])
         for field in range(SPECIES):
@@ -462,18 +491,19 @@
     lax.fori_loop(0, ref.shape[0] // STRIDE, body, 0)
 
 
+def hand_on_kernel(ylo_ref, yhi_ref, ylo_out, yhi_out):
+    ylo_out[...] = ylo_ref[...]
+    yhi_out[...] = yhi_ref[...]
+
+
 def prepare_kernel(
     after_ref,
     state_hbm,
     kappa_hbm,
     rate_hbm,
-    ylo_ref,
-    yhi_ref,
     fields_hbm,
     coeffs_hbm,
     upward_hbm,
-    ylo_out,
-    yhi_out,
     fields_ref,
     coeffs,
     upward,
@@ -497,8 +527,6 @@
 
     for slot in range(slots):
         start_all(loads(slot))
-    ylo_out[...] = ylo_ref[...]
-    yhi_out[...] = yhi_ref[...]
 
     def stores(slot):
         return [
@@ -530,10 +558,10 @@
         for tile in range(TILES):
             cols = pl.ds(tile * LANES, LANES)
             for field in range(SPECIES):
-                row = padded_at(field * TILES + tile, 0)
-                first[row : row + FZ, :] = state_ref[slot, field, :, cols]
-            row = padded_at(tile, 0)
-            conduct[row : row + FZ, :] = kappa_ref[slot, :, cols]
+                spot = aligned(slot * FIELD_ROWS + padded_at(field * TILES + tile, 0), FZ)
+                first[spot, :] = state_ref[slot, field, :, cols]
+            spot = aligned(slot * UPWARD_ROWS + padded_at(tile, 0), FZ)
+            conduct[spot, :] = kappa_ref[slot, :, cols]
 
         def keep(kind, tile, ztile, values):
             coeffs[
@@ -543,7 +571,8 @@
         for ztile in range(ZTILES):
 
             def here(tile, shift):
-                return conduct[pl.ds(padded_at(tile, ztile) + shift, 8), :]
+                start = slot * UPWARD_ROWS + padded_at(tile, ztile) + shift
+                return conduct[aligned(start, 8) if shift == 0 else pl.ds(start, 8), :]
 
             center = here(0, 0)
             turned = roll_lanes(center, -EDGE)
@@ -593,7 +622,7 @@
                 coeffs,
                 upward,
                 slot,
-                0,
+                slot * FIELD_ROWS,
                 slot * FIELD_ROWS,
                 ztile,
                 lambda field, tile: None,
@@ -608,7 +637,7 @@
 
 
 def finish_kernel(
-    strips_hbm,
+    strips_ref,
     fields_hbm,
     coeffs_hbm,
     upward_hbm,
@@ -616,7 +645,7 @@
     yr_ref,
     out_hbm,
     avg_hbm,
-    strips_ref,
+    halo_hbm,
     fields_ref,
     coeffs,
     upward,
@@ -625,19 +654,25 @@
     mean_ref,
     avg_ref,
     first,
-    second,
     share,
     drift,
     staged,
     sems,
     in_sems,
-    strips_sem,
+    halo_sems,
     avg_sems,
     *,
     slots,
 ):
-    arrive = pltpu.make_async_copy(strips_hbm.at[:, pl.ds(0, HALO_START)], strips_ref, strips_sem)
-    arrive.start()
+    sources = strips_ref.shape[0]
+    me = lax.axis_index("af")
+    halo_rows = pl.ds(HALO_START, halo_hbm.shape[1])
+    halos = [
+        pltpu.make_async_copy(
+            strips_ref.at[source, halo_rows], halo_hbm.at[side], halo_sems.at[side]
+        )
+        for side, source in enumerate((jnp.maximum(me - 1, 0), jnp.minimum(me + 1, sources - 1)))
+    ]
 
     def loads(slot):
         return [
@@ -656,18 +691,16 @@
         ]
 
     start_all(loads(0))
-    sources = strips_ref.shape[0]
+    start_all(halos)
     clear_pads(first)
-    clear_pads(second)
     for tile in range(TILES):
         ghost_ref[:, tile * LANES : (tile + 1) * LANES] = ghost_table(tile)
     plane_ref[...] = plane_table()
     mean_ref[...] = mean_table()
-    arrive.wait()
-
-    gathered = strips_ref[0]
+
+    gathered = strips_ref[0, 0:HALO_START]
     for source in range(1, sources):
-        gathered = gathered + strips_ref[source]
+        gathered = gathered + strips_ref[source, 0:HALO_START]
     old, new = complete_strips(gathered)
     gathered = jnp.concatenate([old, (new - old) * (1.0 / RATIO)], axis=0)
     quarter = AVG_ROWS // FACES
@@ -705,13 +738,11 @@
                 step = scale * ghosts[(SPECIES + field) * FZ : (SPECIES + field + 1) * FZ]
                 drift[row : row + FZ, :] = step
                 share[row : row + FZ, :] = old + step
-                row = padded_at(field * TILES + tile, 0)
-                second[row : row + FZ, :] = (
-                    fields_ref[aligned(base + row, FZ), :] + DIFFUSE[field] * old
-                )
+                spot = aligned(base + padded_at(field * TILES + tile, 0), FZ)
+                fields_ref[spot, :] = fields_ref[spot, :] + DIFFUSE[field] * old
 
         for step in range(1, RATIO):
-            source, target = (second, first) if step % 2 else (first, second)
+            source, target = (fields_ref, first) if step % 2 else (first, fields_ref)
             for ztile in range(ZTILES):
 
                 def ghosts(field, tile):
@@ -721,18 +752,18 @@
                         share[spot, :] = value + drift[spot, :]
                     return value
 
-                advance(source, target, coeffs, upward, slot, 0, 0, ztile, ghosts)
+                advance(source, target, coeffs, upward, slot, base, base, ztile, ghosts)
 
         for tile in range(TILES):
             for field in range(SPECIES):
-                row = padded_at(field * TILES + tile, 0)
-                staged[slot, field, :, pl.ds(tile * LANES, LANES)] = first[row : row + FZ, :]
+                spot = aligned(base + padded_at(field * TILES + tile, 0), FZ)
+                staged[slot, field, :, pl.ds(tile * LANES, LANES)] = first[spot, :]
         send_out(slot).start()
 
         sums = []
         for field in range(SPECIES):
             for plane in range(NZC):
-                start = field * TILES * STRIDE + PAD + RATIO * plane
+                start = base + field * TILES * STRIDE + PAD + RATIO * plane
                 part = first[pl.ds(start, TILES, stride=STRIDE), :]
                 for z in range(1, RATIO):
                     part = part + first[pl.ds(start + z, TILES, stride=STRIDE), :]
@@ -761,15 +792,15 @@
     start_all(copies)
     for copy in copies:
         copy.wait()
+    for copy in halos:
+        copy.wait()
     for slot in range(slots):
         send_out(slot).wait()
 
 
-def place_kernel(
-    place_ref,
-    avg_ref,
+def edges_kernel(
     new_hbm,
-    strips_hbm,
+    halo_hbm,
     xlo_ref,
     xhi_ref,
     ylo_ref,
@@ -783,20 +814,12 @@
     *,
     cells_x,
     cells_y,
-    group,
-    slots,
 ):
     me = lax.axis_index("af")
-    last = strips_hbm.shape[0] - 1
-    rows = pl.ds(HALO_START, halo_ref.shape[1])
+    last = lax.axis_size("af") - 1
     fetches = [
-        pltpu.make_async_copy(
-            strips_hbm.at[jnp.maximum(me - 1, 0), rows], halo_ref.at[0], sems.at[0]
-        ),
-        pltpu.make_async_copy(
-            strips_hbm.at[jnp.minimum(me + 1, last), rows], halo_ref.at[1], sems.at[1]
-        ),
-        pltpu.make_async_copy(new_hbm, new_ref, sems.at[2]),
+        pltpu.make_async_copy(halo_hbm, halo_ref, sems.at[0]),
+        pltpu.make_async_copy(new_hbm, new_ref, sems.at[1]),
     ]
     start_all(fetches)
 
@@ -813,24 +836,6 @@
 
     lower = edge_share(ylo_ref, yl_ref)
     upper = edge_share(yhi_ref, yr_ref)
-
-    width = slots * BLK
-    quarter = AVG_ROWS // FACES
-    per_tile = LANES // width
-    part = lane_ids((quarter, LANES)) // width
-    columns = []
-    for tile in range(group * BLK // LANES):
-        rows = []
-        for index in range(FACES):
-            merged = jnp.zeros((quarter, LANES), jnp.float32)
-            for place in range(per_tile):
-                piece = roll_lanes(avg_ref[tile * per_tile + place], (place - index) * width)
-                merged = jnp.where(part == place, piece, merged)
-            rows.append(merged)
-        columns.append(jnp.concatenate(rows, axis=0))
-    high, low = split_pair(jnp.concatenate(columns, axis=1))
-    ones = jnp.ones((16, high.shape[1]), jnp.bfloat16)
-    stacked = jnp.concatenate([high, low, ones], axis=0)
 
     for copy in fetches:
         copy.wait()
@@ -864,18 +869,7 @@
     after = side_share(xhi_ref, 1, me < last)
     block_cols = cells_x // BLK
     for column in range(block_cols):
-        placed = lax.dot_general(
-            stacked,
-            selector(place_ref, column, cells_y),
-            (((1,), (1,)), ((), ())),
-            preferred_element_type=jnp.float32,
-        )
-        covered = placed[2 * AVG_ROWS : 2 * AVG_ROWS + 8] > 0.5
         for plane in range(PLANES):
-            values = (
-                placed[plane * BLK : (plane + 1) * BLK]
-                + placed[AVG_ROWS + plane * BLK : AVG_ROWS + (plane + 1) * BLK]
-            )
             row = plane * cells_x + column * BLK
             edge_rows = slice(column * BLK, (column + 1) * BLK)
             for half in range(halves):
@@ -893,6 +887,48 @@
                 if half == halves - 1:
                     share = roll_lanes(upper[edge_rows], LANES - 1 - plane)
                     coarse = coarse + jnp.where(lane == LANES - 1, share, 0.0)
+                out_ref[row : row + BLK, cols] = coarse
+
+
+def place_kernel(
+    place_ref, avg_ref, new_ref, out_ref, *, cells_x, cells_y, group, slots
+):
+    width = slots * BLK
+    quarter = AVG_ROWS // FACES
+    per_tile = LANES // width
+    part = lane_ids((quarter, LANES)) // width
+    columns = []
+    for tile in range(group * BLK // LANES):
+        rows = []
+        for index in range(FACES):
+            merged = jnp.zeros((quarter, LANES), jnp.float32)
+            for place in range(per_tile):
+                piece = roll_lanes(avg_ref[tile * per_tile + place], (place - index) * width)
+                merged = jnp.where(part == place, piece, merged)
+            rows.append(merged)
+        columns.append(jnp.concatenate(rows, axis=0))
+    high, low = split_pair(jnp.concatenate(columns, axis=1))
+    ones = jnp.ones((16, high.shape[1]), jnp.bfloat16)
+    stacked = jnp.concatenate([high, low, ones], axis=0)
+
+    halves = cells_y // LANES
+    for column in range(cells_x // BLK):
+        placed = lax.dot_general(
+            stacked,
+            selector(place_ref, column, cells_y),
+            (((1,), (1,)), ((), ())),
+            preferred_element_type=jnp.float32,
+        )
+        covered = placed[2 * AVG_ROWS : 2 * AVG_ROWS + 8] > 0.5
+        for plane in range(PLANES):
+            values = (
+                placed[plane * BLK : (plane + 1) * BLK]
+                + placed[AVG_ROWS + plane * BLK : AVG_ROWS + (plane + 1) * BLK]
+            )
+            row = plane * cells_x + column * BLK
+            for half in range(halves):
+                cols = slice(half * LANES, (half + 1) * LANES)
+                coarse = new_ref[row : row + BLK, cols]
                 out_ref[row : row + BLK, cols] = jnp.where(
                     covered[:, cols], values[:, cols], coarse
                 )
@@ -974,72 +1010,88 @@
 
     strips = exchange(send)
 
+    ylo_sent, yhi_sent = pl.pallas_call(
+        hand_on_kernel,
+        out_shape=[f32(cells_x, LANES)] * 2,
+        in_specs=[VMEM] * 2,
+        out_specs=[VMEM] * 2,
+        name="hand_on",
+    )(ylo, yhi)
+    yl = shifted(yhi_sent, "col", 1)
+    yr = shifted(ylo_sent, "col", -1)
+
     kept = [hbm32(slots * size, LANES) for size in (FIELD_ROWS, COEFF_ROWS, UPWARD_ROWS)]
     kept_scratch = [pltpu.VMEM((slots * size, LANES), jnp.float32)
         for size in (FIELD_ROWS, COEFF_ROWS, UPWARD_ROWS)]
-    fields, coeffs, upward, ylo_sent, yhi_sent = pl.pallas_call(
+    fields, coeffs, upward = pl.pallas_call(
         functools.partial(prepare_kernel, slots=slots),
-        out_shape=kept + [f32(cells_x, LANES)] * 2,
-        in_specs=[HBM] * 4 + [VMEM] * 2,
-        out_specs=[HBM] * 3 + [VMEM] * 2,
+        out_shape=kept,
+        in_specs=[VMEM] + [HBM] * 3,
+        out_specs=[HBM] * 3,
         scratch_shapes=kept_scratch
         + [
             pltpu.VMEM(fine_state.shape, jnp.float32),
             pltpu.VMEM(fine_kappa.shape, jnp.float32),
             pltpu.VMEM(fine_rate.shape, jnp.float32),
-            pltpu.VMEM((FIELD_ROWS, LANES), jnp.float32),
-            pltpu.VMEM((UPWARD_ROWS, LANES), jnp.float32),
+            pltpu.VMEM((slots * FIELD_ROWS, LANES), jnp.float32),
+            pltpu.VMEM((slots * UPWARD_ROWS, LANES), jnp.float32),
             pltpu.SemaphoreType.DMA((3, slots)),
             pltpu.SemaphoreType.DMA((3, slots)),
         ],
         compiler_params=PARAMS,
         name="prepare",
-    )(*pinned(new, fine_state, fine_kappa, fine_rate), ylo, yhi)
-    yl = shifted(yhi_sent, "col", 1)
-    yr = shifted(ylo_sent, "col", -1)
+    )(ylo_sent, *pinned(fine_state, fine_kappa, fine_rate))
 
     chunk = (AVG_ROWS // FACES, LANES)
-    fine_out, averages = pl.pallas_call(
+    halo_shape = (2, halves * EDGE_ROWS, LANES)
+    fine_out, averages, halo = pl.pallas_call(
         functools.partial(finish_kernel, slots=slots),
-        out_shape=[hbm32(*fine_state.shape), hbm32(af_count, *chunk)],
-        in_specs=[HBM] * 4 + [VMEM] * 2,
-        out_specs=[HBM, HBM],
-        scratch_shapes=[pltpu.VMEM((af_count, HALO_START, LANES), jnp.float32)]
-        + kept_scratch
+        out_shape=[hbm32(*fine_state.shape), hbm32(af_count, *chunk), hbm32(*halo_shape)],
+        in_specs=[VMEM] + [HBM] * 3 + [VMEM] * 2,
+        out_specs=[HBM] * 3,
+        scratch_shapes=kept_scratch
         + [
             pltpu.VMEM((2 * LANES, EDGE * EDGE), jnp.bfloat16),
             pltpu.VMEM((2 * SPECIES * FZ, STRIP_ROWS), jnp.bfloat16),
             pltpu.VMEM((2 * LANES, LANES), jnp.bfloat16),
             pltpu.VMEM(chunk, jnp.float32),
-            pltpu.VMEM((FIELD_ROWS, LANES), jnp.float32),
-            pltpu.VMEM((FIELD_ROWS, LANES), jnp.float32),
+            pltpu.VMEM((slots * FIELD_ROWS, LANES), jnp.float32),
             pltpu.VMEM((SPECIES * TILES * FZ, LANES), jnp.float32),
             pltpu.VMEM((SPECIES * TILES * FZ, LANES), jnp.float32),
             pltpu.VMEM(fine_state.shape, jnp.float32),
             pltpu.SemaphoreType.DMA((slots,)),
             pltpu.SemaphoreType.DMA((3, slots)),
-            pltpu.SemaphoreType.DMA,
+            pltpu.SemaphoreType.DMA((2,)),
             pltpu.SemaphoreType.DMA((af_count,)),
         ],
         compiler_params=PARAMS,
         name="finish",
-    )(*pinned(strips, fields, coeffs, upward), yl, yr)
+    )(strips, *pinned(fields, coeffs, upward), yl, yr)
 
     arrived = exchange(averages)
+
+    whole = pl.pallas_call(
+        functools.partial(edges_kernel, cells_x=cells_x, cells_y=cells_y),
+        out_shape=f32(rows, cells_y),
+        in_specs=[HBM] * 2 + [VMEM] * 6,
+        out_specs=VMEM,
+        scratch_shapes=[
+            pltpu.VMEM((rows, cells_y), jnp.float32),
+            pltpu.VMEM(halo_shape, jnp.float32),
+            pltpu.SemaphoreType.DMA((2,)),
+        ],
+        compiler_params=PARAMS,
+        name="edges",
+    )(*pinned(new, halo), xlo, xhi, ylo, yhi, yl, yr)
 
     placed = pl.pallas_call(
         functools.partial(place_kernel, slots=slots, **sizes),
         out_shape=f32(rows, cells_y),
-        in_specs=[VMEM] * 2 + [HBM] * 2 + [VMEM] * 6,
+        in_specs=[VMEM] * 3,
         out_specs=VMEM,
-        scratch_shapes=[
-            pltpu.VMEM((rows, cells_y), jnp.float32),
-            pltpu.VMEM((2, halves * EDGE_ROWS, LANES), jnp.float32),
-            pltpu.SemaphoreType.DMA((3,)),
-        ],
         compiler_params=PARAMS,
         name="place",
-    )(place, arrived, *pinned(new, strips), xlo, xhi, ylo, yhi, yl, yr)
+    )(place, arrived, whole)
     return (placed.reshape(coarse_state.shape), fine_out)
 
 

time: 53.9 us -> 51.7 us (0.959)
  the two profiles are of different devices: /device:TPU:0 before, /device:TPU:2 now
where the time goes in v1:
time: 51.7 us; the launch traced here: 51.2 us
  Pallas kernels  24.7 us (48%)
  starting transfers between devices  17.4 us (34%)
  waiting for transfers between devices  6.54 us (13%)
  local copies, waits for them, and re-layouts  1.89 us (4%)
  between operations  0.75 us (1%)
    all_to_all x2, starting transfers between devices, exchange(): return lax.all_to_all(chunks, 'af', split_axis=0, concat_axis=0, tiled=True)  11.8 us
    pallas_call x1, Pallas kernels, per_device(): pl.pallas_call(functools.partial(finish_kernel, slots=slots), out_shape=[...  10.2 us
    pallas_call x1, Pallas kernels, per_device(): pl.pallas_call(functools.partial(prepare_kernel, slots=slots), out_shape=...  6.96 us
    all_to_all x2, waiting for transfers between devices, exchange(): return lax.all_to_all(chunks, 'af', split_axis=0, concat_axis=0, tiled=True)  6.54 us
    ppermute x2, starting transfers between devices, shifted(): return lax.ppermute(values, axis, pairs)  5.55 us
    pallas_call x1, Pallas kernels, per_device(): pl.pallas_call(functools.partial(strips_kernel, slots=slots, **sizes), ou...  3.8 us
    unnamed x10, local copies, waits for them, and re-layouts  1.89 us
    pallas_call x1, Pallas kernels, per_device(): pl.pallas_call(hand_on_kernel, out_shape=[f32(cells_x, LANES)] * 2, in_sp...  1.32 us
  transfers between devices with their start and end apart: 4, of which 1 were waited for; matrix products, arithmetic and copies ran while one was open for 0% of the time, Pallas kernels for 19%

profile of v1, /device:TPU:2, one launch (start us, length us, event | category | flops | bytes accessed | tf_op | source)
XLA Modules:
  0.0 51.2 jit_solution(7557695001841752058)
XLA Ops:
  0.6 3.8 %strips.1 = (f32[384,256]{1,0:T(8,128)}, f32[8,128,128]{2,1,0:T(8,128)}, s32[16,256]{1,0:T(8,128)S(1)}, f32[32,256]{1,0:T(8,128)S(1)}, f32[32,256]{1,0:T(8,128)S...) custom-call(s32[2,128]{1,0:T(2,128)} %bitcast.9, f32[384,256]{1,0:T(8,128)} %bitcast.5, f32[128,256]{1,0:T(8,128)} %bitcast.7, ...), custom_call_target="tpu_custom_call" | custom-call | tf_op jit(solution)/shard_map/strips/pallas_call | solution.py:979
  4.4 0.0 copy-start
  4.4 0.6 %copy-done = f32[16,128]{1,0:T(8,128)} copy-done((f32[16,128]{1,0:T(8,128)}, f32[16,128]{1,0:T(8,128)S(1)}, u32[]{:S(2)}) %copy-start) | copy-done | bytes 8216
  5.0 0.0 copy-start.2
  5.0 0.6 %copy-done.2 = f32[16,128]{1,0:T(8,128)} copy-done((f32[16,128]{1,0:T(8,128)}, f32[16,128]{1,0:T(8,128)S(1)}, u32[]{:S(2)}) %copy-start.2) | copy-done | bytes 8216
  5.6 5.8 %all-to-all-start = ((f32[8,128,128]{2,1,0:T(8,128)}), f32[8,128,128]{2,1,0:T(8,128)S(1)}, u32[]{:S(2)}, u32[]{:S(2)}) async-start(f32[8,128,128]{2,1,0:T(8,128)} %get-tuple-element.18), calls=%async_computation | async-start | bytes 1048576 | tf_op jit(solution)/shard_map/all_to_all | solution.py:961
  11.5 1.3 %hand_on.1 = (f32[16,128]{1,0:T(8,128)}, f32[16,128]{1,0:T(8,128)}) custom-call(f32[16,128]{1,0:T(8,128)} %copy-done, f32[16,128]{1,0:T(8,128)} %copy-done.2), custom_call_target="tpu_custom_call" | custom-call | tf_op jit(solution)/shard_map/hand_on/pallas_call | solution.py:1013
  12.8 1.9 %collective-permute-start = (f32[16,128]{1,0:T(8,128)}, f32[16,128]{1,0:T(8,128)S(1)}, u32[]{:S(2)}, u32[]{:S(2)}) collective-permute-start(f32[16,128]{1,0:T(8,128)} %get-tuple-element.25), channel_id=1, source_target_pairs={{0,8},{8,16},{16,24},{1,9},{9,17},{17,25},{2,10},{10,18},{18,26},{... | collective-permute-start | bytes 24584 | tf_op jit(solution)/shard_map/ppermute | solution.py:957
  14.7 3.6 %collective-permute-start.1 = (f32[16,128]{1,0:T(8,128)}, f32[16,128]{1,0:T(8,128)S(1)}, u32[]{:S(2)}, u32[]{:S(2)}) collective-permute-start(f32[16,128]{1,0:T(8,128)} %get-tuple-element.21.after_ref), channel_id=1, source_target_pairs={{8,0},{16,8},{24,16},{9,1},{17,9},{25,17},{10,2},{18,10},{26,18},{... | collective-permute-start | bytes 24584 | tf_op jit(solution)/shard_map/ppermute | solution.py:957
  18.3 0.0 copy-start.4
  18.4 0.7 %copy-done.4 = f32[16,128]{1,0:T(8,128)S(1)} copy-done((f32[16,128]{1,0:T(8,128)S(1)}, f32[16,128]{1,0:T(8,128)}, u32[]{:S(2)}) %copy-start.4) | copy-done | bytes 8216
  19.1 7.0 %prepare.1 = (f32[4608,128]{1,0:T(8,128)}, f32[9216,128]{1,0:T(8,128)}, f32[1536,128]{1,0:T(8,128)}) custom-call(f32[16,128]{1,0:T(8,128)S(1)} %copy-done.4, f32[4,3,32,1024]{3,2,1,0:T(8,128)} %state_hbm.1, f32[4,32,1024]{2,1,0:T(8,128)} %kappa_hbm.1, f32[4,32,1024]{2,1,0:T(8,128)} %rate_hbm.1), custom_call_target="tpu_custom_call" | custom-call | tf_op jit(solution)/shard_map/prepare/pallas_call | solution.py:1026
  26.0 0.0 collective-permute-done.yl_ref
  26.0 0.0 collective-permute-done.1.yr_ref
  26.0 0.0 all-to-all-done.strips_ref
  26.1 0.0 copy-start.1
  26.1 0.0 copy-start.3
  26.1 10.2 %finish.1 = (f32[4,3,32,1024]{3,2,1,0:T(8,128)}, f32[8,48,128]{2,1,0:T(8,128)}, f32[2,64,128]{2,1,0:T(8,128)}) custom-call(f32[8,128,128]{2,1,0:T(8,128)S(1)} %all-to-all-done.strips_ref, f32[4608,128]{1,0:T(8,128)} %get-tuple-element.22.fields_hbm, f32[9216,128]{1,0:T(8,128)} %get-tuple-element.23.coeffs_hbm, f32[1536,128]{1,0:T(8,128)} %get-tuple-element.24.upward_hbm, ...), custom_call_target="tpu_custom_call" | custom-call | tf_op jit(solution)/shard_map/finish/pallas_call | solution.py:1047
  36.2 6.0 %all-to-all-start.1 = ((f32[8,48,128]{2,1,0:T(8,128)}), f32[8,48,128]{2,1,0:T(8,128)S(1)}, u32[]{:S(2)}, u32[]{:S(2)}) async-start(f32[8,48,128]{2,1,0:T(8,128)} %get-tuple-element.26), calls=%async_computation.1 | async-start | bytes 393216 | tf_op jit(solution)/shard_map/all_to_all | solution.py:961
  42.3 0.0 copy-done.1
  42.3 0.0 copy-done.3
  42.3 1.2 %edges.1.new_ref = f32[384,256]{1,0:T(8,128)S(1)} custom-call(f32[384,256]{1,0:T(8,128)} %get-tuple-element.27.new_hbm, f32[2,64,128]{2,1,0:T(8,128)} %get-tuple-element.28.halo_hbm, f32[32,256]{1,0:T(8,128)S(1)} %get-tuple-element.29.xlo_ref, f32[32,256]{1,0:T(8,128)S(1)} %get-tuple-element.30.xhi_ref, f32[16,128]{1,0:T(8,128)S(1)} %copy-done.1, ...), custom_call_target="tpu_custom_call" | custom-call | tf_op jit(solution)/shard_map/edges/pallas_call | solution.py:1073
  43.5 6.5 %all-to-all-done.1.avg_ref = f32[8,48,128]{2,1,0:T(8,128)S(1)} async-done(((f32[8,48,128]{2,1,0:T(8,128)}), f32[8,48,128]{2,1,0:T(8,128)S(1)}, u32[]{:S(2)}, u32[]{:S(2)}) %all-to-all-start.1) | async-done | bytes 196640 | tf_op jit(solution)/shard_map/all_to_all | solution.py:961
  50.0 1.2 %place.1 = f32[384,256]{1,0:T(8,128)} custom-call(s32[16,256]{1,0:T(8,128)S(1)} %get-tuple-element.17.place_ref, f32[8,48,128]{2,1,0:T(8,128)S(1)} %all-to-all-done.1.avg_ref, f32[384,256]{1,0:T(8,128)S(1)} %edges.1.new_ref), custom_call_target="tpu_custom_call" | custom-call | tf_op jit(solution)/shard_map/place/pallas_call | solution.py:1087
Async XLA Ops:
  4.4 0.6 %copy-start = (f32[16,128]{1,0:T(8,128)}, f32[16,128]{1,0:T(8,128)S(1)}, u32[]{:S(2)}) copy-start(f32[16,128]{1,0:T(8,128)S(1)} %get-tuple-element.19.ylo_ref) | copy-start | bytes 24580
  5.0 0.6 %copy-start.2 = (f32[16,128]{1,0:T(8,128)}, f32[16,128]{1,0:T(8,128)S(1)}, u32[]{:S(2)}) copy-start(f32[16,128]{1,0:T(8,128)S(1)} %get-tuple-element.20.yhi_ref) | copy-start | bytes 24580
  5.6 20.4 %all-to-all-start = ((f32[8,128,128]{2,1,0:T(8,128)}), f32[8,128,128]{2,1,0:T(8,128)S(1)}, u32[]{:S(2)}, u32[]{:S(2)}) async-start(f32[8,128,128]{2,1,0:T(8,128)} %get-tuple-element.18), calls=%async_computation | async-start | bytes 1048576 | tf_op jit(solution)/shard_map/all_to_all | solution.py:961
  12.8 13.2 %collective-permute-start = (f32[16,128]{1,0:T(8,128)}, f32[16,128]{1,0:T(8,128)S(1)}, u32[]{:S(2)}, u32[]{:S(2)}) collective-permute-start(f32[16,128]{1,0:T(8,128)} %get-tuple-element.25), channel_id=1, source_target_pairs={{0,8},{8,16},{16,24},{1,9},{9,17},{17,25},{2,10},{10,18},{18,26},{... | collective-permute-start | bytes 24584 | tf_op jit(solution)/shard_map/ppermute | solution.py:957
  14.7 11.3 %collective-permute-start.1 = (f32[16,128]{1,0:T(8,128)}, f32[16,128]{1,0:T(8,128)S(1)}, u32[]{:S(2)}, u32[]{:S(2)}) collective-permute-start(f32[16,128]{1,0:T(8,128)} %get-tuple-element.21.after_ref), channel_id=1, source_target_pairs={{8,0},{16,8},{24,16},{9,1},{17,9},{25,17},{10,2},{18,10},{26,18},{... | collective-permute-start | bytes 24584 | tf_op jit(solution)/shard_map/ppermute | solution.py:957
  18.3 0.7 %copy-start.4 = (f32[16,128]{1,0:T(8,128)S(1)}, f32[16,128]{1,0:T(8,128)}, u32[]{:S(2)}) copy-start(f32[16,128]{1,0:T(8,128)} %get-tuple-element.21.after_ref) | copy-start | bytes 24580
  26.1 16.2 %copy-start.1 = (f32[16,128]{1,0:T(8,128)S(1)}, f32[16,128]{1,0:T(8,128)}, u32[]{:S(2)}) copy-start(f32[16,128]{1,0:T(8,128)} %copy-done) | copy-start | bytes 24580
  26.1 16.2 %copy-start.3 = (f32[16,128]{1,0:T(8,128)S(1)}, f32[16,128]{1,0:T(8,128)}, u32[]{:S(2)}) copy-start(f32[16,128]{1,0:T(8,128)} %copy-done.2) | copy-start | bytes 24580
  36.2 13.8 %all-to-all-start.1 = ((f32[8,48,128]{2,1,0:T(8,128)}), f32[8,48,128]{2,1,0:T(8,128)S(1)}, u32[]{:S(2)}, u32[]{:S(2)}) async-start(f32[8,48,128]{2,1,0:T(8,128)} %get-tuple-element.26), calls=%async_computation.1 | async-start | bytes 393216 | tf_op jit(solution)/shard_map/all_to_all | solution.py:961

commit v2 on v1

--- a/solution.py
+++ b/solution.py
@@ -28,7 +28,7 @@
 UPWARD_ROWS = TILES * STRIDE
 EDGE_ROWS = PLANES + NZC
 BESIDE_ROWS = 2 * NZC
-HALO_START = STRIP_ROWS + BESIDE_ROWS
+CHUNK_ROWS = STRIP_ROWS + BESIDE_ROWS
 
 DT_COARSE = 1.0 / 28.0
 DIFFUSE = (1.0, 0.7, 0.45)
@@ -249,11 +249,11 @@
         below = jnp.zeros((STRIP_ROWS, cells_y), jnp.float32)
         above = jnp.zeros((STRIP_ROWS, cells_y), jnp.float32)
         for x in range(BLK):
-            strip = rows_at(column * BLK + x)
-            below = jnp.where(spot == x, roll_lanes(strip, x + 1), below)
-            above = jnp.where(spot == x, roll_lanes(strip, x - BLK), above)
+            turned = roll_lanes(rows_at(column * BLK + x), x + 1)
+            below = jnp.where(spot == x, turned, below)
+            above = jnp.where(spot == (x + 1) % BLK, turned, above)
         lower_y.append(below)
-        upper_y.append(above)
+        upper_y.append(roll_lanes(above, -1 - BLK))
 
     first_row = edge_at(0)
     last_row = edge_at(cells_x - 1)
@@ -325,7 +325,6 @@
             at += 2 * size
 
     width = slots * BLK
-    me = lax.axis_index("af")
     for target in range(group // slots):
         first = target * width
         tile = first // LANES * LANES
@@ -342,12 +341,6 @@
                     part == index, roll_lanes(piece, index * width - (first - tile)), chunk
                 )
             send_ref[target, start : start + size, :] = chunk
-        halo = jnp.where(me < target, last_row, first_row)
-        for half in range(halves):
-            start = HALO_START + half * EDGE_ROWS
-            send_ref[target, start : start + EDGE_ROWS, :] = halo[
-                :, half * LANES : (half + 1) * LANES
-            ]
     keep_new.wait()
 
 
@@ -491,9 +484,9 @@
     lax.fori_loop(0, ref.shape[0] // STRIDE, body, 0)
 
 
-def hand_on_kernel(ylo_ref, yhi_ref, ylo_out, yhi_out):
-    ylo_out[...] = ylo_ref[...]
-    yhi_out[...] = yhi_ref[...]
+def hand_on_kernel(low_ref, high_ref, low_out, high_out):
+    low_out[...] = low_ref[...]
+    high_out[...] = high_ref[...]
 
 
 def prepare_kernel(
@@ -641,11 +634,10 @@
     fields_hbm,
     coeffs_hbm,
     upward_hbm,
-    yl_ref,
-    yr_ref,
+    xl_ref,
+    xr_ref,
     out_hbm,
     avg_hbm,
-    halo_hbm,
     fields_ref,
     coeffs,
     upward,
@@ -659,20 +651,11 @@
     staged,
     sems,
     in_sems,
-    halo_sems,
     avg_sems,
     *,
     slots,
 ):
     sources = strips_ref.shape[0]
-    me = lax.axis_index("af")
-    halo_rows = pl.ds(HALO_START, halo_hbm.shape[1])
-    halos = [
-        pltpu.make_async_copy(
-            strips_ref.at[source, halo_rows], halo_hbm.at[side], halo_sems.at[side]
-        )
-        for side, source in enumerate((jnp.maximum(me - 1, 0), jnp.minimum(me + 1, sources - 1)))
-    ]
 
     def loads(slot):
         return [
@@ -691,16 +674,15 @@
         ]
 
     start_all(loads(0))
-    start_all(halos)
     clear_pads(first)
     for tile in range(TILES):
         ghost_ref[:, tile * LANES : (tile + 1) * LANES] = ghost_table(tile)
     plane_ref[...] = plane_table()
     mean_ref[...] = mean_table()
 
-    gathered = strips_ref[0, 0:HALO_START]
+    gathered = strips_ref[0]
     for source in range(1, sources):
-        gathered = gathered + strips_ref[source, 0:HALO_START]
+        gathered = gathered + strips_ref[source]
     old, new = complete_strips(gathered)
     gathered = jnp.concatenate([old, (new - old) * (1.0 / RATIO)], axis=0)
     quarter = AVG_ROWS // FACES
@@ -792,36 +774,31 @@
     start_all(copies)
     for copy in copies:
         copy.wait()
-    for copy in halos:
-        copy.wait()
     for slot in range(slots):
         send_out(slot).wait()
 
 
 def edges_kernel(
     new_hbm,
-    halo_hbm,
     xlo_ref,
     xhi_ref,
     ylo_ref,
     yhi_ref,
+    xl_ref,
+    xr_ref,
     yl_ref,
     yr_ref,
     out_ref,
     new_ref,
-    halo_ref,
-    sems,
+    sem,
     *,
     cells_x,
     cells_y,
 ):
     me = lax.axis_index("af")
     last = lax.axis_size("af") - 1
-    fetches = [
-        pltpu.make_async_copy(halo_hbm, halo_ref, sems.at[0]),
-        pltpu.make_async_copy(new_hbm, new_ref, sems.at[1]),
-    ]
-    start_all(fetches)
+    fetch = pltpu.make_async_copy(new_hbm, new_ref, sem)
+    fetch.start()
 
     def edge_share(own_ref, other_ref):
         own = own_ref[...]
@@ -837,17 +814,15 @@
     lower = edge_share(ylo_ref, yl_ref)
     upper = edge_share(yhi_ref, yr_ref)
 
-    for copy in fetches:
-        copy.wait()
     lane = lane_ids((BLK, LANES))
     row_id = lax.broadcasted_iota(jnp.int32, (BLK, LANES), 0)
     halves = cells_y // LANES
 
-    def side_share(own_ref, side, exists):
+    def side_share(own_ref, other_ref, exists):
         shares = []
         for half in range(halves):
             own = own_ref[:, half * LANES : (half + 1) * LANES]
-            other = halo_ref[side, half * EDGE_ROWS : (half + 1) * EDGE_ROWS]
+            other = other_ref[:, half * LANES : (half + 1) * LANES]
             coeff = face(DT_COARSE, own[PLANES:], other[PLANES:])
             coeff = jnp.where(exists, coeff, 0.0)
             shares.append(
@@ -865,8 +840,9 @@
             )
         return shares
 
-    before = side_share(xlo_ref, 0, me > 0)
-    after = side_share(xhi_ref, 1, me < last)
+    before = side_share(xlo_ref, xl_ref, me > 0)
+    after = side_share(xhi_ref, xr_ref, me < last)
+    fetch.wait()
     block_cols = cells_x // BLK
     for column in range(block_cols):
         for plane in range(PLANES):
@@ -975,12 +951,11 @@
     sizes = dict(cells_x=cells_x, cells_y=cells_y, group=group)
 
     span = cells_x + 2 * PAD
-    chunk_rows = HALO_START + halves * EDGE_ROWS
     new, send, place, xlo, xhi, ylo, yhi = pl.pallas_call(
         functools.partial(strips_kernel, slots=slots, **sizes),
         out_shape=[
             hbm32(rows, cells_y),
-            f32(af_count, chunk_rows, LANES),
+            f32(af_count, CHUNK_ROWS, LANES),
             jax.ShapeDtypeStruct((16, lanes), jnp.int32),
         ]
         + [f32(EDGE_ROWS, cells_y)] * 2
@@ -1010,15 +985,16 @@
 
     strips = exchange(send)
 
-    ylo_sent, yhi_sent = pl.pallas_call(
+    xlo_sent, xhi_sent = pl.pallas_call(
         hand_on_kernel,
-        out_shape=[f32(cells_x, LANES)] * 2,
+        out_shape=[f32(EDGE_ROWS, cells_y)] * 2,
         in_specs=[VMEM] * 2,
         out_specs=[VMEM] * 2,
+        compiler_params=pltpu.CompilerParams(vmem_limit_bytes=1024 * 1024),
         name="hand_on",
-    )(ylo, yhi)
-    yl = shifted(yhi_sent, "col", 1)
-    yr = shifted(ylo_sent, "col", -1)
+    )(xlo, xhi)
+    xl = shifted(xhi_sent, "af", 1)
+    xr = shifted(xlo_sent, "af", -1)
 
     kept = [hbm32(slots * size, LANES) for size in (FIELD_ROWS, COEFF_ROWS, UPWARD_ROWS)]
     kept_scratch = [pltpu.VMEM((slots * size, LANES), jnp.float32)
@@ -1040,15 +1016,14 @@
         ],
         compiler_params=PARAMS,
         name="prepare",
-    )(ylo_sent, *pinned(fine_state, fine_kappa, fine_rate))
+    )(xlo_sent, *pinned(fine_state, fine_kappa, fine_rate))
 
     chunk = (AVG_ROWS // FACES, LANES)
-    halo_shape = (2, halves * EDGE_ROWS, LANES)
-    fine_out, averages, halo = pl.pallas_call(
+    fine_out, averages = pl.pallas_call(
         functools.partial(finish_kernel, slots=slots),
-        out_shape=[hbm32(*fine_state.shape), hbm32(af_count, *chunk), hbm32(*halo_shape)],
+        out_shape=[hbm32(*fine_state.shape), hbm32(af_count, *chunk)],
         in_specs=[VMEM] + [HBM] * 3 + [VMEM] * 2,
-        out_specs=[HBM] * 3,
+        out_specs=[HBM] * 2,
         scratch_shapes=kept_scratch
         + [
             pltpu.VMEM((2 * LANES, EDGE * EDGE), jnp.bfloat16),
@@ -1061,28 +1036,25 @@
             pltpu.VMEM(fine_state.shape, jnp.float32),
             pltpu.SemaphoreType.DMA((slots,)),
             pltpu.SemaphoreType.DMA((3, slots)),
-            pltpu.SemaphoreType.DMA((2,)),
             pltpu.SemaphoreType.DMA((af_count,)),
         ],
         compiler_params=PARAMS,
         name="finish",
-    )(strips, *pinned(fields, coeffs, upward), yl, yr)
+    )(strips, *pinned(fields, coeffs, upward), xl, xr)
 
     arrived = exchange(averages)
 
+    yl = shifted(yhi, "col", 1)
+    yr = shifted(ylo, "col", -1)
     whole = pl.pallas_call(
         functools.partial(edges_kernel, cells_x=cells_x, cells_y=cells_y),
         out_shape=f32(rows, cells_y),
-        in_specs=[HBM] * 2 + [VMEM] * 6,
+        in_specs=[HBM] + [VMEM] * 8,
         out_specs=VMEM,
-        scratch_shapes=[
-            pltpu.VMEM((rows, cells_y), jnp.float32),
-            pltpu.VMEM(halo_shape, jnp.float32),
-            pltpu.SemaphoreType.DMA((2,)),
-        ],
+        scratch_shapes=[pltpu.VMEM((rows, cells_y), jnp.float32), pltpu.SemaphoreType.DMA],
         compiler_params=PARAMS,
         name="edges",
-    )(*pinned(new, halo), xlo, xhi, ylo, yhi, yl, yr)
+    )(*pinned(new), xlo, xhi, ylo, yhi, xl, xr, yl, yr)
 
     placed = pl.pallas_call(
         functools.partial(place_kernel, slots=slots, **sizes),

time: 51.7 us -> 50.3 us (0.973)
  the two profiles are of different devices: /device:TPU:2 before, /device:TPU:0 now
where the time goes in v2:
time: 50.3 us; the launch traced here: 49.8 us
  starting transfers between devices  23.5 us (47%)
  Pallas kernels  23.3 us (46%)
  waiting for transfers between devices  2.27 us (5%)
  between operations  0.73 us (1%)
    all_to_all x2, starting transfers between devices, exchange(): return lax.all_to_all(chunks, 'af', split_axis=0, concat_axis=0, tiled=True)  13.9 us
    pallas_call x1, Pallas kernels, per_device(): pl.pallas_call(functools.partial(finish_kernel, slots=slots), out_shape=[...  10.1 us
    ppermute x4, starting transfers between devices, shifted(): return lax.ppermute(values, axis, pairs)  9.53 us
    pallas_call x1, Pallas kernels, per_device(): pl.pallas_call(functools.partial(prepare_kernel, slots=slots), out_shape=...  6.96 us
    pallas_call x1, Pallas kernels, per_device(): pl.pallas_call(functools.partial(strips_kernel, slots=slots, **sizes), ou...  3.89 us
    all_to_all x2, waiting for transfers between devices, exchange(): return lax.all_to_all(chunks, 'af', split_axis=0, concat_axis=0, tiled=True)  1.47 us
    pallas_call x1, Pallas kernels, per_device(): pl.pallas_call(functools.partial(place_kernel, slots=slots, **sizes), out...  1.21 us
    pallas_call x1, Pallas kernels, per_device(): pl.pallas_call(functools.partial(edges_kernel, cells_x=cells_x, cells_y=c...  1.17 us
  transfers between devices with their start and end apart: 6, of which 2 were waited for; matrix products, arithmetic and copies ran while one was open for 0% of the time, Pallas kernels for 16%

profile of v2, /device:TPU:0, one launch (start us, length us, event | category | flops | bytes accessed | tf_op | source)
XLA Modules:
  0.0 49.8 jit_solution(1667913054346416884)
XLA Ops:
  0.6 3.9 %strips.1 = (f32[384,256]{1,0:T(8,128)}, f32[8,64,128]{2,1,0:T(8,128)}, s32[16,256]{1,0:T(8,128)S(1)}, f32[32,256]{1,0:T(8,128)S(1)}, f32[32,256]{1,0:T(8,128)S(...) custom-call(s32[2,128]{1,0:T(2,128)} %bitcast.9, f32[384,256]{1,0:T(8,128)} %bitcast.5, f32[128,256]{1,0:T(8,128)} %bitcast.7, ...), custom_call_target="tpu_custom_call" | custom-call | tf_op jit(solution)/shard_map/strips/pallas_call | solution.py:954
  4.5 7.3 %all-to-all-start = ((f32[8,64,128]{2,1,0:T(8,128)}), f32[8,64,128]{2,1,0:T(8,128)S(1)}, u32[]{:S(2)}, u32[]{:S(2)}) async-start(f32[8,64,128]{2,1,0:T(8,128)} %get-tuple-element.17), calls=%async_computation | async-start | bytes 524288 | tf_op jit(solution)/shard_map/all_to_all | solution.py:937
  11.8 3.9 %collective-permute-start = (f32[32,256]{1,0:T(8,128)S(1)}, f32[32,256]{1,0:T(8,128)S(1)}, u32[]{:S(2)}, u32[]{:S(2)}) collective-permute-start(f32[32,256]{1,0:T(8,128)S(1)} %get-tuple-element.24), channel_id=1, source_target_pairs={{0,1},{1,2},{2,3},{3,4},{4,5},{5,6},{6,7},{8,9},{9,10},{10,11},{11... | collective-permute-start | bytes 98312 | tf_op jit(solution)/shard_map/ppermute | solution.py:933
  15.8 1.3 %collective-permute-start.1 = (f32[32,256]{1,0:T(8,128)S(1)}, f32[32,256]{1,0:T(8,128)S(1)}, u32[]{:S(2)}, u32[]{:S(2)}) collective-permute-start(f32[32,256]{1,0:T(8,128)S(1)} %get-tuple-element.20.after_ref), channel_id=1, source_target_pairs={{1,0},{2,1},{3,2},{4,3},{5,4},{6,5},{7,6},{9,8},{10,9},{11,10},{12... | collective-permute-start | bytes 98312 | tf_op jit(solution)/shard_map/ppermute | solution.py:933
  17.1 7.0 %prepare.1 = (f32[4608,128]{1,0:T(8,128)}, f32[9216,128]{1,0:T(8,128)}, f32[1536,128]{1,0:T(8,128)}) custom-call(f32[32,256]{1,0:T(8,128)S(1)} %get-tuple-element.20.after_ref, f32[4,3,32,1024]{3,2,1,0:T(8,128)} %state_hbm.1, f32[4,32,1024]{2,1,0:T(8,128)} %kappa_hbm.1, f32[4,32,1024]{2,1,0:T(8,128)} %rate_hbm.1), custom_call_target="tpu_custom_call" | custom-call | tf_op jit(solution)/shard_map/prepare/pallas_call | solution.py:1002
  24.0 0.0 collective-permute-done.xl_ref
  24.0 0.0 collective-permute-done.1.xr_ref
  24.0 0.0 all-to-all-done.strips_ref
  24.1 10.1 %finish.1 = (f32[4,3,32,1024]{3,2,1,0:T(8,128)}, f32[8,48,128]{2,1,0:T(8,128)}) custom-call(f32[8,64,128]{2,1,0:T(8,128)S(1)} %all-to-all-done.strips_ref, f32[4608,128]{1,0:T(8,128)} %get-tuple-element.21.fields_hbm, f32[9216,128]{1,0:T(8,128)} %get-tuple-element.22.coeffs_hbm, f32[1536,128]{1,0:T(8,128)} %get-tuple-element.23.upward_hbm, ...), custom_call_target="tpu_custom_call" | custom-call | tf_op jit(solution)/shard_map/finish/pallas_call | solution.py:1022
  34.2 6.6 %all-to-all-start.1 = ((f32[8,48,128]{2,1,0:T(8,128)}), f32[8,48,128]{2,1,0:T(8,128)S(1)}, u32[]{:S(2)}, u32[]{:S(2)}) async-start(f32[8,48,128]{2,1,0:T(8,128)} %get-tuple-element.25), calls=%async_computation.1 | async-start | bytes 393216 | tf_op jit(solution)/shard_map/all_to_all | solution.py:937
  40.8 1.3 %collective-permute-start.3 = (f32[16,128]{1,0:T(8,128)S(1)}, f32[16,128]{1,0:T(8,128)S(1)}, u32[]{:S(2)}, u32[]{:S(2)}) collective-permute-start(f32[16,128]{1,0:T(8,128)S(1)} %get-tuple-element.27.ylo_ref), channel_id=1, source_target_pairs={{8,0},{16,8},{24,16},{9,1},{17,9},{25,17},{10,2},{18,10},{26,18},{... | collective-permute-start | bytes 24584 | tf_op jit(solution)/shard_map/ppermute | solution.py:933
  42.1 3.0 %collective-permute-start.2 = (f32[16,128]{1,0:T(8,128)S(1)}, f32[16,128]{1,0:T(8,128)S(1)}, u32[]{:S(2)}, u32[]{:S(2)}) collective-permute-start(f32[16,128]{1,0:T(8,128)S(1)} %get-tuple-element.28.yhi_ref), channel_id=1, source_target_pairs={{0,8},{8,16},{16,24},{1,9},{9,17},{17,25},{2,10},{10,18},{18,26},{... | collective-permute-start | bytes 24584 | tf_op jit(solution)/shard_map/ppermute | solution.py:933
  45.1 0.0 collective-permute-done.3.yr_ref
  45.1 0.8 %collective-permute-done.2.yl_ref = f32[16,128]{1,0:T(8,128)S(1)} collective-permute-done((f32[16,128]{1,0:T(8,128)S(1)}, f32[16,128]{1,0:T(8,128)S(1)}, u32[]{:S(2)}, u32[]{:S(2)}) %collective-permute-start.2) | collective-permute-done | bytes 8224 | tf_op jit(solution)/shard_map/ppermute | solution.py:933
  45.9 1.2 %edges.1.new_ref = f32[384,256]{1,0:T(8,128)S(1)} custom-call(f32[384,256]{1,0:T(8,128)} %get-tuple-element.26.new_hbm, f32[32,256]{1,0:T(8,128)S(1)} %get-tuple-element.18.low_ref.xlo_ref, f32[32,256]{1,0:T(8,128)S(1)} %get-tuple-element.19.high_ref.xhi_ref, f32[16,128]{1,0:T(8,128)S(1)} %get-tuple-element.27.ylo_ref, ...), custom_call_target="tpu_custom_call" | custom-call | tf_op jit(solution)/shard_map/edges/pallas_call | solution.py:1049
  47.1 1.5 %all-to-all-done.1.avg_ref = f32[8,48,128]{2,1,0:T(8,128)S(1)} async-done(((f32[8,48,128]{2,1,0:T(8,128)}), f32[8,48,128]{2,1,0:T(8,128)S(1)}, u32[]{:S(2)}, u32[]{:S(2)}) %all-to-all-start.1) | async-done | bytes 196640 | tf_op jit(solution)/shard_map/all_to_all | solution.py:937
  48.6 1.2 %place.1 = f32[384,256]{1,0:T(8,128)} custom-call(s32[16,256]{1,0:T(8,128)S(1)} %get-tuple-element.16.place_ref, f32[8,48,128]{2,1,0:T(8,128)S(1)} %all-to-all-done.1.avg_ref, f32[384,256]{1,0:T(8,128)S(1)} %edges.1.new_ref), custom_call_target="tpu_custom_call" | custom-call | tf_op jit(solution)/shard_map/place/pallas_call | solution.py:1059
  (1 shorter events, 0.0 us)
Async XLA Ops:
  4.5 19.5 %all-to-all-start = ((f32[8,64,128]{2,1,0:T(8,128)}), f32[8,64,128]{2,1,0:T(8,128)S(1)}, u32[]{:S(2)}, u32[]{:S(2)}) async-start(f32[8,64,128]{2,1,0:T(8,128)} %get-tuple-element.17), calls=%async_computation | async-start | bytes 524288 | tf_op jit(solution)/shard_map/all_to_all | solution.py:937
  11.8 12.2 %collective-permute-start = (f32[32,256]{1,0:T(8,128)S(1)}, f32[32,256]{1,0:T(8,128)S(1)}, u32[]{:S(2)}, u32[]{:S(2)}) collective-permute-start(f32[32,256]{1,0:T(8,128)S(1)} %get-tuple-element.24), channel_id=1, source_target_pairs={{0,1},{1,2},{2,3},{3,4},{4,5},{5,6},{6,7},{8,9},{9,10},{10,11},{11... | collective-permute-start | bytes 98312 | tf_op jit(solution)/shard_map/ppermute | solution.py:933
  15.8 8.3 %collective-permute-start.1 = (f32[32,256]{1,0:T(8,128)S(1)}, f32[32,256]{1,0:T(8,128)S(1)}, u32[]{:S(2)}, u32[]{:S(2)}) collective-permute-start(f32[32,256]{1,0:T(8,128)S(1)} %get-tuple-element.20.after_ref), channel_id=1, source_target_pairs={{1,0},{2,1},{3,2},{4,3},{5,4},{6,5},{7,6},{9,8},{10,9},{11,10},{12... | collective-permute-start | bytes 98312 | tf_op jit(solution)/shard_map/ppermute | solution.py:933
  34.2 14.4 %all-to-all-start.1 = ((f32[8,48,128]{2,1,0:T(8,128)}), f32[8,48,128]{2,1,0:T(8,128)S(1)}, u32[]{:S(2)}, u32[]{:S(2)}) async-start(f32[8,48,128]{2,1,0:T(8,128)} %get-tuple-element.25), calls=%async_computation.1 | async-start | bytes 393216 | tf_op jit(solution)/shard_map/all_to_all | solution.py:937
  40.8 4.3 %collective-permute-start.3 = (f32[16,128]{1,0:T(8,128)S(1)}, f32[16,128]{1,0:T(8,128)S(1)}, u32[]{:S(2)}, u32[]{:S(2)}) collective-permute-start(f32[16,128]{1,0:T(8,128)S(1)} %get-tuple-element.27.ylo_ref), channel_id=1, source_target_pairs={{8,0},{16,8},{24,16},{9,1},{17,9},{25,17},{10,2},{18,10},{26,18},{... | collective-permute-start | bytes 24584 | tf_op jit(solution)/shard_map/ppermute | solution.py:933
  42.1 3.8 %collective-permute-start.2 = (f32[16,128]{1,0:T(8,128)S(1)}, f32[16,128]{1,0:T(8,128)S(1)}, u32[]{:S(2)}, u32[]{:S(2)}) collective-permute-start(f32[16,128]{1,0:T(8,128)S(1)} %get-tuple-element.28.yhi_ref), channel_id=1, source_target_pairs={{0,8},{8,16},{16,24},{1,9},{9,17},{17,25},{2,10},{10,18},{18,26},{... | collective-permute-start | bytes 24584 | tf_op jit(solution)/shard_map/ppermute | solution.py:933

commit v3 on v2

--- a/solution.py
+++ b/solution.py
@@ -22,9 +22,10 @@
 PLANES = SPECIES * NZC
 STRIP_ROWS = 2 * PLANES
 AVG_ROWS = PLANES * BLK
-KINDS = 9
+GROUPS = LANES // EDGE
+NEXT_X, NEXT_Y, PREV_Y, RATE, KEEP, SCALE = 0, 9, 17, 25, 33, 57
 FIELD_ROWS = SPECIES * TILES * STRIDE
-COEFF_ROWS = KINDS * TILES * FZ
+COEFF_ROWS = 65 * FZ
 UPWARD_ROWS = TILES * STRIDE
 EDGE_ROWS = PLANES + NZC
 BESIDE_ROWS = 2 * NZC
@@ -347,7 +348,7 @@
 def ghost_table(tile):
     lane = lane_ids((BLK, LANES))
     pos = lax.broadcasted_iota(jnp.int32, (BLK, LANES), 0)
-    x = tile * (LANES // EDGE) + lane // EDGE
+    x = tile + TILES * (lane // EDGE)
     y = lane % EDGE
     along_y = y // RATIO == pos
     along_x = x // RATIO == pos
@@ -372,8 +373,9 @@
 
 def mean_table():
     shape = (2 * LANES, LANES)
-    rows = lax.broadcasted_iota(jnp.int32, shape, 0)
-    same = rows % EDGE // RATIO == lane_ids(shape) % BLK
+    rows = lax.broadcasted_iota(jnp.int32, shape, 0) % LANES
+    lane = lane_ids(shape)
+    same = (rows // EDGE == lane // EDGE) & (rows % EDGE // RATIO == lane % BLK)
     return jnp.where(same, 1.0 / RATIO**3, 0.0).astype(jnp.bfloat16)
 
 
@@ -424,39 +426,34 @@
 
 
 def advance(source, target, coeffs, upward, slot, from_rows, to_rows, ztile, ghosts):
-    lane = lane_ids((8, LANES))
-
     def value(field, tile, shift):
         start = from_rows + padded_at(field * TILES + tile, ztile) + shift
         return source[aligned(start, 8) if shift == 0 else pl.ds(start, 8), :]
 
     def get(kind, tile):
-        return coeffs[
-            aligned(slot * COEFF_ROWS + (kind * TILES + tile) * FZ + 8 * ztile, 8), :
-        ]
-
-    centers = [value(field, 0, 0) for field in range(SPECIES)]
-    down = [roll_lanes(center, -EDGE) for center in centers]
-    up = [roll_lanes(center, EDGE) for center in centers]
-    up_before = list(up)
+        return coeffs[aligned(slot * COEFF_ROWS + (kind + tile) * FZ + 8 * ztile, 8), :]
+
+    fields = range(SPECIES)
+    center = [value(field, 0, 0) for field in fields]
+    behind = [roll_lanes(value(field, TILES - 1, 0), EDGE) for field in fields]
+    beyond = [roll_lanes(center[field], -EDGE) for field in fields]
+    prev_x = get(NEXT_X, 0)
     for tile in range(TILES):
         if tile + 1 < TILES:
-            centers_after = [value(field, tile + 1, 0) for field in range(SPECIES)]
-            down_after = [roll_lanes(center, -EDGE) for center in centers_after]
-        next_x, prev_x, next_y, prev_y, rate = [get(kind, tile) for kind in range(5)]
+            ahead = [value(field, tile + 1, 0) for field in fields]
+        else:
+            ahead = beyond
+        next_x, next_y, prev_y, rate = [
+            get(kind, tile) for kind in (NEXT_X + 1, NEXT_Y, PREV_Y, RATE)
+        ]
         base = slot * UPWARD_ROWS + padded_at(tile, ztile)
         next_z = upward[aligned(base, 8), :]
         prev_z = upward[pl.ds(base - 1, 8), :]
-        forward = rate * (centers[0] * centers[1] - centers[2])
-        for field in range(SPECIES):
-            center = centers[field]
-            ahead, behind = down[field], up[field]
-            if tile + 1 < TILES:
-                ahead = jnp.where(lane < LANES - EDGE, ahead, down_after[field])
-            if tile > 0:
-                behind = jnp.where(lane >= EDGE, behind, up_before[field])
-            flux = (next_x * ahead + prev_x * behind) + (
-                next_y * roll_lanes(center, -1) + prev_y * roll_lanes(center, 1)
+        forward = rate * (center[0] * center[1] - center[2])
+        for field in fields:
+            own = center[field]
+            flux = (next_x * ahead[field] + prev_x * behind[field]) + (
+                next_y * roll_lanes(own, -1) + prev_y * roll_lanes(own, 1)
             )
             flux = flux + (next_z * value(field, tile, 1) + prev_z * value(field, tile, -1))
             share = ghosts(field, tile)
@@ -464,13 +461,39 @@
                 flux = flux + share
             if DIFFUSE[field] != 1.0:
                 flux = DIFFUSE[field] * flux
-            result = get(5 + field, tile) * center + flux
+            result = get(KEEP + field * TILES, tile) * own + flux
             result = result - forward if SIGNS[field] < 0 else result + forward
             target[aligned(to_rows + padded_at(field * TILES + tile, ztile), 8), :] = result
-        if tile + 1 < TILES:
-            up_before = up
-            centers, down = centers_after, down_after
-            up = [roll_lanes(center, EDGE) for center in centers]
+        behind, center, prev_x = center, ahead, next_x
+
+
+def regroup(tiles):
+    lane = lane_ids((8, LANES))
+    low = lane < LANES // 2
+    even = lane // EDGE % 2 == 0
+
+    def turn(one, two, three, four):
+        one, three = (
+            jnp.where(low, one, roll_lanes(three, LANES // 2)),
+            jnp.where(low, roll_lanes(one, LANES // 2), three),
+        )
+        two, four = (
+            jnp.where(low, two, roll_lanes(four, LANES // 2)),
+            jnp.where(low, roll_lanes(two, LANES // 2), four),
+        )
+        return (
+            jnp.where(even, one, roll_lanes(two, EDGE)),
+            jnp.where(even, roll_lanes(one, -EDGE), two),
+            jnp.where(even, three, roll_lanes(four, EDGE)),
+            jnp.where(even, roll_lanes(three, -EDGE), four),
+        )
+
+    return turn(*tiles[0::2]) + turn(*tiles[1::2])
+
+
+def regroup_back(tiles):
+    one = regroup([tiles[order] for order in (0, 4, 1, 5, 2, 6, 3, 7)])
+    return tuple(one[order] for order in (0, 4, 1, 5, 2, 6, 3, 7))
 
 
 def clear_pads(ref):
@@ -548,18 +571,23 @@
         for copy in loads(slot):
             copy.wait()
 
-        for tile in range(TILES):
-            cols = pl.ds(tile * LANES, LANES)
+        def regrouped(ref, index, ztile):
+            rows = pl.ds(8 * ztile, 8)
+            return regroup(
+                [ref[(*index, rows, pl.ds(tile * LANES, LANES))] for tile in range(TILES)]
+            )
+
+        for ztile in range(ZTILES):
             for field in range(SPECIES):
-                spot = aligned(slot * FIELD_ROWS + padded_at(field * TILES + tile, 0), FZ)
-                first[spot, :] = state_ref[slot, field, :, cols]
-            spot = aligned(slot * UPWARD_ROWS + padded_at(tile, 0), FZ)
-            conduct[spot, :] = kappa_ref[slot, :, cols]
+                for tile, values in enumerate(regrouped(state_ref, (slot, field), ztile)):
+                    start = slot * FIELD_ROWS + padded_at(field * TILES + tile, ztile)
+                    first[aligned(start, 8), :] = values
+            for tile, values in enumerate(regrouped(kappa_ref, (slot,), ztile)):
+                conduct[aligned(slot * UPWARD_ROWS + padded_at(tile, ztile), 8), :] = values
 
         def keep(kind, tile, ztile, values):
-            coeffs[
-                aligned(slot * COEFF_ROWS + (kind * TILES + tile) * FZ + 8 * ztile, 8), :
-            ] = values
+            row = slot * COEFF_ROWS + (kind + tile) * FZ + 8 * ztile
+            coeffs[aligned(row, 8), :] = values
 
         for ztile in range(ZTILES):
 
@@ -568,19 +596,18 @@
                 return conduct[aligned(start, 8) if shift == 0 else pl.ds(start, 8), :]
 
             center = here(0, 0)
-            turned = roll_lanes(center, -EDGE)
-            back_before = None
+            beyond = roll_lanes(center, -EDGE)
+            wrapped = face(FINE_SCALE, here(TILES - 1, 0), beyond)
+            wrapped = jnp.where(lane < LANES - EDGE, wrapped, 0.0)
+            prev_x = roll_lanes(wrapped, EDGE)
+            keep(NEXT_X, 0, ztile, prev_x)
+            rates = regrouped(rate_ref, (slot,), ztile)
             for tile in range(TILES):
-                other = turned
                 if tile + 1 < TILES:
-                    center_after = here(tile + 1, 0)
-                    turned_after = roll_lanes(center_after, -EDGE)
-                    other = jnp.where(lane < LANES - EDGE, turned, turned_after)
-                next_x = face(FINE_SCALE, center, other)
-                if tile == TILES - 1:
-                    next_x = jnp.where(lane < LANES - EDGE, next_x, 0.0)
-                back = roll_lanes(next_x, EDGE)
-                prev_x = jnp.where(lane >= EDGE, back, 0.0 if tile == 0 else back_before)
+                    ahead = here(tile + 1, 0)
+                    next_x = face(FINE_SCALE, center, ahead)
+                else:
+                    ahead, next_x = beyond, wrapped
                 next_y = jnp.where(
                     column < EDGE - 1, face(FINE_SCALE, center, roll_lanes(center, -1)), 0.0
                 )
@@ -595,18 +622,14 @@
                 scale = FINE_SCALE * center
                 total = (next_x + prev_x) + (next_y + prev_y) + (next_z + prev_z) + sides * scale
                 upward[aligned(slot * UPWARD_ROWS + padded_at(tile, ztile), 8), :] = next_z
-                keep(0, tile, ztile, next_x)
-                keep(1, tile, ztile, prev_x)
-                keep(2, tile, ztile, next_y)
-                keep(3, tile, ztile, prev_y)
-                rate = rate_ref[slot, pl.ds(8 * ztile, 8), pl.ds(tile * LANES, LANES)]
-                keep(4, tile, ztile, DT_FINE * rate)
+                keep(NEXT_X + 1, tile, ztile, next_x)
+                keep(NEXT_Y, tile, ztile, next_y)
+                keep(PREV_Y, tile, ztile, prev_y)
+                keep(RATE, tile, ztile, DT_FINE * rates[tile])
                 for field in range(SPECIES):
-                    keep(5 + field, tile, ztile, 1.0 - DIFFUSE[field] * total)
-                keep(8, tile, ztile, scale)
-                back_before = back
-                if tile + 1 < TILES:
-                    center, turned = center_after, turned_after
+                    keep(KEEP + field * TILES, tile, ztile, 1.0 - DIFFUSE[field] * total)
+                keep(SCALE, tile, ztile, scale)
+                center, prev_x = ahead, next_x
 
         for ztile in range(ZTILES):
             advance(
@@ -649,6 +672,7 @@
     share,
     drift,
     staged,
+    sums,
     sems,
     in_sems,
     avg_sems,
@@ -686,7 +710,7 @@
     old, new = complete_strips(gathered)
     gathered = jnp.concatenate([old, (new - old) * (1.0 / RATIO)], axis=0)
     quarter = AVG_ROWS // FACES
-    group_of = lane_ids((quarter, LANES)) // BLK
+    slot_of = lane_ids((quarter, LANES)) // BLK % slots
 
     def send_out(slot):
         return pltpu.make_async_copy(staged.at[slot], out_hbm.at[slot], sems.at[slot])
@@ -713,7 +737,7 @@
                 ghost_ref[:, tile * LANES : (tile + 1) * LANES],
                 preferred_element_type=jnp.float32,
             )
-            scale = coeffs[aligned(scales + (8 * TILES + tile) * FZ, FZ), :]
+            scale = coeffs[aligned(scales + (SCALE + tile) * FZ, FZ), :]
             for field in range(SPECIES):
                 row = (field * TILES + tile) * FZ
                 old = scale * ghosts[field * FZ : (field + 1) * FZ]
@@ -736,32 +760,36 @@
 
                 advance(source, target, coeffs, upward, slot, base, base, ztile, ghosts)
 
-        for tile in range(TILES):
-            for field in range(SPECIES):
-                spot = aligned(base + padded_at(field * TILES + tile, 0), FZ)
-                staged[slot, field, :, pl.ds(tile * LANES, LANES)] = first[spot, :]
+        for field in range(SPECIES):
+            for ztile in range(ZTILES):
+                values = [
+                    first[aligned(base + padded_at(field * TILES + tile, ztile), 8), :]
+                    for tile in range(TILES)
+                ]
+                for tile, native in enumerate(regroup_back(values)):
+                    staged[slot, field, pl.ds(8 * ztile, 8), pl.ds(tile * LANES, LANES)] = native
         send_out(slot).start()
 
-        sums = []
         for field in range(SPECIES):
-            for plane in range(NZC):
-                start = base + field * TILES * STRIDE + PAD + RATIO * plane
-                part = first[pl.ds(start, TILES, stride=STRIDE), :]
-                for z in range(1, RATIO):
-                    part = part + first[pl.ds(start + z, TILES, stride=STRIDE), :]
-                sums.append(part)
+            for part in range(2):
+                pieces = [
+                    first[aligned(base + padded_at(field * TILES + part * RATIO + x, 0), FZ), :]
+                    for x in range(RATIO)
+                ]
+                row = (field * 2 + part) * FZ
+                sums[row : row + FZ, :] = (pieces[0] + pieces[1]) + (pieces[2] + pieces[3])
+        parts = []
+        for index in range(SPECIES * 2):
+            pieces = [
+                sums[pl.ds(index * FZ + z, NZC, stride=RATIO), :] for z in range(RATIO)
+            ]
+            parts.append((pieces[0] + pieces[1]) + (pieces[2] + pieces[3]))
         means = jnp.dot(
-            jnp.concatenate(split_pair(jnp.concatenate(sums, axis=0)), axis=1),
+            jnp.concatenate(split_pair(jnp.concatenate(parts, axis=0)), axis=1),
             mean_ref[...],
             preferred_element_type=jnp.float32,
         )
-        chunk = avg_ref[...]
-        for part in range(FACES):
-            chunk = jnp.where(
-                group_of == part * slots + slot,
-                means[part * quarter : (part + 1) * quarter],
-                chunk,
-            )
+        chunk = jnp.where(slot_of == slot, means, avg_ref[...])
         avg_ref[...] = chunk
         return carry
 
@@ -867,7 +895,7 @@
 
 
 def place_kernel(
-    place_ref, avg_ref, new_ref, out_ref, *, cells_x, cells_y, group, slots
+    place_ref, avg_ref, new_ref, out_ref, placed_ref, *, cells_x, cells_y, group, slots
 ):
     width = slots * BLK
     quarter = AVG_ROWS // FACES
@@ -882,7 +910,12 @@
                 piece = roll_lanes(avg_ref[tile * per_tile + place], (place - index) * width)
                 merged = jnp.where(part == place, piece, merged)
             rows.append(merged)
-        columns.append(jnp.concatenate(rows, axis=0))
+        ordered = []
+        for field in range(SPECIES):
+            for x in range(BLK):
+                at = (field * 2 + x % 2) * NZC
+                ordered.append(rows[x // 2][at : at + NZC])
+        columns.append(jnp.concatenate(ordered, axis=0))
     high, low = split_pair(jnp.concatenate(columns, axis=1))
     ones = jnp.ones((16, high.shape[1]), jnp.bfloat16)
     stacked = jnp.concatenate([high, low, ones], axis=0)
@@ -896,18 +929,17 @@
             preferred_element_type=jnp.float32,
         )
         covered = placed[2 * AVG_ROWS : 2 * AVG_ROWS + 8] > 0.5
-        for plane in range(PLANES):
-            values = (
-                placed[plane * BLK : (plane + 1) * BLK]
-                + placed[AVG_ROWS + plane * BLK : AVG_ROWS + (plane + 1) * BLK]
-            )
-            row = plane * cells_x + column * BLK
-            for half in range(halves):
-                cols = slice(half * LANES, (half + 1) * LANES)
+        values = placed[:AVG_ROWS] + placed[AVG_ROWS : 2 * AVG_ROWS]
+        for half in range(halves):
+            cols = slice(half * LANES, (half + 1) * LANES)
+            start = (column * halves + half) * AVG_ROWS
+            placed_ref[start : start + AVG_ROWS, :] = values[:, cols]
+            for plane in range(PLANES):
+                field, z = divmod(plane, NZC)
+                chosen = placed_ref[pl.ds(start + field * BLK * NZC + z, BLK, stride=NZC), :]
+                row = plane * cells_x + column * BLK
                 coarse = new_ref[row : row + BLK, cols]
-                out_ref[row : row + BLK, cols] = jnp.where(
-                    covered[:, cols], values[:, cols], coarse
-                )
+                out_ref[row : row + BLK, cols] = jnp.where(covered[:, cols], chosen, coarse)
 
 
 VMEM = pl.BlockSpec(memory_space=pltpu.VMEM)
@@ -1034,6 +1066,7 @@
             pltpu.VMEM((SPECIES * TILES * FZ, LANES), jnp.float32),
             pltpu.VMEM((SPECIES * TILES * FZ, LANES), jnp.float32),
             pltpu.VMEM(fine_state.shape, jnp.float32),
+            pltpu.VMEM((SPECIES * 2 * FZ, LANES), jnp.float32),
             pltpu.SemaphoreType.DMA((slots,)),
             pltpu.SemaphoreType.DMA((3, slots)),
             pltpu.SemaphoreType.DMA((af_count,)),
@@ -1061,6 +1094,9 @@
         out_shape=f32(rows, cells_y),
         in_specs=[VMEM] * 3,
         out_specs=VMEM,
+        scratch_shapes=[
+            pltpu.VMEM((cells_x // BLK * halves * AVG_ROWS, LANES), jnp.float32),
+        ],
         compiler_params=PARAMS,
         name="place",
     )(place, arrived, whole)

time: 50.3 us -> 61.9 us (1.23)
  Pallas kernels: 23.3 us -> 34.9 us
    pallas_call x1, Pallas kernels: 6.96 us -> 15.8 us  [per_device(): pl.pallas_call(functools.partial(prepare_kernel, slots=slots), out_shape=...]
    pallas_call x1, Pallas kernels: 10.1 us -> 12.8 us  [per_device(): pl.pallas_call(functools.partial(finish_kernel, slots=slots), out_shape=[...]
  transfers between devices with their start and end apart: 6 -> 6, of which waited for: 2 -> 2; matrix products, arithmetic and copies ran while one was open for 0% -> 0% of each run, Pallas kernels for 16% -> 28%
where the time goes in v3:
time: 61.9 us; the launch traced here: 61.4 us
  Pallas kernels  34.9 us (56%)
  starting transfers between devices  23.5 us (38%)
  waiting for transfers between devices  2.27 us (4%)
  between operations  0.73 us (1%)
    pallas_call x1, Pallas kernels, per_device(): pl.pallas_call(functools.partial(prepare_kernel, slots=slots), out_shape=...  15.8 us
    all_to_all x2, starting transfers between devices, exchange(): return lax.all_to_all(chunks, 'af', split_axis=0, concat_axis=0, tiled=True)  13.9 us
    pallas_call x1, Pallas kernels, per_device(): pl.pallas_call(functools.partial(finish_kernel, slots=slots), out_shape=[...  12.8 us
    ppermute x4, starting transfers between devices, shifted(): return lax.ppermute(values, axis, pairs)  9.53 us
    pallas_call x1, Pallas kernels, per_device(): pl.pallas_call(functools.partial(strips_kernel, slots=slots, **sizes), ou...  3.89 us
    all_to_all x2, waiting for transfers between devices, exchange(): return lax.all_to_all(chunks, 'af', split_axis=0, concat_axis=0, tiled=True)  1.47 us
    pallas_call x1, Pallas kernels, per_device(): pl.pallas_call(functools.partial(place_kernel, slots=slots, **sizes), out...  1.25 us
  transfers between devices with their start and end apart: 6, of which 2 were waited for; matrix products, arithmetic and copies ran while one was open for 0% of the time, Pallas kernels for 28%

profile of v3, /device:TPU:0, one launch (start us, length us, event | category | flops | bytes accessed | tf_op | source)
XLA Modules:
  0.0 61.4 jit_solution(12100521138789125179)
XLA Ops:
  0.6 3.9 %strips.1 = (f32[384,256]{1,0:T(8,128)}, f32[8,64,128]{2,1,0:T(8,128)}, s32[16,256]{1,0:T(8,128)S(1)}, f32[32,256]{1,0:T(8,128)S(1)}, f32[32,256]{1,0:T(8,128)S(...) custom-call(s32[2,128]{1,0:T(2,128)} %bitcast.9, f32[384,256]{1,0:T(8,128)} %bitcast.5, f32[128,256]{1,0:T(8,128)} %bitcast.7, ...), custom_call_target="tpu_custom_call" | custom-call | tf_op jit(solution)/shard_map/strips/pallas_call | solution.py:986
  4.5 7.3 %all-to-all-start = ((f32[8,64,128]{2,1,0:T(8,128)}), f32[8,64,128]{2,1,0:T(8,128)S(1)}, u32[]{:S(2)}, u32[]{:S(2)}) async-start(f32[8,64,128]{2,1,0:T(8,128)} %get-tuple-element.17), calls=%async_computation | async-start | bytes 524288 | tf_op jit(solution)/shard_map/all_to_all | solution.py:969
  11.8 3.9 %collective-permute-start = (f32[32,256]{1,0:T(8,128)S(1)}, f32[32,256]{1,0:T(8,128)S(1)}, u32[]{:S(2)}, u32[]{:S(2)}) collective-permute-start(f32[32,256]{1,0:T(8,128)S(1)} %get-tuple-element.24), channel_id=1, source_target_pairs={{0,1},{1,2},{2,3},{3,4},{4,5},{5,6},{6,7},{8,9},{9,10},{10,11},{11... | collective-permute-start | bytes 98312 | tf_op jit(solution)/shard_map/ppermute | solution.py:965
  15.8 1.3 %collective-permute-start.1 = (f32[32,256]{1,0:T(8,128)S(1)}, f32[32,256]{1,0:T(8,128)S(1)}, u32[]{:S(2)}, u32[]{:S(2)}) collective-permute-start(f32[32,256]{1,0:T(8,128)S(1)} %get-tuple-element.20.after_ref), channel_id=1, source_target_pairs={{1,0},{2,1},{3,2},{4,3},{5,4},{6,5},{7,6},{9,8},{10,9},{11,10},{12... | collective-permute-start | bytes 98312 | tf_op jit(solution)/shard_map/ppermute | solution.py:965
  17.1 15.8 %prepare.1 = (f32[4608,128]{1,0:T(8,128)}, f32[8320,128]{1,0:T(8,128)}, f32[1536,128]{1,0:T(8,128)}) custom-call(f32[32,256]{1,0:T(8,128)S(1)} %get-tuple-element.20.after_ref, f32[4,3,32,1024]{3,2,1,0:T(8,128)} %state_hbm.1, f32[4,32,1024]{2,1,0:T(8,128)} %kappa_hbm.1, f32[4,32,1024]{2,1,0:T(8,128)} %rate_hbm.1), custom_call_target="tpu_custom_call" | custom-call | tf_op jit(solution)/shard_map/prepare/pallas_call | solution.py:1034
  32.9 0.0 collective-permute-done.xl_ref
  32.9 0.0 collective-permute-done.1.xr_ref
  32.9 0.0 all-to-all-done.strips_ref
  32.9 12.8 %finish.1 = (f32[4,3,32,1024]{3,2,1,0:T(8,128)}, f32[8,48,128]{2,1,0:T(8,128)}) custom-call(f32[8,64,128]{2,1,0:T(8,128)S(1)} %all-to-all-done.strips_ref, f32[4608,128]{1,0:T(8,128)} %get-tuple-element.21.fields_hbm, f32[8320,128]{1,0:T(8,128)} %get-tuple-element.22.coeffs_hbm, f32[1536,128]{1,0:T(8,128)} %get-tuple-element.23.upward_hbm, ...), custom_call_target="tpu_custom_call" | custom-call | tf_op jit(solution)/shard_map/finish/pallas_call | solution.py:1054
  45.7 6.6 %all-to-all-start.1 = ((f32[8,48,128]{2,1,0:T(8,128)}), f32[8,48,128]{2,1,0:T(8,128)S(1)}, u32[]{:S(2)}, u32[]{:S(2)}) async-start(f32[8,48,128]{2,1,0:T(8,128)} %get-tuple-element.25), calls=%async_computation.1 | async-start | bytes 393216 | tf_op jit(solution)/shard_map/all_to_all | solution.py:969
  52.4 1.3 %collective-permute-start.3 = (f32[16,128]{1,0:T(8,128)S(1)}, f32[16,128]{1,0:T(8,128)S(1)}, u32[]{:S(2)}, u32[]{:S(2)}) collective-permute-start(f32[16,128]{1,0:T(8,128)S(1)} %get-tuple-element.27.ylo_ref), channel_id=1, source_target_pairs={{8,0},{16,8},{24,16},{9,1},{17,9},{25,17},{10,2},{18,10},{26,18},{... | collective-permute-start | bytes 24584 | tf_op jit(solution)/shard_map/ppermute | solution.py:965
  53.7 3.0 %collective-permute-start.2 = (f32[16,128]{1,0:T(8,128)S(1)}, f32[16,128]{1,0:T(8,128)S(1)}, u32[]{:S(2)}, u32[]{:S(2)}) collective-permute-start(f32[16,128]{1,0:T(8,128)S(1)} %get-tuple-element.28.yhi_ref), channel_id=1, source_target_pairs={{0,8},{8,16},{16,24},{1,9},{9,17},{17,25},{2,10},{10,18},{18,26},{... | collective-permute-start | bytes 24584 | tf_op jit(solution)/shard_map/ppermute | solution.py:965
  56.7 0.0 collective-permute-done.3.yr_ref
  56.7 0.8 %collective-permute-done.2.yl_ref = f32[16,128]{1,0:T(8,128)S(1)} collective-permute-done((f32[16,128]{1,0:T(8,128)S(1)}, f32[16,128]{1,0:T(8,128)S(1)}, u32[]{:S(2)}, u32[]{:S(2)}) %collective-permute-start.2) | collective-permute-done | bytes 8224 | tf_op jit(solution)/shard_map/ppermute | solution.py:965
  57.5 1.2 %edges.1.new_ref = f32[384,256]{1,0:T(8,128)S(1)} custom-call(f32[384,256]{1,0:T(8,128)} %get-tuple-element.26.new_hbm, f32[32,256]{1,0:T(8,128)S(1)} %get-tuple-element.18.low_ref.xlo_ref, f32[32,256]{1,0:T(8,128)S(1)} %get-tuple-element.19.high_ref.xhi_ref, f32[16,128]{1,0:T(8,128)S(1)} %get-tuple-element.27.ylo_ref, ...), custom_call_target="tpu_custom_call" | custom-call | tf_op jit(solution)/shard_map/edges/pallas_call | solution.py:1082
  58.7 1.5 %all-to-all-done.1.avg_ref = f32[8,48,128]{2,1,0:T(8,128)S(1)} async-done(((f32[8,48,128]{2,1,0:T(8,128)}), f32[8,48,128]{2,1,0:T(8,128)S(1)}, u32[]{:S(2)}, u32[]{:S(2)}) %all-to-all-start.1) | async-done | bytes 196640 | tf_op jit(solution)/shard_map/all_to_all | solution.py:969
  60.1 1.3 %place.1 = f32[384,256]{1,0:T(8,128)} custom-call(s32[16,256]{1,0:T(8,128)S(1)} %get-tuple-element.16.place_ref, f32[8,48,128]{2,1,0:T(8,128)S(1)} %all-to-all-done.1.avg_ref, f32[384,256]{1,0:T(8,128)S(1)} %edges.1.new_ref), custom_call_target="tpu_custom_call" | custom-call | tf_op jit(solution)/shard_map/place/pallas_call | solution.py:1092
  (1 shorter events, 0.0 us)
Async XLA Ops:
  4.5 28.4 %all-to-all-start = ((f32[8,64,128]{2,1,0:T(8,128)}), f32[8,64,128]{2,1,0:T(8,128)S(1)}, u32[]{:S(2)}, u32[]{:S(2)}) async-start(f32[8,64,128]{2,1,0:T(8,128)} %get-tuple-element.17), calls=%async_computation | async-start | bytes 524288 | tf_op jit(solution)/shard_map/all_to_all | solution.py:969
  11.8 21.1 %collective-permute-start = (f32[32,256]{1,0:T(8,128)S(1)}, f32[32,256]{1,0:T(8,128)S(1)}, u32[]{:S(2)}, u32[]{:S(2)}) collective-permute-start(f32[32,256]{1,0:T(8,128)S(1)} %get-tuple-element.24), channel_id=1, source_target_pairs={{0,1},{1,2},{2,3},{3,4},{4,5},{5,6},{6,7},{8,9},{9,10},{10,11},{11... | collective-permute-start | bytes 98312 | tf_op jit(solution)/shard_map/ppermute | solution.py:965
  15.8 17.1 %collective-permute-start.1 = (f32[32,256]{1,0:T(8,128)S(1)}, f32[32,256]{1,0:T(8,128)S(1)}, u32[]{:S(2)}, u32[]{:S(2)}) collective-permute-start(f32[32,256]{1,0:T(8,128)S(1)} %get-tuple-element.20.after_ref), channel_id=1, source_target_pairs={{1,0},{2,1},{3,2},{4,3},{5,4},{6,5},{7,6},{9,8},{10,9},{11,10},{12... | collective-permute-start | bytes 98312 | tf_op jit(solution)/shard_map/ppermute | solution.py:965
  45.7 14.4 %all-to-all-start.1 = ((f32[8,48,128]{2,1,0:T(8,128)}), f32[8,48,128]{2,1,0:T(8,128)S(1)}, u32[]{:S(2)}, u32[]{:S(2)}) async-start(f32[8,48,128]{2,1,0:T(8,128)} %get-tuple-element.25), calls=%async_computation.1 | async-start | bytes 393216 | tf_op jit(solution)/shard_map/all_to_all | solution.py:969
  52.4 4.3 %collective-permute-start.3 = (f32[16,128]{1,0:T(8,128)S(1)}, f32[16,128]{1,0:T(8,128)S(1)}, u32[]{:S(2)}, u32[]{:S(2)}) collective-permute-start(f32[16,128]{1,0:T(8,128)S(1)} %get-tuple-element.27.ylo_ref), channel_id=1, source_target_pairs={{8,0},{16,8},{24,16},{9,1},{17,9},{25,17},{10,2},{18,10},{26,18},{... | collective-permute-start | bytes 24584 | tf_op jit(solution)/shard_map/ppermute | solution.py:965
  53.7 3.8 %collective-permute-start.2 = (f32[16,128]{1,0:T(8,128)S(1)}, f32[16,128]{1,0:T(8,128)S(1)}, u32[]{:S(2)}, u32[]{:S(2)}) collective-permute-start(f32[16,128]{1,0:T(8,128)S(1)} %get-tuple-element.28.yhi_ref), channel_id=1, source_target_pairs={{0,8},{8,16},{16,24},{1,9},{9,17},{17,25},{2,10},{10,18},{18,26},{... | collective-permute-start | bytes 24584 | tf_op jit(solution)/shard_map/ppermute | solution.py:965

commit v4 on v2

--- a/solution.py
+++ b/solution.py
@@ -15,7 +15,8 @@
 FZ = NZC * RATIO
 LANES = 128
 TILES = EDGE * EDGE // LANES
-ZTILES = FZ // 8
+DEPTH = 16
+ZTILES = FZ // DEPTH
 STRIDE = 48
 PAD = 8
 FACES = 4
@@ -79,7 +80,7 @@
     kappa_hbm,
     rate_hbm,
     new_hbm,
-    send_ref,
+    send_hbm,
     place_ref,
     xlo_ref,
     xhi_ref,
@@ -92,7 +93,9 @@
     new_ref,
     padded,
     fresh,
+    send_ref,
     sems,
+    send_sems,
     *,
     cells_x,
     cells_y,
@@ -325,6 +328,10 @@
             at += 2 * size
 
     width = slots * BLK
+    outgoing = [
+        pltpu.make_async_copy(send_ref.at[target], send_hbm.at[target], send_sems.at[target])
+        for target in range(group // slots)
+    ]
     for target in range(group // slots):
         first = target * width
         tile = first // LANES * LANES
@@ -341,6 +348,9 @@
                     part == index, roll_lanes(piece, index * width - (first - tile)), chunk
                 )
             send_ref[target, start : start + size, :] = chunk
+        outgoing[target].start()
+    for copy in outgoing:
+        copy.wait()
     keep_new.wait()
 
 
@@ -420,19 +430,19 @@
 
 
 def padded_at(block, ztile):
-    return block * STRIDE + PAD + 8 * ztile
+    return block * STRIDE + PAD + DEPTH * ztile
 
 
 def advance(source, target, coeffs, upward, slot, from_rows, to_rows, ztile, ghosts):
-    lane = lane_ids((8, LANES))
+    lane = lane_ids((DEPTH, LANES))
 
     def value(field, tile, shift):
         start = from_rows + padded_at(field * TILES + tile, ztile) + shift
-        return source[aligned(start, 8) if shift == 0 else pl.ds(start, 8), :]
+        return source[aligned(start, DEPTH) if shift == 0 else pl.ds(start, DEPTH), :]
 
     def get(kind, tile):
         return coeffs[
-            aligned(slot * COEFF_ROWS + (kind * TILES + tile) * FZ + 8 * ztile, 8), :
+            aligned(slot * COEFF_ROWS + (kind * TILES + tile) * FZ + DEPTH * ztile, DEPTH), :
         ]
 
     centers = [value(field, 0, 0) for field in range(SPECIES)]
@@ -445,8 +455,8 @@
             down_after = [roll_lanes(center, -EDGE) for center in centers_after]
         next_x, prev_x, next_y, prev_y, rate = [get(kind, tile) for kind in range(5)]
         base = slot * UPWARD_ROWS + padded_at(tile, ztile)
-        next_z = upward[aligned(base, 8), :]
-        prev_z = upward[pl.ds(base - 1, 8), :]
+        next_z = upward[aligned(base, DEPTH), :]
+        prev_z = upward[pl.ds(base - 1, DEPTH), :]
         forward = rate * (centers[0] * centers[1] - centers[2])
         for field in range(SPECIES):
             center = centers[field]
@@ -466,7 +476,7 @@
                 flux = DIFFUSE[field] * flux
             result = get(5 + field, tile) * center + flux
             result = result - forward if SIGNS[field] < 0 else result + forward
-            target[aligned(to_rows + padded_at(field * TILES + tile, ztile), 8), :] = result
+            target[aligned(to_rows + padded_at(field * TILES + tile, ztile), DEPTH), :] = result
         if tile + 1 < TILES:
             up_before = up
             centers, down = centers_after, down_after
@@ -540,7 +550,7 @@
     for ref in (fields_ref, upward, first, conduct):
         clear_pads(ref)
 
-    lane = lane_ids((8, LANES))
+    lane = lane_ids((DEPTH, LANES))
     column = lane % EDGE
     side_y = jnp.where((column == 0) | (column == EDGE - 1), 1.0, 0.0)
 
@@ -558,14 +568,14 @@
 
         def keep(kind, tile, ztile, values):
             coeffs[
-                aligned(slot * COEFF_ROWS + (kind * TILES + tile) * FZ + 8 * ztile, 8), :
+                aligned(slot * COEFF_ROWS + (kind * TILES + tile) * FZ + DEPTH * ztile, DEPTH), :
             ] = values
 
         for ztile in range(ZTILES):
 
             def here(tile, shift):
                 start = slot * UPWARD_ROWS + padded_at(tile, ztile) + shift
-                return conduct[aligned(start, 8) if shift == 0 else pl.ds(start, 8), :]
+                return conduct[aligned(start, DEPTH) if shift == 0 else pl.ds(start, DEPTH), :]
 
             center = here(0, 0)
             turned = roll_lanes(center, -EDGE)
@@ -594,12 +604,12 @@
                     sides = sides + jnp.where(lane >= LANES - EDGE, 1.0, 0.0)
                 scale = FINE_SCALE * center
                 total = (next_x + prev_x) + (next_y + prev_y) + (next_z + prev_z) + sides * scale
-                upward[aligned(slot * UPWARD_ROWS + padded_at(tile, ztile), 8), :] = next_z
+                upward[aligned(slot * UPWARD_ROWS + padded_at(tile, ztile), DEPTH), :] = next_z
                 keep(0, tile, ztile, next_x)
                 keep(1, tile, ztile, prev_x)
                 keep(2, tile, ztile, next_y)
                 keep(3, tile, ztile, prev_y)
-                rate = rate_ref[slot, pl.ds(8 * ztile, 8), pl.ds(tile * LANES, LANES)]
+                rate = rate_ref[slot, pl.ds(DEPTH * ztile, DEPTH), pl.ds(tile * LANES, LANES)]
                 keep(4, tile, ztile, DT_FINE * rate)
                 for field in range(SPECIES):
                     keep(5 + field, tile, ztile, 1.0 - DIFFUSE[field] * total)
@@ -728,7 +738,7 @@
             for ztile in range(ZTILES):
 
                 def ghosts(field, tile):
-                    spot = pl.ds((field * TILES + tile) * FZ + 8 * ztile, 8)
+                    spot = pl.ds((field * TILES + tile) * FZ + DEPTH * ztile, DEPTH)
                     value = share[spot, :]
                     if step + 1 < RATIO:
                         share[spot, :] = value + drift[spot, :]
@@ -955,13 +965,13 @@
         functools.partial(strips_kernel, slots=slots, **sizes),
         out_shape=[
             hbm32(rows, cells_y),
-            f32(af_count, CHUNK_ROWS, LANES),
+            hbm32(af_count, CHUNK_ROWS, LANES),
             jax.ShapeDtypeStruct((16, lanes), jnp.int32),
         ]
         + [f32(EDGE_ROWS, cells_y)] * 2
         + [f32(cells_x, LANES)] * 2,
         in_specs=[HBM] * 4,
-        out_specs=[HBM] + [VMEM] * 6,
+        out_specs=[HBM] * 2 + [VMEM] * 5,
         scratch_shapes=[
             pltpu.VMEM((2, boxes.shape[0]), jnp.int32),
             pltpu.VMEM((rows, cells_y), jnp.float32),
@@ -970,7 +980,9 @@
             pltpu.VMEM((rows, cells_y), jnp.float32),
             pltpu.VMEM(((SPECIES + 1) * halves * NZC * span, LANES), jnp.float32),
             pltpu.VMEM((rows * halves, LANES), jnp.float32),
+            pltpu.VMEM((af_count, CHUNK_ROWS, LANES), jnp.float32),
             pltpu.SemaphoreType.DMA((4,)),
+            pltpu.SemaphoreType.DMA((af_count,)),
         ],
         compiler_params=PARAMS,
         name="strips",

time: 50.3 us -> 51.8 us (1.030)
  Pallas kernels: 23.3 us -> 24.9 us
    pallas_call x1, Pallas kernels: 6.96 us -> 8.73 us  [per_device(): pl.pallas_call(functools.partial(prepare_kernel, slots=slots), out_shape=...]
  transfers between devices with their start and end apart: 6 -> 6, of which waited for: 2 -> 2; matrix products, arithmetic and copies ran while one was open for 0% -> 0% of each run, Pallas kernels for 16% -> 19%
where the time goes in v4:
time: 51.8 us; the launch traced here: 51.4 us
  Pallas kernels  24.9 us (48%)
  starting transfers between devices  23.4 us (45%)
  waiting for transfers between devices  2.27 us (4%)
  between operations  0.73 us (1%)
    all_to_all x2, starting transfers between devices, exchange(): return lax.all_to_all(chunks, 'af', split_axis=0, concat_axis=0, tiled=True)  13.9 us
    pallas_call x1, Pallas kernels, per_device(): pl.pallas_call(functools.partial(finish_kernel, slots=slots), out_shape=[...  10.2 us
    ppermute x4, starting transfers between devices, shifted(): return lax.ppermute(values, axis, pairs)  9.53 us
    pallas_call x1, Pallas kernels, per_device(): pl.pallas_call(functools.partial(prepare_kernel, slots=slots), out_shape=...  8.73 us
    pallas_call x1, Pallas kernels, per_device(): pl.pallas_call(functools.partial(strips_kernel, slots=slots, **sizes), ou...  3.63 us
    all_to_all x2, waiting for transfers between devices, exchange(): return lax.all_to_all(chunks, 'af', split_axis=0, concat_axis=0, tiled=True)  1.47 us
    pallas_call x1, Pallas kernels, per_device(): pl.pallas_call(functools.partial(place_kernel, slots=slots, **sizes), out...  1.21 us
    pallas_call x1, Pallas kernels, per_device(): pl.pallas_call(functools.partial(edges_kernel, cells_x=cells_x, cells_y=c...  1.17 us
  transfers between devices with their start and end apart: 6, of which 2 were waited for; matrix products, arithmetic and copies ran while one was open for 0% of the time, Pallas kernels for 19%

profile of v4, /device:TPU:0, one launch (start us, length us, event | category | flops | bytes accessed | tf_op | source)
XLA Modules:
  0.0 51.4 jit_solution(12042645386405309398)
XLA Ops:
  0.6 3.6 %strips.1 = (f32[384,256]{1,0:T(8,128)}, f32[8,64,128]{2,1,0:T(8,128)}, s32[16,256]{1,0:T(8,128)S(1)}, f32[32,256]{1,0:T(8,128)S(1)}, f32[32,256]{1,0:T(8,128)S(...) custom-call(s32[2,128]{1,0:T(2,128)} %bitcast.9, f32[384,256]{1,0:T(8,128)} %bitcast.5, f32[128,256]{1,0:T(8,128)} %bitcast.7, ...), custom_call_target="tpu_custom_call" | custom-call | tf_op jit(solution)/shard_map/strips/pallas_call | solution.py:964
  4.3 7.3 %all-to-all-start = ((f32[8,64,128]{2,1,0:T(8,128)}), f32[8,64,128]{2,1,0:T(8,128)S(1)}, u32[]{:S(2)}, u32[]{:S(2)}) async-start(f32[8,64,128]{2,1,0:T(8,128)} %get-tuple-element.17), calls=%async_computation | async-start | bytes 524288 | tf_op jit(solution)/shard_map/all_to_all | solution.py:947
  11.6 3.9 %collective-permute-start = (f32[32,256]{1,0:T(8,128)S(1)}, f32[32,256]{1,0:T(8,128)S(1)}, u32[]{:S(2)}, u32[]{:S(2)}) collective-permute-start(f32[32,256]{1,0:T(8,128)S(1)} %get-tuple-element.24), channel_id=1, source_target_pairs={{0,1},{1,2},{2,3},{3,4},{4,5},{5,6},{6,7},{8,9},{9,10},{10,11},{11... | collective-permute-start | bytes 98312 | tf_op jit(solution)/shard_map/ppermute | solution.py:943
  15.5 1.3 %collective-permute-start.1 = (f32[32,256]{1,0:T(8,128)S(1)}, f32[32,256]{1,0:T(8,128)S(1)}, u32[]{:S(2)}, u32[]{:S(2)}) collective-permute-start(f32[32,256]{1,0:T(8,128)S(1)} %get-tuple-element.20.after_ref), channel_id=1, source_target_pairs={{1,0},{2,1},{3,2},{4,3},{5,4},{6,5},{7,6},{9,8},{10,9},{11,10},{12... | collective-permute-start | bytes 98312 | tf_op jit(solution)/shard_map/ppermute | solution.py:943
  16.8 8.7 %prepare.1 = (f32[4608,128]{1,0:T(8,128)}, f32[9216,128]{1,0:T(8,128)}, f32[1536,128]{1,0:T(8,128)}) custom-call(f32[32,256]{1,0:T(8,128)S(1)} %get-tuple-element.20.after_ref, f32[4,3,32,1024]{3,2,1,0:T(8,128)} %state_hbm.1, f32[4,32,1024]{2,1,0:T(8,128)} %kappa_hbm.1, f32[4,32,1024]{2,1,0:T(8,128)} %rate_hbm.1), custom_call_target="tpu_custom_call" | custom-call | tf_op jit(solution)/shard_map/prepare/pallas_call | solution.py:1014
  25.5 0.0 collective-permute-done.xl_ref
  25.5 0.0 collective-permute-done.1.xr_ref
  25.6 0.0 all-to-all-done.strips_ref
  25.6 10.2 %finish.1 = (f32[4,3,32,1024]{3,2,1,0:T(8,128)}, f32[8,48,128]{2,1,0:T(8,128)}) custom-call(f32[8,64,128]{2,1,0:T(8,128)S(1)} %all-to-all-done.strips_ref, f32[4608,128]{1,0:T(8,128)} %get-tuple-element.21.fields_hbm, f32[9216,128]{1,0:T(8,128)} %get-tuple-element.22.coeffs_hbm, f32[1536,128]{1,0:T(8,128)} %get-tuple-element.23.upward_hbm, ...), custom_call_target="tpu_custom_call" | custom-call | tf_op jit(solution)/shard_map/finish/pallas_call | solution.py:1034
  35.7 6.6 %all-to-all-start.1 = ((f32[8,48,128]{2,1,0:T(8,128)}), f32[8,48,128]{2,1,0:T(8,128)S(1)}, u32[]{:S(2)}, u32[]{:S(2)}) async-start(f32[8,48,128]{2,1,0:T(8,128)} %get-tuple-element.25), calls=%async_computation.1 | async-start | bytes 393216 | tf_op jit(solution)/shard_map/all_to_all | solution.py:947
  42.4 1.3 %collective-permute-start.3 = (f32[16,128]{1,0:T(8,128)S(1)}, f32[16,128]{1,0:T(8,128)S(1)}, u32[]{:S(2)}, u32[]{:S(2)}) collective-permute-start(f32[16,128]{1,0:T(8,128)S(1)} %get-tuple-element.27.ylo_ref), channel_id=1, source_target_pairs={{8,0},{16,8},{24,16},{9,1},{17,9},{25,17},{10,2},{18,10},{26,18},{... | collective-permute-start | bytes 24584 | tf_op jit(solution)/shard_map/ppermute | solution.py:943
  43.7 3.0 %collective-permute-start.2 = (f32[16,128]{1,0:T(8,128)S(1)}, f32[16,128]{1,0:T(8,128)S(1)}, u32[]{:S(2)}, u32[]{:S(2)}) collective-permute-start(f32[16,128]{1,0:T(8,128)S(1)} %get-tuple-element.28.yhi_ref), channel_id=1, source_target_pairs={{0,8},{8,16},{16,24},{1,9},{9,17},{17,25},{2,10},{10,18},{18,26},{... | collective-permute-start | bytes 24584 | tf_op jit(solution)/shard_map/ppermute | solution.py:943
  46.7 0.0 collective-permute-done.3.yr_ref
  46.7 0.8 %collective-permute-done.2.yl_ref = f32[16,128]{1,0:T(8,128)S(1)} collective-permute-done((f32[16,128]{1,0:T(8,128)S(1)}, f32[16,128]{1,0:T(8,128)S(1)}, u32[]{:S(2)}, u32[]{:S(2)}) %collective-permute-start.2) | collective-permute-done | bytes 8224 | tf_op jit(solution)/shard_map/ppermute | solution.py:943
  47.5 1.2 %edges.1.new_ref = f32[384,256]{1,0:T(8,128)S(1)} custom-call(f32[384,256]{1,0:T(8,128)} %get-tuple-element.26.new_hbm, f32[32,256]{1,0:T(8,128)S(1)} %get-tuple-element.18.low_ref.xlo_ref, f32[32,256]{1,0:T(8,128)S(1)} %get-tuple-element.19.high_ref.xhi_ref, f32[16,128]{1,0:T(8,128)S(1)} %get-tuple-element.27.ylo_ref, ...), custom_call_target="tpu_custom_call" | custom-call | tf_op jit(solution)/shard_map/edges/pallas_call | solution.py:1061
  48.7 1.5 %all-to-all-done.1.avg_ref = f32[8,48,128]{2,1,0:T(8,128)S(1)} async-done(((f32[8,48,128]{2,1,0:T(8,128)}), f32[8,48,128]{2,1,0:T(8,128)S(1)}, u32[]{:S(2)}, u32[]{:S(2)}) %all-to-all-start.1) | async-done | bytes 196640 | tf_op jit(solution)/shard_map/all_to_all | solution.py:947
  50.1 1.2 %place.1 = f32[384,256]{1,0:T(8,128)} custom-call(s32[16,256]{1,0:T(8,128)S(1)} %get-tuple-element.16.place_ref, f32[8,48,128]{2,1,0:T(8,128)S(1)} %all-to-all-done.1.avg_ref, f32[384,256]{1,0:T(8,128)S(1)} %edges.1.new_ref), custom_call_target="tpu_custom_call" | custom-call | tf_op jit(solution)/shard_map/place/pallas_call | solution.py:1071
  (1 shorter events, 0.0 us)
Async XLA Ops:
  4.3 21.3 %all-to-all-start = ((f32[8,64,128]{2,1,0:T(8,128)}), f32[8,64,128]{2,1,0:T(8,128)S(1)}, u32[]{:S(2)}, u32[]{:S(2)}) async-start(f32[8,64,128]{2,1,0:T(8,128)} %get-tuple-element.17), calls=%async_computation | async-start | bytes 524288 | tf_op jit(solution)/shard_map/all_to_all | solution.py:947
  11.6 14.0 %collective-permute-start = (f32[32,256]{1,0:T(8,128)S(1)}, f32[32,256]{1,0:T(8,128)S(1)}, u32[]{:S(2)}, u32[]{:S(2)}) collective-permute-start(f32[32,256]{1,0:T(8,128)S(1)} %get-tuple-element.24), channel_id=1, source_target_pairs={{0,1},{1,2},{2,3},{3,4},{4,5},{5,6},{6,7},{8,9},{9,10},{10,11},{11... | collective-permute-start | bytes 98312 | tf_op jit(solution)/shard_map/ppermute | solution.py:943
  15.5 10.1 %collective-permute-start.1 = (f32[32,256]{1,0:T(8,128)S(1)}, f32[32,256]{1,0:T(8,128)S(1)}, u32[]{:S(2)}, u32[]{:S(2)}) collective-permute-start(f32[32,256]{1,0:T(8,128)S(1)} %get-tuple-element.20.after_ref), channel_id=1, source_target_pairs={{1,0},{2,1},{3,2},{4,3},{5,4},{6,5},{7,6},{9,8},{10,9},{11,10},{12... | collective-permute-start | bytes 98312 | tf_op jit(solution)/shard_map/ppermute | solution.py:943
  35.7 14.4 %all-to-all-start.1 = ((f32[8,48,128]{2,1,0:T(8,128)}), f32[8,48,128]{2,1,0:T(8,128)S(1)}, u32[]{:S(2)}, u32[]{:S(2)}) async-start(f32[8,48,128]{2,1,0:T(8,128)} %get-tuple-element.25), calls=%async_computation.1 | async-start | bytes 393216 | tf_op jit(solution)/shard_map/all_to_all | solution.py:947
  42.4 4.3 %collective-permute-start.3 = (f32[16,128]{1,0:T(8,128)S(1)}, f32[16,128]{1,0:T(8,128)S(1)}, u32[]{:S(2)}, u32[]{:S(2)}) collective-permute-start(f32[16,128]{1,0:T(8,128)S(1)} %get-tuple-element.27.ylo_ref), channel_id=1, source_target_pairs={{8,0},{16,8},{24,16},{9,1},{17,9},{25,17},{10,2},{18,10},{26,18},{... | collective-permute-start | bytes 24584 | tf_op jit(solution)/shard_map/ppermute | solution.py:943
  43.7 3.8 %collective-permute-start.2 = (f32[16,128]{1,0:T(8,128)S(1)}, f32[16,128]{1,0:T(8,128)S(1)}, u32[]{:S(2)}, u32[]{:S(2)}) collective-permute-start(f32[16,128]{1,0:T(8,128)S(1)} %get-tuple-element.28.yhi_ref), channel_id=1, source_target_pairs={{0,8},{8,16},{16,24},{1,9},{9,17},{17,25},{2,10},{10,18},{18,26},{... | collective-permute-start | bytes 24584 | tf_op jit(solution)/shard_map/ppermute | solution.py:943

commit v5 on v4

--- a/solution.py
+++ b/solution.py
@@ -15,7 +15,7 @@
 FZ = NZC * RATIO
 LANES = 128
 TILES = EDGE * EDGE // LANES
-DEPTH = 16
+DEPTH = 8
 ZTILES = FZ // DEPTH
 STRIDE = 48
 PAD = 8
@@ -23,7 +23,7 @@
 PLANES = SPECIES * NZC
 STRIP_ROWS = 2 * PLANES
 AVG_ROWS = PLANES * BLK
-KINDS = 9
+KINDS = 8
 FIELD_ROWS = SPECIES * TILES * STRIDE
 COEFF_ROWS = KINDS * TILES * FZ
 UPWARD_ROWS = TILES * STRIDE
@@ -453,7 +453,8 @@
         if tile + 1 < TILES:
             centers_after = [value(field, tile + 1, 0) for field in range(SPECIES)]
             down_after = [roll_lanes(center, -EDGE) for center in centers_after]
-        next_x, prev_x, next_y, prev_y, rate = [get(kind, tile) for kind in range(5)]
+        next_x, prev_x, next_y, rate = [get(kind, tile) for kind in range(4)]
+        prev_y = roll_lanes(next_y, 1)
         base = slot * UPWARD_ROWS + padded_at(tile, ztile)
         next_z = upward[aligned(base, DEPTH), :]
         prev_z = upward[pl.ds(base - 1, DEPTH), :]
@@ -474,7 +475,7 @@
                 flux = flux + share
             if DIFFUSE[field] != 1.0:
                 flux = DIFFUSE[field] * flux
-            result = get(5 + field, tile) * center + flux
+            result = get(4 + field, tile) * center + flux
             result = result - forward if SIGNS[field] < 0 else result + forward
             target[aligned(to_rows + padded_at(field * TILES + tile, ztile), DEPTH), :] = result
         if tile + 1 < TILES:
@@ -596,7 +597,9 @@
                 )
                 prev_y = roll_lanes(next_y, 1)
                 next_z = face(FINE_SCALE, center, here(tile, 1))
-                prev_z = face(FINE_SCALE, center, here(tile, -1))
+                spot = slot * UPWARD_ROWS + padded_at(tile, ztile)
+                upward[aligned(spot, DEPTH), :] = next_z
+                prev_z = upward[pl.ds(spot - 1, DEPTH), :]
                 sides = side_y
                 if tile == 0:
                     sides = sides + jnp.where(lane < EDGE, 1.0, 0.0)
@@ -604,16 +607,14 @@
                     sides = sides + jnp.where(lane >= LANES - EDGE, 1.0, 0.0)
                 scale = FINE_SCALE * center
                 total = (next_x + prev_x) + (next_y + prev_y) + (next_z + prev_z) + sides * scale
-                upward[aligned(slot * UPWARD_ROWS + padded_at(tile, ztile), DEPTH), :] = next_z
                 keep(0, tile, ztile, next_x)
                 keep(1, tile, ztile, prev_x)
                 keep(2, tile, ztile, next_y)
-                keep(3, tile, ztile, prev_y)
                 rate = rate_ref[slot, pl.ds(DEPTH * ztile, DEPTH), pl.ds(tile * LANES, LANES)]
-                keep(4, tile, ztile, DT_FINE * rate)
+                keep(3, tile, ztile, DT_FINE * rate)
                 for field in range(SPECIES):
-                    keep(5 + field, tile, ztile, 1.0 - DIFFUSE[field] * total)
-                keep(8, tile, ztile, scale)
+                    keep(4 + field, tile, ztile, 1.0 - DIFFUSE[field] * total)
+                keep(7, tile, ztile, scale)
                 back_before = back
                 if tile + 1 < TILES:
                     center, turned = center_after, turned_after
@@ -657,7 +658,6 @@
     avg_ref,
     first,
     share,
-    drift,
     staged,
     sems,
     in_sems,
@@ -723,13 +723,15 @@
                 ghost_ref[:, tile * LANES : (tile + 1) * LANES],
                 preferred_element_type=jnp.float32,
             )
-            scale = coeffs[aligned(scales + (8 * TILES + tile) * FZ, FZ), :]
+            scale = coeffs[aligned(scales + (7 * TILES + tile) * FZ, FZ), :]
             for field in range(SPECIES):
                 row = (field * TILES + tile) * FZ
                 old = scale * ghosts[field * FZ : (field + 1) * FZ]
-                step = scale * ghosts[(SPECIES + field) * FZ : (SPECIES + field + 1) * FZ]
-                drift[row : row + FZ, :] = step
-                share[row : row + FZ, :] = old + step
+                drift = scale * ghosts[(SPECIES + field) * FZ : (SPECIES + field + 1) * FZ]
+                later = old
+                for step in range(1, RATIO):
+                    later = later + drift
+                    share[step - 1, row : row + FZ, :] = later
                 spot = aligned(base + padded_at(field * TILES + tile, 0), FZ)
                 fields_ref[spot, :] = fields_ref[spot, :] + DIFFUSE[field] * old
 
@@ -739,10 +741,7 @@
 
                 def ghosts(field, tile):
                     spot = pl.ds((field * TILES + tile) * FZ + DEPTH * ztile, DEPTH)
-                    value = share[spot, :]
-                    if step + 1 < RATIO:
-                        share[spot, :] = value + drift[spot, :]
-                    return value
+                    return share[step - 1, spot, :]
 
                 advance(source, target, coeffs, upward, slot, base, base, ztile, ghosts)
 
@@ -1043,8 +1042,7 @@
             pltpu.VMEM((2 * LANES, LANES), jnp.bfloat16),
             pltpu.VMEM(chunk, jnp.float32),
             pltpu.VMEM((slots * FIELD_ROWS, LANES), jnp.float32),
-            pltpu.VMEM((SPECIES * TILES * FZ, LANES), jnp.float32),
-            pltpu.VMEM((SPECIES * TILES * FZ, LANES), jnp.float32),
+            pltpu.VMEM((RATIO - 1, SPECIES * TILES * FZ, LANES), jnp.float32),
             pltpu.VMEM(fine_state.shape, jnp.float32),
             pltpu.SemaphoreType.DMA((slots,)),
             pltpu.SemaphoreType.DMA((3, slots)),

time: 51.8 us -> 50.3 us (0.971)
  Pallas kernels: 24.9 us -> 23.4 us
    pallas_call x1, Pallas kernels: 8.73 us -> 7.07 us  [per_device(): pl.pallas_call(functools.partial(prepare_kernel, slots=slots), out_shape=...]
  transfers between devices with their start and end apart: 6 -> 6, of which waited for: 2 -> 2; matrix products, arithmetic and copies ran while one was open for 0% -> 0% of each run, Pallas kernels for 19% -> 17%
where the time goes in v5:
time: 50.3 us; the launch traced here: 49.8 us
  Pallas kernels  23.4 us (47%)
  starting transfers between devices  23.4 us (47%)
  waiting for transfers between devices  2.27 us (5%)
  between operations  0.73 us (1%)
    all_to_all x2, starting transfers between devices, exchange(): return lax.all_to_all(chunks, 'af', split_axis=0, concat_axis=0, tiled=True)  13.9 us
    pallas_call x1, Pallas kernels, per_device(): pl.pallas_call(functools.partial(finish_kernel, slots=slots), out_shape=[...  10.3 us
    ppermute x4, starting transfers between devices, shifted(): return lax.ppermute(values, axis, pairs)  9.53 us
    pallas_call x1, Pallas kernels, per_device(): pl.pallas_call(functools.partial(prepare_kernel, slots=slots), out_shape=...  7.07 us
    pallas_call x1, Pallas kernels, per_device(): pl.pallas_call(functools.partial(strips_kernel, slots=slots, **sizes), ou...  3.63 us
    all_to_all x2, waiting for transfers between devices, exchange(): return lax.all_to_all(chunks, 'af', split_axis=0, concat_axis=0, tiled=True)  1.47 us
    pallas_call x1, Pallas kernels, per_device(): pl.pallas_call(functools.partial(place_kernel, slots=slots, **sizes), out...  1.21 us
    pallas_call x1, Pallas kernels, per_device(): pl.pallas_call(functools.partial(edges_kernel, cells_x=cells_x, cells_y=c...  1.17 us
  transfers between devices with their start and end apart: 6, of which 2 were waited for; matrix products, arithmetic and copies ran while one was open for 0% of the time, Pallas kernels for 17%

profile of v5, /device:TPU:0, one launch (start us, length us, event | category | flops | bytes accessed | tf_op | source)
XLA Modules:
  0.0 49.8 jit_solution(17380303465844318683)
XLA Ops:
  0.6 3.6 %strips.1 = (f32[384,256]{1,0:T(8,128)}, f32[8,64,128]{2,1,0:T(8,128)}, s32[16,256]{1,0:T(8,128)S(1)}, f32[32,256]{1,0:T(8,128)S(1)}, f32[32,256]{1,0:T(8,128)S(...) custom-call(s32[2,128]{1,0:T(2,128)} %bitcast.9, f32[384,256]{1,0:T(8,128)} %bitcast.5, f32[128,256]{1,0:T(8,128)} %bitcast.7, ...), custom_call_target="tpu_custom_call" | custom-call | tf_op jit(solution)/shard_map/strips/pallas_call | solution.py:963
  4.3 7.3 %all-to-all-start = ((f32[8,64,128]{2,1,0:T(8,128)}), f32[8,64,128]{2,1,0:T(8,128)S(1)}, u32[]{:S(2)}, u32[]{:S(2)}) async-start(f32[8,64,128]{2,1,0:T(8,128)} %get-tuple-element.17), calls=%async_computation | async-start | bytes 524288 | tf_op jit(solution)/shard_map/all_to_all | solution.py:946
  11.6 3.9 %collective-permute-start = (f32[32,256]{1,0:T(8,128)S(1)}, f32[32,256]{1,0:T(8,128)S(1)}, u32[]{:S(2)}, u32[]{:S(2)}) collective-permute-start(f32[32,256]{1,0:T(8,128)S(1)} %get-tuple-element.24), channel_id=1, source_target_pairs={{0,1},{1,2},{2,3},{3,4},{4,5},{5,6},{6,7},{8,9},{9,10},{10,11},{11... | collective-permute-start | bytes 98312 | tf_op jit(solution)/shard_map/ppermute | solution.py:942
  15.5 1.3 %collective-permute-start.1 = (f32[32,256]{1,0:T(8,128)S(1)}, f32[32,256]{1,0:T(8,128)S(1)}, u32[]{:S(2)}, u32[]{:S(2)}) collective-permute-start(f32[32,256]{1,0:T(8,128)S(1)} %get-tuple-element.20.after_ref), channel_id=1, source_target_pairs={{1,0},{2,1},{3,2},{4,3},{5,4},{6,5},{7,6},{9,8},{10,9},{11,10},{12... | collective-permute-start | bytes 98312 | tf_op jit(solution)/shard_map/ppermute | solution.py:942
  16.8 7.1 %prepare.1 = (f32[4608,128]{1,0:T(8,128)}, f32[8192,128]{1,0:T(8,128)}, f32[1536,128]{1,0:T(8,128)}) custom-call(f32[32,256]{1,0:T(8,128)S(1)} %get-tuple-element.20.after_ref, f32[4,3,32,1024]{3,2,1,0:T(8,128)} %state_hbm.1, f32[4,32,1024]{2,1,0:T(8,128)} %kappa_hbm.1, f32[4,32,1024]{2,1,0:T(8,128)} %rate_hbm.1), custom_call_target="tpu_custom_call" | custom-call | tf_op jit(solution)/shard_map/prepare/pallas_call | solution.py:1013
  23.9 0.0 collective-permute-done.xl_ref
  23.9 0.0 collective-permute-done.1.xr_ref
  23.9 0.0 all-to-all-done.strips_ref
  23.9 10.3 %finish.1 = (f32[4,3,32,1024]{3,2,1,0:T(8,128)}, f32[8,48,128]{2,1,0:T(8,128)}) custom-call(f32[8,64,128]{2,1,0:T(8,128)S(1)} %all-to-all-done.strips_ref, f32[4608,128]{1,0:T(8,128)} %get-tuple-element.21.fields_hbm, f32[8192,128]{1,0:T(8,128)} %get-tuple-element.22.coeffs_hbm, f32[1536,128]{1,0:T(8,128)} %get-tuple-element.23.upward_hbm, ...), custom_call_target="tpu_custom_call" | custom-call | tf_op jit(solution)/shard_map/finish/pallas_call | solution.py:1033
  34.2 6.6 %all-to-all-start.1 = ((f32[8,48,128]{2,1,0:T(8,128)}), f32[8,48,128]{2,1,0:T(8,128)S(1)}, u32[]{:S(2)}, u32[]{:S(2)}) async-start(f32[8,48,128]{2,1,0:T(8,128)} %get-tuple-element.25), calls=%async_computation.1 | async-start | bytes 393216 | tf_op jit(solution)/shard_map/all_to_all | solution.py:946
  40.8 1.3 %collective-permute-start.3 = (f32[16,128]{1,0:T(8,128)S(1)}, f32[16,128]{1,0:T(8,128)S(1)}, u32[]{:S(2)}, u32[]{:S(2)}) collective-permute-start(f32[16,128]{1,0:T(8,128)S(1)} %get-tuple-element.27.ylo_ref), channel_id=1, source_target_pairs={{8,0},{16,8},{24,16},{9,1},{17,9},{25,17},{10,2},{18,10},{26,18},{... | collective-permute-start | bytes 24584 | tf_op jit(solution)/shard_map/ppermute | solution.py:942
  42.1 3.0 %collective-permute-start.2 = (f32[16,128]{1,0:T(8,128)S(1)}, f32[16,128]{1,0:T(8,128)S(1)}, u32[]{:S(2)}, u32[]{:S(2)}) collective-permute-start(f32[16,128]{1,0:T(8,128)S(1)} %get-tuple-element.28.yhi_ref), channel_id=1, source_target_pairs={{0,8},{8,16},{16,24},{1,9},{9,17},{17,25},{2,10},{10,18},{18,26},{... | collective-permute-start | bytes 24584 | tf_op jit(solution)/shard_map/ppermute | solution.py:942
  45.2 0.0 collective-permute-done.3.yr_ref
  45.2 0.8 %collective-permute-done.2.yl_ref = f32[16,128]{1,0:T(8,128)S(1)} collective-permute-done((f32[16,128]{1,0:T(8,128)S(1)}, f32[16,128]{1,0:T(8,128)S(1)}, u32[]{:S(2)}, u32[]{:S(2)}) %collective-permute-start.2) | collective-permute-done | bytes 8224 | tf_op jit(solution)/shard_map/ppermute | solution.py:942
  46.0 1.2 %edges.1.new_ref = f32[384,256]{1,0:T(8,128)S(1)} custom-call(f32[384,256]{1,0:T(8,128)} %get-tuple-element.26.new_hbm, f32[32,256]{1,0:T(8,128)S(1)} %get-tuple-element.18.low_ref.xlo_ref, f32[32,256]{1,0:T(8,128)S(1)} %get-tuple-element.19.high_ref.xhi_ref, f32[16,128]{1,0:T(8,128)S(1)} %get-tuple-element.27.ylo_ref, ...), custom_call_target="tpu_custom_call" | custom-call | tf_op jit(solution)/shard_map/edges/pallas_call | solution.py:1059
  47.1 1.5 %all-to-all-done.1.avg_ref = f32[8,48,128]{2,1,0:T(8,128)S(1)} async-done(((f32[8,48,128]{2,1,0:T(8,128)}), f32[8,48,128]{2,1,0:T(8,128)S(1)}, u32[]{:S(2)}, u32[]{:S(2)}) %all-to-all-start.1) | async-done | bytes 196640 | tf_op jit(solution)/shard_map/all_to_all | solution.py:946
  48.6 1.2 %place.1 = f32[384,256]{1,0:T(8,128)} custom-call(s32[16,256]{1,0:T(8,128)S(1)} %get-tuple-element.16.place_ref, f32[8,48,128]{2,1,0:T(8,128)S(1)} %all-to-all-done.1.avg_ref, f32[384,256]{1,0:T(8,128)S(1)} %edges.1.new_ref), custom_call_target="tpu_custom_call" | custom-call | tf_op jit(solution)/shard_map/place/pallas_call | solution.py:1069
  (1 shorter events, 0.0 us)
Async XLA Ops:
  4.3 19.6 %all-to-all-start = ((f32[8,64,128]{2,1,0:T(8,128)}), f32[8,64,128]{2,1,0:T(8,128)S(1)}, u32[]{:S(2)}, u32[]{:S(2)}) async-start(f32[8,64,128]{2,1,0:T(8,128)} %get-tuple-element.17), calls=%async_computation | async-start | bytes 524288 | tf_op jit(solution)/shard_map/all_to_all | solution.py:946
  11.6 12.3 %collective-permute-start = (f32[32,256]{1,0:T(8,128)S(1)}, f32[32,256]{1,0:T(8,128)S(1)}, u32[]{:S(2)}, u32[]{:S(2)}) collective-permute-start(f32[32,256]{1,0:T(8,128)S(1)} %get-tuple-element.24), channel_id=1, source_target_pairs={{0,1},{1,2},{2,3},{3,4},{4,5},{5,6},{6,7},{8,9},{9,10},{10,11},{11... | collective-permute-start | bytes 98312 | tf_op jit(solution)/shard_map/ppermute | solution.py:942
  15.5 8.4 %collective-permute-start.1 = (f32[32,256]{1,0:T(8,128)S(1)}, f32[32,256]{1,0:T(8,128)S(1)}, u32[]{:S(2)}, u32[]{:S(2)}) collective-permute-start(f32[32,256]{1,0:T(8,128)S(1)} %get-tuple-element.20.after_ref), channel_id=1, source_target_pairs={{1,0},{2,1},{3,2},{4,3},{5,4},{6,5},{7,6},{9,8},{10,9},{11,10},{12... | collective-permute-start | bytes 98312 | tf_op jit(solution)/shard_map/ppermute | solution.py:942
  34.2 14.4 %all-to-all-start.1 = ((f32[8,48,128]{2,1,0:T(8,128)}), f32[8,48,128]{2,1,0:T(8,128)S(1)}, u32[]{:S(2)}, u32[]{:S(2)}) async-start(f32[8,48,128]{2,1,0:T(8,128)} %get-tuple-element.25), calls=%async_computation.1 | async-start | bytes 393216 | tf_op jit(solution)/shard_map/all_to_all | solution.py:946
  40.8 4.3 %collective-permute-start.3 = (f32[16,128]{1,0:T(8,128)S(1)}, f32[16,128]{1,0:T(8,128)S(1)}, u32[]{:S(2)}, u32[]{:S(2)}) collective-permute-start(f32[16,128]{1,0:T(8,128)S(1)} %get-tuple-element.27.ylo_ref), channel_id=1, source_target_pairs={{8,0},{16,8},{24,16},{9,1},{17,9},{25,17},{10,2},{18,10},{26,18},{... | collective-permute-start | bytes 24584 | tf_op jit(solution)/shard_map/ppermute | solution.py:942
  42.1 3.8 %collective-permute-start.2 = (f32[16,128]{1,0:T(8,128)S(1)}, f32[16,128]{1,0:T(8,128)S(1)}, u32[]{:S(2)}, u32[]{:S(2)}) collective-permute-start(f32[16,128]{1,0:T(8,128)S(1)} %get-tuple-element.28.yhi_ref), channel_id=1, source_target_pairs={{0,8},{8,16},{16,24},{1,9},{9,17},{17,25},{2,10},{10,18},{18,26},{... | collective-permute-start | bytes 24584 | tf_op jit(solution)/shard_map/ppermute | solution.py:942

commit v6 on v5

--- a/solution.py
+++ b/solution.py
@@ -17,16 +17,16 @@
 TILES = EDGE * EDGE // LANES
 DEPTH = 8
 ZTILES = FZ // DEPTH
-STRIDE = 48
+STRIDE = 40
 PAD = 8
 FACES = 4
 PLANES = SPECIES * NZC
 STRIP_ROWS = 2 * PLANES
 AVG_ROWS = PLANES * BLK
 KINDS = 8
-FIELD_ROWS = SPECIES * TILES * STRIDE
+FIELD_ROWS = SPECIES * TILES * STRIDE + PAD
 COEFF_ROWS = KINDS * TILES * FZ
-UPWARD_ROWS = TILES * STRIDE
+UPWARD_ROWS = TILES * STRIDE + PAD
 EDGE_ROWS = PLANES + NZC
 BESIDE_ROWS = 2 * NZC
 CHUNK_ROWS = STRIP_ROWS + BESIDE_ROWS
@@ -484,15 +484,11 @@
             up = [roll_lanes(center, EDGE) for center in centers]
 
 
-def clear_pads(ref):
+def clear_pads(ref, size):
     edge = jnp.zeros((PAD, LANES), jnp.float32)
-
-    def body(block, carry):
-        ref[aligned(block * STRIDE, PAD), :] = edge
-        ref[aligned(block * STRIDE + PAD + FZ, PAD), :] = edge
-        return carry
-
-    lax.fori_loop(0, ref.shape[0] // STRIDE, body, 0)
+    for start in range(0, ref.shape[0], size):
+        for row in range(start, start + size, STRIDE):
+            ref[row : row + PAD, :] = edge
 
 
 def hand_on_kernel(low_ref, high_ref, low_out, high_out):
@@ -548,8 +544,13 @@
             )
         ]
 
-    for ref in (fields_ref, upward, first, conduct):
-        clear_pads(ref)
+    for ref, size in (
+        (conduct, UPWARD_ROWS),
+        (upward, UPWARD_ROWS),
+        (first, FIELD_ROWS),
+        (fields_ref, FIELD_ROWS),
+    ):
+        clear_pads(ref, size)
 
     lane = lane_ids((DEPTH, LANES))
     column = lane % EDGE
@@ -656,6 +657,7 @@
     plane_ref,
     mean_ref,
     avg_ref,
+    ghosts_ref,
     first,
     share,
     staged,
@@ -684,7 +686,7 @@
         ]
 
     start_all(loads(0))
-    clear_pads(first)
+    clear_pads(first, FIELD_ROWS)
     for tile in range(TILES):
         ghost_ref[:, tile * LANES : (tile + 1) * LANES] = ghost_table(tile)
     plane_ref[...] = plane_table()
@@ -701,6 +703,22 @@
     def send_out(slot):
         return pltpu.make_async_copy(staged.at[slot], out_hbm.at[slot], sems.at[slot])
 
+    stretched = [
+        jnp.dot(
+            plane_ref[...],
+            jnp.concatenate(split_pair(roll_lanes(gathered, -slot * BLK)), axis=1),
+            preferred_element_type=jnp.float32,
+        ).astype(jnp.bfloat16)
+        for slot in range(slots)
+    ]
+    ghost_rows = 2 * SPECIES * FZ
+    for pair in range(TILES // 2):
+        cols = slice(2 * pair * LANES, 2 * (pair + 1) * LANES)
+        for slot in range(slots):
+            ghosts_ref[slot * ghost_rows : (slot + 1) * ghost_rows, cols] = jnp.dot(
+                stretched[slot], ghost_ref[:, cols], preferred_element_type=jnp.float32
+            )
+
     def one_patch(slot, carry):
         for copy in loads(slot):
             copy.wait()
@@ -709,25 +727,16 @@
         def _():
             start_all(loads(slot + 1))
 
-        turned = pltpu.roll(gathered, (LANES - slot * BLK) % LANES, 1)
-        stretched = jnp.dot(
-            plane_ref[...],
-            jnp.concatenate(split_pair(turned), axis=1),
-            preferred_element_type=jnp.float32,
-        ).astype(jnp.bfloat16)
         base = slot * FIELD_ROWS
         scales = slot * COEFF_ROWS
         for tile in range(TILES):
-            ghosts = jnp.dot(
-                stretched,
-                ghost_ref[:, tile * LANES : (tile + 1) * LANES],
-                preferred_element_type=jnp.float32,
-            )
+            cols = pl.ds(tile * LANES, LANES)
             scale = coeffs[aligned(scales + (7 * TILES + tile) * FZ, FZ), :]
             for field in range(SPECIES):
                 row = (field * TILES + tile) * FZ
-                old = scale * ghosts[field * FZ : (field + 1) * FZ]
-                drift = scale * ghosts[(SPECIES + field) * FZ : (SPECIES + field + 1) * FZ]
+                ghost = slot * ghost_rows + field * FZ
+                old = scale * ghosts_ref[aligned(ghost, FZ), cols]
+                drift = scale * ghosts_ref[aligned(ghost + SPECIES * FZ, FZ), cols]
                 later = old
                 for step in range(1, RATIO):
                     later = later + drift
@@ -751,31 +760,27 @@
                 staged[slot, field, :, pl.ds(tile * LANES, LANES)] = first[spot, :]
         send_out(slot).start()
 
-        sums = []
+        return carry
+
+    lax.fori_loop(0, slots, one_patch, 0)
+    sums = []
+    for slot in range(slots):
         for field in range(SPECIES):
             for plane in range(NZC):
-                start = base + field * TILES * STRIDE + PAD + RATIO * plane
-                part = first[pl.ds(start, TILES, stride=STRIDE), :]
-                for z in range(1, RATIO):
-                    part = part + first[pl.ds(start + z, TILES, stride=STRIDE), :]
-                sums.append(part)
-        means = jnp.dot(
-            jnp.concatenate(split_pair(jnp.concatenate(sums, axis=0)), axis=1),
-            mean_ref[...],
-            preferred_element_type=jnp.float32,
-        )
-        chunk = avg_ref[...]
+                start = slot * FIELD_ROWS + field * TILES * STRIDE + PAD + RATIO * plane
+                part = [first[pl.ds(start + z, TILES, stride=STRIDE), :] for z in range(RATIO)]
+                sums.append((part[0] + part[1]) + (part[2] + part[3]))
+    means = jnp.dot(
+        jnp.concatenate(split_pair(jnp.concatenate(sums, axis=0)), axis=1),
+        mean_ref[...],
+        preferred_element_type=jnp.float32,
+    )
+    chunk = jnp.zeros((quarter, LANES), jnp.float32)
+    for slot in range(slots):
         for part in range(FACES):
-            chunk = jnp.where(
-                group_of == part * slots + slot,
-                means[part * quarter : (part + 1) * quarter],
-                chunk,
-            )
-        avg_ref[...] = chunk
-        return carry
-
-    avg_ref[...] = jnp.zeros((quarter, LANES), jnp.float32)
-    lax.fori_loop(0, slots, one_patch, 0)
+            row = slot * AVG_ROWS + part * quarter
+            chunk = jnp.where(group_of == part * slots + slot, means[row : row + quarter], chunk)
+    avg_ref[...] = chunk
     copies = [
         pltpu.make_async_copy(avg_ref, avg_hbm.at[target], avg_sems.at[target])
         for target in range(sources)
@@ -1041,6 +1046,7 @@
             pltpu.VMEM((2 * SPECIES * FZ, STRIP_ROWS), jnp.bfloat16),
             pltpu.VMEM((2 * LANES, LANES), jnp.bfloat16),
             pltpu.VMEM(chunk, jnp.float32),
+            pltpu.VMEM((slots * 2 * SPECIES * FZ, EDGE * EDGE), jnp.float32),
             pltpu.VMEM((slots * FIELD_ROWS, LANES), jnp.float32),
             pltpu.VMEM((RATIO - 1, SPECIES * TILES * FZ, LANES), jnp.float32),
             pltpu.VMEM(fine_state.shape, jnp.float32),

time: 50.3 us -> 48.7 us (0.968)
  Pallas kernels: 23.4 us -> 21.6 us
    pallas_call x1, Pallas kernels: 10.3 us -> 8.79 us  [per_device(): pl.pallas_call(functools.partial(finish_kernel, slots=slots), out_shape=[...]
where the time goes in v6:
time: 48.7 us; the launch traced here: 48.1 us
  starting transfers between devices  23.4 us (48%)
  Pallas kernels  21.6 us (44%)
  waiting for transfers between devices  2.27 us (5%)
  between operations  0.73 us (1%)
    all_to_all x2, starting transfers between devices, exchange(): return lax.all_to_all(chunks, 'af', split_axis=0, concat_axis=0, tiled=True)  13.9 us
    ppermute x4, starting transfers between devices, shifted(): return lax.ppermute(values, axis, pairs)  9.53 us
    pallas_call x1, Pallas kernels, per_device(): pl.pallas_call(functools.partial(finish_kernel, slots=slots), out_shape=[...  8.79 us
    pallas_call x1, Pallas kernels, per_device(): pl.pallas_call(functools.partial(prepare_kernel, slots=slots), out_shape=...  6.81 us
    pallas_call x1, Pallas kernels, per_device(): pl.pallas_call(functools.partial(strips_kernel, slots=slots, **sizes), ou...  3.63 us
    all_to_all x2, waiting for transfers between devices, exchange(): return lax.all_to_all(chunks, 'af', split_axis=0, concat_axis=0, tiled=True)  1.47 us
    pallas_call x1, Pallas kernels, per_device(): pl.pallas_call(functools.partial(place_kernel, slots=slots, **sizes), out...  1.21 us
    pallas_call x1, Pallas kernels, per_device(): pl.pallas_call(functools.partial(edges_kernel, cells_x=cells_x, cells_y=c...  1.17 us
  transfers between devices with their start and end apart: 6, of which 2 were waited for; matrix products, arithmetic and copies ran while one was open for 0% of the time, Pallas kernels for 17%

profile of v6, /device:TPU:0, one launch (start us, length us, event | category | flops | bytes accessed | tf_op | source)
XLA Modules:
  0.0 48.1 jit_solution(6519813203157725699)
XLA Ops:
  0.6 3.6 %strips.1 = (f32[384,256]{1,0:T(8,128)}, f32[8,64,128]{2,1,0:T(8,128)}, s32[16,256]{1,0:T(8,128)S(1)}, f32[32,256]{1,0:T(8,128)S(1)}, f32[32,256]{1,0:T(8,128)S(...) custom-call(s32[2,128]{1,0:T(2,128)} %bitcast.9, f32[384,256]{1,0:T(8,128)} %bitcast.5, f32[128,256]{1,0:T(8,128)} %bitcast.7, ...), custom_call_target="tpu_custom_call" | custom-call | tf_op jit(solution)/shard_map/strips/pallas_call | solution.py:968
  4.3 7.3 %all-to-all-start = ((f32[8,64,128]{2,1,0:T(8,128)}), f32[8,64,128]{2,1,0:T(8,128)S(1)}, u32[]{:S(2)}, u32[]{:S(2)}) async-start(f32[8,64,128]{2,1,0:T(8,128)} %get-tuple-element.17), calls=%async_computation | async-start | bytes 524288 | tf_op jit(solution)/shard_map/all_to_all | solution.py:951
  11.6 3.9 %collective-permute-start = (f32[32,256]{1,0:T(8,128)S(1)}, f32[32,256]{1,0:T(8,128)S(1)}, u32[]{:S(2)}, u32[]{:S(2)}) collective-permute-start(f32[32,256]{1,0:T(8,128)S(1)} %get-tuple-element.24), channel_id=1, source_target_pairs={{0,1},{1,2},{2,3},{3,4},{4,5},{5,6},{6,7},{8,9},{9,10},{10,11},{11... | collective-permute-start | bytes 98312 | tf_op jit(solution)/shard_map/ppermute | solution.py:947
  15.5 1.3 %collective-permute-start.1 = (f32[32,256]{1,0:T(8,128)S(1)}, f32[32,256]{1,0:T(8,128)S(1)}, u32[]{:S(2)}, u32[]{:S(2)}) collective-permute-start(f32[32,256]{1,0:T(8,128)S(1)} %get-tuple-element.20.after_ref), channel_id=1, source_target_pairs={{1,0},{2,1},{3,2},{4,3},{5,4},{6,5},{7,6},{9,8},{10,9},{11,10},{12... | collective-permute-start | bytes 98312 | tf_op jit(solution)/shard_map/ppermute | solution.py:947
  16.8 6.8 %prepare.1 = (f32[3872,128]{1,0:T(8,128)}, f32[8192,128]{1,0:T(8,128)}, f32[1312,128]{1,0:T(8,128)}) custom-call(f32[32,256]{1,0:T(8,128)S(1)} %get-tuple-element.20.after_ref, f32[4,3,32,1024]{3,2,1,0:T(8,128)} %state_hbm.1, f32[4,32,1024]{2,1,0:T(8,128)} %kappa_hbm.1, f32[4,32,1024]{2,1,0:T(8,128)} %rate_hbm.1), custom_call_target="tpu_custom_call" | custom-call | tf_op jit(solution)/shard_map/prepare/pallas_call | solution.py:1018
  23.6 0.0 collective-permute-done.xl_ref
  23.6 0.0 collective-permute-done.1.xr_ref
  23.6 0.0 all-to-all-done.strips_ref
  23.7 8.8 %finish.1 = (f32[4,3,32,1024]{3,2,1,0:T(8,128)}, f32[8,48,128]{2,1,0:T(8,128)}) custom-call(f32[8,64,128]{2,1,0:T(8,128)S(1)} %all-to-all-done.strips_ref, f32[3872,128]{1,0:T(8,128)} %get-tuple-element.21.fields_hbm, f32[8192,128]{1,0:T(8,128)} %get-tuple-element.22.coeffs_hbm, f32[1312,128]{1,0:T(8,128)} %get-tuple-element.23.upward_hbm, ...), custom_call_target="tpu_custom_call" | custom-call | tf_op jit(solution)/shard_map/finish/pallas_call | solution.py:1038
  32.5 6.6 %all-to-all-start.1 = ((f32[8,48,128]{2,1,0:T(8,128)}), f32[8,48,128]{2,1,0:T(8,128)S(1)}, u32[]{:S(2)}, u32[]{:S(2)}) async-start(f32[8,48,128]{2,1,0:T(8,128)} %get-tuple-element.25), calls=%async_computation.1 | async-start | bytes 393216 | tf_op jit(solution)/shard_map/all_to_all | solution.py:951
  39.1 1.3 %collective-permute-start.3 = (f32[16,128]{1,0:T(8,128)S(1)}, f32[16,128]{1,0:T(8,128)S(1)}, u32[]{:S(2)}, u32[]{:S(2)}) collective-permute-start(f32[16,128]{1,0:T(8,128)S(1)} %get-tuple-element.27.ylo_ref), channel_id=1, source_target_pairs={{8,0},{16,8},{24,16},{9,1},{17,9},{25,17},{10,2},{18,10},{26,18},{... | collective-permute-start | bytes 24584 | tf_op jit(solution)/shard_map/ppermute | solution.py:947
  40.4 3.0 %collective-permute-start.2 = (f32[16,128]{1,0:T(8,128)S(1)}, f32[16,128]{1,0:T(8,128)S(1)}, u32[]{:S(2)}, u32[]{:S(2)}) collective-permute-start(f32[16,128]{1,0:T(8,128)S(1)} %get-tuple-element.28.yhi_ref), channel_id=1, source_target_pairs={{0,8},{8,16},{16,24},{1,9},{9,17},{17,25},{2,10},{10,18},{18,26},{... | collective-permute-start | bytes 24584 | tf_op jit(solution)/shard_map/ppermute | solution.py:947
  43.4 0.0 collective-permute-done.3.yr_ref
  43.4 0.8 %collective-permute-done.2.yl_ref = f32[16,128]{1,0:T(8,128)S(1)} collective-permute-done((f32[16,128]{1,0:T(8,128)S(1)}, f32[16,128]{1,0:T(8,128)S(1)}, u32[]{:S(2)}, u32[]{:S(2)}) %collective-permute-start.2) | collective-permute-done | bytes 8224 | tf_op jit(solution)/shard_map/ppermute | solution.py:947
  44.2 1.2 %edges.1.new_ref = f32[384,256]{1,0:T(8,128)S(1)} custom-call(f32[384,256]{1,0:T(8,128)} %get-tuple-element.26.new_hbm, f32[32,256]{1,0:T(8,128)S(1)} %get-tuple-element.18.low_ref.xlo_ref, f32[32,256]{1,0:T(8,128)S(1)} %get-tuple-element.19.high_ref.xhi_ref, f32[16,128]{1,0:T(8,128)S(1)} %get-tuple-element.27.ylo_ref, ...), custom_call_target="tpu_custom_call" | custom-call | tf_op jit(solution)/shard_map/edges/pallas_call | solution.py:1065
  45.4 1.5 %all-to-all-done.1.avg_ref = f32[8,48,128]{2,1,0:T(8,128)S(1)} async-done(((f32[8,48,128]{2,1,0:T(8,128)}), f32[8,48,128]{2,1,0:T(8,128)S(1)}, u32[]{:S(2)}, u32[]{:S(2)}) %all-to-all-start.1) | async-done | bytes 196640 | tf_op jit(solution)/shard_map/all_to_all | solution.py:951
  46.9 1.2 %place.1 = f32[384,256]{1,0:T(8,128)} custom-call(s32[16,256]{1,0:T(8,128)S(1)} %get-tuple-element.16.place_ref, f32[8,48,128]{2,1,0:T(8,128)S(1)} %all-to-all-done.1.avg_ref, f32[384,256]{1,0:T(8,128)S(1)} %edges.1.new_ref), custom_call_target="tpu_custom_call" | custom-call | tf_op jit(solution)/shard_map/place/pallas_call | solution.py:1075
  (1 shorter events, 0.0 us)
Async XLA Ops:
  4.3 19.4 %all-to-all-start = ((f32[8,64,128]{2,1,0:T(8,128)}), f32[8,64,128]{2,1,0:T(8,128)S(1)}, u32[]{:S(2)}, u32[]{:S(2)}) async-start(f32[8,64,128]{2,1,0:T(8,128)} %get-tuple-element.17), calls=%async_computation | async-start | bytes 524288 | tf_op jit(solution)/shard_map/all_to_all | solution.py:951
  11.6 12.1 %collective-permute-start = (f32[32,256]{1,0:T(8,128)S(1)}, f32[32,256]{1,0:T(8,128)S(1)}, u32[]{:S(2)}, u32[]{:S(2)}) collective-permute-start(f32[32,256]{1,0:T(8,128)S(1)} %get-tuple-element.24), channel_id=1, source_target_pairs={{0,1},{1,2},{2,3},{3,4},{4,5},{5,6},{6,7},{8,9},{9,10},{10,11},{11... | collective-permute-start | bytes 98312 | tf_op jit(solution)/shard_map/ppermute | solution.py:947
  15.5 8.1 %collective-permute-start.1 = (f32[32,256]{1,0:T(8,128)S(1)}, f32[32,256]{1,0:T(8,128)S(1)}, u32[]{:S(2)}, u32[]{:S(2)}) collective-permute-start(f32[32,256]{1,0:T(8,128)S(1)} %get-tuple-element.20.after_ref), channel_id=1, source_target_pairs={{1,0},{2,1},{3,2},{4,3},{5,4},{6,5},{7,6},{9,8},{10,9},{11,10},{12... | collective-permute-start | bytes 98312 | tf_op jit(solution)/shard_map/ppermute | solution.py:947
  32.5 14.4 %all-to-all-start.1 = ((f32[8,48,128]{2,1,0:T(8,128)}), f32[8,48,128]{2,1,0:T(8,128)S(1)}, u32[]{:S(2)}, u32[]{:S(2)}) async-start(f32[8,48,128]{2,1,0:T(8,128)} %get-tuple-element.25), calls=%async_computation.1 | async-start | bytes 393216 | tf_op jit(solution)/shard_map/all_to_all | solution.py:951
  39.1 4.3 %collective-permute-start.3 = (f32[16,128]{1,0:T(8,128)S(1)}, f32[16,128]{1,0:T(8,128)S(1)}, u32[]{:S(2)}, u32[]{:S(2)}) collective-permute-start(f32[16,128]{1,0:T(8,128)S(1)} %get-tuple-element.27.ylo_ref), channel_id=1, source_target_pairs={{8,0},{16,8},{24,16},{9,1},{17,9},{25,17},{10,2},{18,10},{26,18},{... | collective-permute-start | bytes 24584 | tf_op jit(solution)/shard_map/ppermute | solution.py:947
  40.4 3.8 %collective-permute-start.2 = (f32[16,128]{1,0:T(8,128)S(1)}, f32[16,128]{1,0:T(8,128)S(1)}, u32[]{:S(2)}, u32[]{:S(2)}) collective-permute-start(f32[16,128]{1,0:T(8,128)S(1)} %get-tuple-element.28.yhi_ref), channel_id=1, source_target_pairs={{0,8},{8,16},{16,24},{1,9},{9,17},{17,25},{2,10},{10,18},{18,26},{... | collective-permute-start | bytes 24584 | tf_op jit(solution)/shard_map/ppermute | solution.py:947

commit v7 on v6

--- a/solution.py
+++ b/solution.py
@@ -426,7 +426,7 @@
 
 
 def aligned(start, size):
-    return pl.ds(pl.multiple_of(start, 8), size)
+    return pl.ds(start if isinstance(start, int) else pl.multiple_of(start, 8), size)
 
 
 def padded_at(block, ztile):
@@ -528,7 +528,7 @@
     for slot in range(slots):
         start_all(loads(slot))
 
-    def stores(slot):
+    def stores(slot, start, stop):
         return [
             pltpu.make_async_copy(
                 source.at[aligned(slot * size, size)],
@@ -542,6 +542,7 @@
                     (upward, upward_hbm, UPWARD_ROWS),
                 )
             )
+            if start <= order < stop
         ]
 
     for ref, size in (
@@ -556,7 +557,7 @@
     column = lane % EDGE
     side_y = jnp.where((column == 0) | (column == EDGE - 1), 1.0, 0.0)
 
-    def one_patch(slot, carry):
+    def one_patch(slot):
         for copy in loads(slot):
             copy.wait()
 
@@ -620,6 +621,7 @@
                 if tile + 1 < TILES:
                     center, turned = center_after, turned_after
 
+        start_all(stores(slot, 1, 3))
         for ztile in range(ZTILES):
             advance(
                 first,
@@ -632,12 +634,12 @@
                 ztile,
                 lambda field, tile: None,
             )
-        start_all(stores(slot))
-        return carry
-
-    lax.fori_loop(0, slots, one_patch, 0)
+        start_all(stores(slot, 0, 1))
+
     for slot in range(slots):
-        for copy in stores(slot):
+        one_patch(slot)
+    for slot in range(slots):
+        for copy in stores(slot, 0, 3):
             copy.wait()
 
 
@@ -719,14 +721,11 @@
                 stretched[slot], ghost_ref[:, cols], preferred_element_type=jnp.float32
             )
 
-    def one_patch(slot, carry):
+    def one_patch(slot):
         for copy in loads(slot):
             copy.wait()
-
-        @pl.when(slot + 1 < slots)
-        def _():
+        if slot + 1 < slots:
             start_all(loads(slot + 1))
-
         base = slot * FIELD_ROWS
         scales = slot * COEFF_ROWS
         for tile in range(TILES):
@@ -760,9 +759,8 @@
                 staged[slot, field, :, pl.ds(tile * LANES, LANES)] = first[spot, :]
         send_out(slot).start()
 
-        return carry
-
-    lax.fori_loop(0, slots, one_patch, 0)
+    for slot in range(slots):
+        one_patch(slot)
     sums = []
     for slot in range(slots):
         for field in range(SPECIES):

time: 48.7 us -> 47.9 us (0.984)
  Pallas kernels: 21.6 us -> 20.9 us
    pallas_call x1, Pallas kernels: 8.79 us -> 8.29 us  [per_device(): pl.pallas_call(functools.partial(finish_kernel, slots=slots), out_shape=[...]
  transfers between devices with their start and end apart: 6 -> 6, of which waited for: 2 -> 2; matrix products, arithmetic and copies ran while one was open for 0% -> 0% of each run, Pallas kernels for 17% -> 16%
where the time goes in v7:
time: 47.9 us; the launch traced here: 47.3 us
  starting transfers between devices  23.4 us (49%)
  Pallas kernels  20.9 us (44%)
  waiting for transfers between devices  2.27 us (5%)
  between operations  0.73 us (2%)
    all_to_all x2, starting transfers between devices, exchange(): return lax.all_to_all(chunks, 'af', split_axis=0, concat_axis=0, tiled=True)  13.9 us
    ppermute x4, starting transfers between devices, shifted(): return lax.ppermute(values, axis, pairs)  9.53 us
    pallas_call x1, Pallas kernels, per_device(): pl.pallas_call(functools.partial(finish_kernel, slots=slots), out_shape=[...  8.29 us
    pallas_call x1, Pallas kernels, per_device(): pl.pallas_call(functools.partial(prepare_kernel, slots=slots), out_shape=...  6.59 us
    pallas_call x1, Pallas kernels, per_device(): pl.pallas_call(functools.partial(strips_kernel, slots=slots, **sizes), ou...  3.63 us
    all_to_all x2, waiting for transfers between devices, exchange(): return lax.all_to_all(chunks, 'af', split_axis=0, concat_axis=0, tiled=True)  1.47 us
    pallas_call x1, Pallas kernels, per_device(): pl.pallas_call(functools.partial(place_kernel, slots=slots, **sizes), out...  1.21 us
    pallas_call x1, Pallas kernels, per_device(): pl.pallas_call(functools.partial(edges_kernel, cells_x=cells_x, cells_y=c...  1.17 us
  transfers between devices with their start and end apart: 6, of which 2 were waited for; matrix products, arithmetic and copies ran while one was open for 0% of the time, Pallas kernels for 16%

profile of v7, /device:TPU:0, one launch (start us, length us, event | category | flops | bytes accessed | tf_op | source)
XLA Modules:
  0.0 47.3 jit_solution(5720546484384906957)
XLA Ops:
  0.6 3.6 %strips.1 = (f32[384,256]{1,0:T(8,128)}, f32[8,64,128]{2,1,0:T(8,128)}, s32[16,256]{1,0:T(8,128)S(1)}, f32[32,256]{1,0:T(8,128)S(1)}, f32[32,256]{1,0:T(8,128)S(...) custom-call(s32[2,128]{1,0:T(2,128)} %bitcast.9, f32[384,256]{1,0:T(8,128)} %bitcast.5, f32[128,256]{1,0:T(8,128)} %bitcast.7, ...), custom_call_target="tpu_custom_call" | custom-call | tf_op jit(solution)/shard_map/strips/pallas_call | solution.py:966
  4.3 7.3 %all-to-all-start = ((f32[8,64,128]{2,1,0:T(8,128)}), f32[8,64,128]{2,1,0:T(8,128)S(1)}, u32[]{:S(2)}, u32[]{:S(2)}) async-start(f32[8,64,128]{2,1,0:T(8,128)} %get-tuple-element.17), calls=%async_computation | async-start | bytes 524288 | tf_op jit(solution)/shard_map/all_to_all | solution.py:949
  11.6 3.9 %collective-permute-start = (f32[32,256]{1,0:T(8,128)S(1)}, f32[32,256]{1,0:T(8,128)S(1)}, u32[]{:S(2)}, u32[]{:S(2)}) collective-permute-start(f32[32,256]{1,0:T(8,128)S(1)} %get-tuple-element.24), channel_id=1, source_target_pairs={{0,1},{1,2},{2,3},{3,4},{4,5},{5,6},{6,7},{8,9},{9,10},{10,11},{11... | collective-permute-start | bytes 98312 | tf_op jit(solution)/shard_map/ppermute | solution.py:945
  15.5 1.3 %collective-permute-start.1 = (f32[32,256]{1,0:T(8,128)S(1)}, f32[32,256]{1,0:T(8,128)S(1)}, u32[]{:S(2)}, u32[]{:S(2)}) collective-permute-start(f32[32,256]{1,0:T(8,128)S(1)} %get-tuple-element.20.after_ref), channel_id=1, source_target_pairs={{1,0},{2,1},{3,2},{4,3},{5,4},{6,5},{7,6},{9,8},{10,9},{11,10},{12... | collective-permute-start | bytes 98312 | tf_op jit(solution)/shard_map/ppermute | solution.py:945
  16.8 6.6 %prepare.1 = (f32[3872,128]{1,0:T(8,128)}, f32[8192,128]{1,0:T(8,128)}, f32[1312,128]{1,0:T(8,128)}) custom-call(f32[32,256]{1,0:T(8,128)S(1)} %get-tuple-element.20.after_ref, f32[4,3,32,1024]{3,2,1,0:T(8,128)} %state_hbm.1, f32[4,32,1024]{2,1,0:T(8,128)} %kappa_hbm.1, f32[4,32,1024]{2,1,0:T(8,128)} %rate_hbm.1), custom_call_target="tpu_custom_call" | custom-call | tf_op jit(solution)/shard_map/prepare/pallas_call | solution.py:1016
  23.4 0.0 collective-permute-done.xl_ref
  23.4 0.0 collective-permute-done.1.xr_ref
  23.4 0.0 all-to-all-done.strips_ref
  23.4 8.3 %finish.1 = (f32[4,3,32,1024]{3,2,1,0:T(8,128)}, f32[8,48,128]{2,1,0:T(8,128)}) custom-call(f32[8,64,128]{2,1,0:T(8,128)S(1)} %all-to-all-done.strips_ref, f32[3872,128]{1,0:T(8,128)} %get-tuple-element.21.fields_hbm, f32[8192,128]{1,0:T(8,128)} %get-tuple-element.22.coeffs_hbm, f32[1312,128]{1,0:T(8,128)} %get-tuple-element.23.upward_hbm, ...), custom_call_target="tpu_custom_call" | custom-call | tf_op jit(solution)/shard_map/finish/pallas_call | solution.py:1036
  31.7 6.6 %all-to-all-start.1 = ((f32[8,48,128]{2,1,0:T(8,128)}), f32[8,48,128]{2,1,0:T(8,128)S(1)}, u32[]{:S(2)}, u32[]{:S(2)}) async-start(f32[8,48,128]{2,1,0:T(8,128)} %get-tuple-element.25), calls=%async_computation.1 | async-start | bytes 393216 | tf_op jit(solution)/shard_map/all_to_all | solution.py:949
  38.4 1.3 %collective-permute-start.3 = (f32[16,128]{1,0:T(8,128)S(1)}, f32[16,128]{1,0:T(8,128)S(1)}, u32[]{:S(2)}, u32[]{:S(2)}) collective-permute-start(f32[16,128]{1,0:T(8,128)S(1)} %get-tuple-element.27.ylo_ref), channel_id=1, source_target_pairs={{8,0},{16,8},{24,16},{9,1},{17,9},{25,17},{10,2},{18,10},{26,18},{... | collective-permute-start | bytes 24584 | tf_op jit(solution)/shard_map/ppermute | solution.py:945
  39.6 3.0 %collective-permute-start.2 = (f32[16,128]{1,0:T(8,128)S(1)}, f32[16,128]{1,0:T(8,128)S(1)}, u32[]{:S(2)}, u32[]{:S(2)}) collective-permute-start(f32[16,128]{1,0:T(8,128)S(1)} %get-tuple-element.28.yhi_ref), channel_id=1, source_target_pairs={{0,8},{8,16},{16,24},{1,9},{9,17},{17,25},{2,10},{10,18},{18,26},{... | collective-permute-start | bytes 24584 | tf_op jit(solution)/shard_map/ppermute | solution.py:945
  42.7 0.0 collective-permute-done.3.yr_ref
  42.7 0.8 %collective-permute-done.2.yl_ref = f32[16,128]{1,0:T(8,128)S(1)} collective-permute-done((f32[16,128]{1,0:T(8,128)S(1)}, f32[16,128]{1,0:T(8,128)S(1)}, u32[]{:S(2)}, u32[]{:S(2)}) %collective-permute-start.2) | collective-permute-done | bytes 8224 | tf_op jit(solution)/shard_map/ppermute | solution.py:945
  43.5 1.2 %edges.1.new_ref = f32[384,256]{1,0:T(8,128)S(1)} custom-call(f32[384,256]{1,0:T(8,128)} %get-tuple-element.26.new_hbm, f32[32,256]{1,0:T(8,128)S(1)} %get-tuple-element.18.low_ref.xlo_ref, f32[32,256]{1,0:T(8,128)S(1)} %get-tuple-element.19.high_ref.xhi_ref, f32[16,128]{1,0:T(8,128)S(1)} %get-tuple-element.27.ylo_ref, ...), custom_call_target="tpu_custom_call" | custom-call | tf_op jit(solution)/shard_map/edges/pallas_call | solution.py:1063
  44.7 1.5 %all-to-all-done.1.avg_ref = f32[8,48,128]{2,1,0:T(8,128)S(1)} async-done(((f32[8,48,128]{2,1,0:T(8,128)}), f32[8,48,128]{2,1,0:T(8,128)S(1)}, u32[]{:S(2)}, u32[]{:S(2)}) %all-to-all-start.1) | async-done | bytes 196640 | tf_op jit(solution)/shard_map/all_to_all | solution.py:949
  46.1 1.2 %place.1 = f32[384,256]{1,0:T(8,128)} custom-call(s32[16,256]{1,0:T(8,128)S(1)} %get-tuple-element.16.place_ref, f32[8,48,128]{2,1,0:T(8,128)S(1)} %all-to-all-done.1.avg_ref, f32[384,256]{1,0:T(8,128)S(1)} %edges.1.new_ref), custom_call_target="tpu_custom_call" | custom-call | tf_op jit(solution)/shard_map/place/pallas_call | solution.py:1073
  (1 shorter events, 0.0 us)
Async XLA Ops:
  4.3 19.1 %all-to-all-start = ((f32[8,64,128]{2,1,0:T(8,128)}), f32[8,64,128]{2,1,0:T(8,128)S(1)}, u32[]{:S(2)}, u32[]{:S(2)}) async-start(f32[8,64,128]{2,1,0:T(8,128)} %get-tuple-element.17), calls=%async_computation | async-start | bytes 524288 | tf_op jit(solution)/shard_map/all_to_all | solution.py:949
  11.6 11.8 %collective-permute-start = (f32[32,256]{1,0:T(8,128)S(1)}, f32[32,256]{1,0:T(8,128)S(1)}, u32[]{:S(2)}, u32[]{:S(2)}) collective-permute-start(f32[32,256]{1,0:T(8,128)S(1)} %get-tuple-element.24), channel_id=1, source_target_pairs={{0,1},{1,2},{2,3},{3,4},{4,5},{5,6},{6,7},{8,9},{9,10},{10,11},{11... | collective-permute-start | bytes 98312 | tf_op jit(solution)/shard_map/ppermute | solution.py:945
  15.5 7.9 %collective-permute-start.1 = (f32[32,256]{1,0:T(8,128)S(1)}, f32[32,256]{1,0:T(8,128)S(1)}, u32[]{:S(2)}, u32[]{:S(2)}) collective-permute-start(f32[32,256]{1,0:T(8,128)S(1)} %get-tuple-element.20.after_ref), channel_id=1, source_target_pairs={{1,0},{2,1},{3,2},{4,3},{5,4},{6,5},{7,6},{9,8},{10,9},{11,10},{12... | collective-permute-start | bytes 98312 | tf_op jit(solution)/shard_map/ppermute | solution.py:945
  31.7 14.4 %all-to-all-start.1 = ((f32[8,48,128]{2,1,0:T(8,128)}), f32[8,48,128]{2,1,0:T(8,128)S(1)}, u32[]{:S(2)}, u32[]{:S(2)}) async-start(f32[8,48,128]{2,1,0:T(8,128)} %get-tuple-element.25), calls=%async_computation.1 | async-start | bytes 393216 | tf_op jit(solution)/shard_map/all_to_all | solution.py:949
  38.4 4.3 %collective-permute-start.3 = (f32[16,128]{1,0:T(8,128)S(1)}, f32[16,128]{1,0:T(8,128)S(1)}, u32[]{:S(2)}, u32[]{:S(2)}) collective-permute-start(f32[16,128]{1,0:T(8,128)S(1)} %get-tuple-element.27.ylo_ref), channel_id=1, source_target_pairs={{8,0},{16,8},{24,16},{9,1},{17,9},{25,17},{10,2},{18,10},{26,18},{... | collective-permute-start | bytes 24584 | tf_op jit(solution)/shard_map/ppermute | solution.py:945
  39.6 3.8 %collective-permute-start.2 = (f32[16,128]{1,0:T(8,128)S(1)}, f32[16,128]{1,0:T(8,128)S(1)}, u32[]{:S(2)}, u32[]{:S(2)}) collective-permute-start(f32[16,128]{1,0:T(8,128)S(1)} %get-tuple-element.28.yhi_ref), channel_id=1, source_target_pairs={{0,8},{8,16},{16,24},{1,9},{9,17},{17,25},{2,10},{10,18},{18,26},{... | collective-permute-start | bytes 24584 | tf_op jit(solution)/shard_map/ppermute | solution.py:945

commit v8 on v7

--- a/solution.py
+++ b/solution.py
@@ -705,20 +705,18 @@
     def send_out(slot):
         return pltpu.make_async_copy(staged.at[slot], out_hbm.at[slot], sems.at[slot])
 
-    stretched = [
-        jnp.dot(
+    ghost_rows = 2 * SPECIES * FZ
+
+    def make_ghosts(slot):
+        stretched = jnp.dot(
             plane_ref[...],
             jnp.concatenate(split_pair(roll_lanes(gathered, -slot * BLK)), axis=1),
             preferred_element_type=jnp.float32,
         ).astype(jnp.bfloat16)
-        for slot in range(slots)
-    ]
-    ghost_rows = 2 * SPECIES * FZ
-    for pair in range(TILES // 2):
-        cols = slice(2 * pair * LANES, 2 * (pair + 1) * LANES)
-        for slot in range(slots):
+        for pair in range(TILES // 2):
+            cols = slice(2 * pair * LANES, 2 * (pair + 1) * LANES)
             ghosts_ref[slot * ghost_rows : (slot + 1) * ghost_rows, cols] = jnp.dot(
-                stretched[slot], ghost_ref[:, cols], preferred_element_type=jnp.float32
+                stretched, ghost_ref[:, cols], preferred_element_type=jnp.float32
             )
 
     def one_patch(slot):
@@ -743,6 +741,8 @@
                 spot = aligned(base + padded_at(field * TILES + tile, 0), FZ)
                 fields_ref[spot, :] = fields_ref[spot, :] + DIFFUSE[field] * old
 
+        if slot + 1 < slots:
+            make_ghosts(slot + 1)
         for step in range(1, RATIO):
             source, target = (fields_ref, first) if step % 2 else (first, fields_ref)
             for ztile in range(ZTILES):
@@ -759,26 +759,26 @@
                 staged[slot, field, :, pl.ds(tile * LANES, LANES)] = first[spot, :]
         send_out(slot).start()
 
-    for slot in range(slots):
-        one_patch(slot)
-    sums = []
-    for slot in range(slots):
+        sums = []
         for field in range(SPECIES):
             for plane in range(NZC):
                 start = slot * FIELD_ROWS + field * TILES * STRIDE + PAD + RATIO * plane
                 part = [first[pl.ds(start + z, TILES, stride=STRIDE), :] for z in range(RATIO)]
                 sums.append((part[0] + part[1]) + (part[2] + part[3]))
-    means = jnp.dot(
-        jnp.concatenate(split_pair(jnp.concatenate(sums, axis=0)), axis=1),
-        mean_ref[...],
-        preferred_element_type=jnp.float32,
-    )
-    chunk = jnp.zeros((quarter, LANES), jnp.float32)
+        means = jnp.dot(
+            jnp.concatenate(split_pair(jnp.concatenate(sums, axis=0)), axis=1),
+            mean_ref[...],
+            preferred_element_type=jnp.float32,
+        )
+        chunk = jnp.zeros((quarter, LANES), jnp.float32) if slot == 0 else avg_ref[...]
+        for part in range(FACES):
+            row = part * quarter
+            chunk = jnp.where(group_of == part * slots + slot, means[row : row + quarter], chunk)
+        avg_ref[...] = chunk
+
+    make_ghosts(0)
     for slot in range(slots):
-        for part in range(FACES):
-            row = slot * AVG_ROWS + part * quarter
-            chunk = jnp.where(group_of == part * slots + slot, means[row : row + quarter], chunk)
-    avg_ref[...] = chunk
+        one_patch(slot)
     copies = [
         pltpu.make_async_copy(avg_ref, avg_hbm.at[target], avg_sems.at[target])
         for target in range(sources)

time: 47.9 us -> 48.6 us (1.015)
  Pallas kernels: 20.9 us -> 21.6 us
    pallas_call x1, Pallas kernels: 8.29 us -> 8.99 us  [per_device(): pl.pallas_call(functools.partial(finish_kernel, slots=slots), out_shape=[...]
where the time goes in v8:
time: 48.6 us; the launch traced here: 48.1 us
  starting transfers between devices  23.4 us (48%)
  Pallas kernels  21.6 us (44%)
  waiting for transfers between devices  2.27 us (5%)
  between operations  0.73 us (2%)
    all_to_all x2, starting transfers between devices, exchange(): return lax.all_to_all(chunks, 'af', split_axis=0, concat_axis=0, tiled=True)  13.9 us
    ppermute x4, starting transfers between devices, shifted(): return lax.ppermute(values, axis, pairs)  9.53 us
    pallas_call x1, Pallas kernels, per_device(): pl.pallas_call(functools.partial(finish_kernel, slots=slots), out_shape=[...  8.99 us
    pallas_call x1, Pallas kernels, per_device(): pl.pallas_call(functools.partial(prepare_kernel, slots=slots), out_shape=...  6.59 us
    pallas_call x1, Pallas kernels, per_device(): pl.pallas_call(functools.partial(strips_kernel, slots=slots, **sizes), ou...  3.63 us
    all_to_all x2, waiting for transfers between devices, exchange(): return lax.all_to_all(chunks, 'af', split_axis=0, concat_axis=0, tiled=True)  1.47 us
    pallas_call x1, Pallas kernels, per_device(): pl.pallas_call(functools.partial(place_kernel, slots=slots, **sizes), out...  1.21 us
    pallas_call x1, Pallas kernels, per_device(): pl.pallas_call(functools.partial(edges_kernel, cells_x=cells_x, cells_y=c...  1.17 us
  transfers between devices with their start and end apart: 6, of which 2 were waited for; matrix products, arithmetic and copies ran while one was open for 0% of the time, Pallas kernels for 16%

profile of v8, /device:TPU:0, one launch (start us, length us, event | category | flops | bytes accessed | tf_op | source)
XLA Modules:
  0.0 48.1 jit_solution(6328130346383712083)
XLA Ops:
  0.6 3.6 %strips.1 = (f32[384,256]{1,0:T(8,128)}, f32[8,64,128]{2,1,0:T(8,128)}, s32[16,256]{1,0:T(8,128)S(1)}, f32[32,256]{1,0:T(8,128)S(1)}, f32[32,256]{1,0:T(8,128)S(...) custom-call(s32[2,128]{1,0:T(2,128)} %bitcast.9, f32[384,256]{1,0:T(8,128)} %bitcast.5, f32[128,256]{1,0:T(8,128)} %bitcast.7, ...), custom_call_target="tpu_custom_call" | custom-call | tf_op jit(solution)/shard_map/strips/pallas_call | solution.py:966
  4.3 7.3 %all-to-all-start = ((f32[8,64,128]{2,1,0:T(8,128)}), f32[8,64,128]{2,1,0:T(8,128)S(1)}, u32[]{:S(2)}, u32[]{:S(2)}) async-start(f32[8,64,128]{2,1,0:T(8,128)} %get-tuple-element.17), calls=%async_computation | async-start | bytes 524288 | tf_op jit(solution)/shard_map/all_to_all | solution.py:949
  11.6 3.9 %collective-permute-start = (f32[32,256]{1,0:T(8,128)S(1)}, f32[32,256]{1,0:T(8,128)S(1)}, u32[]{:S(2)}, u32[]{:S(2)}) collective-permute-start(f32[32,256]{1,0:T(8,128)S(1)} %get-tuple-element.24), channel_id=1, source_target_pairs={{0,1},{1,2},{2,3},{3,4},{4,5},{5,6},{6,7},{8,9},{9,10},{10,11},{11... | collective-permute-start | bytes 98312 | tf_op jit(solution)/shard_map/ppermute | solution.py:945
  15.5 1.3 %collective-permute-start.1 = (f32[32,256]{1,0:T(8,128)S(1)}, f32[32,256]{1,0:T(8,128)S(1)}, u32[]{:S(2)}, u32[]{:S(2)}) collective-permute-start(f32[32,256]{1,0:T(8,128)S(1)} %get-tuple-element.20.after_ref), channel_id=1, source_target_pairs={{1,0},{2,1},{3,2},{4,3},{5,4},{6,5},{7,6},{9,8},{10,9},{11,10},{12... | collective-permute-start | bytes 98312 | tf_op jit(solution)/shard_map/ppermute | solution.py:945
  16.8 6.6 %prepare.1 = (f32[3872,128]{1,0:T(8,128)}, f32[8192,128]{1,0:T(8,128)}, f32[1312,128]{1,0:T(8,128)}) custom-call(f32[32,256]{1,0:T(8,128)S(1)} %get-tuple-element.20.after_ref, f32[4,3,32,1024]{3,2,1,0:T(8,128)} %state_hbm.1, f32[4,32,1024]{2,1,0:T(8,128)} %kappa_hbm.1, f32[4,32,1024]{2,1,0:T(8,128)} %rate_hbm.1), custom_call_target="tpu_custom_call" | custom-call | tf_op jit(solution)/shard_map/prepare/pallas_call | solution.py:1016
  23.4 0.0 collective-permute-done.xl_ref
  23.4 0.0 collective-permute-done.1.xr_ref
  23.4 0.0 all-to-all-done.strips_ref
  23.4 9.0 %finish.1 = (f32[4,3,32,1024]{3,2,1,0:T(8,128)}, f32[8,48,128]{2,1,0:T(8,128)}) custom-call(f32[8,64,128]{2,1,0:T(8,128)S(1)} %all-to-all-done.strips_ref, f32[3872,128]{1,0:T(8,128)} %get-tuple-element.21.fields_hbm, f32[8192,128]{1,0:T(8,128)} %get-tuple-element.22.coeffs_hbm, f32[1312,128]{1,0:T(8,128)} %get-tuple-element.23.upward_hbm, ...), custom_call_target="tpu_custom_call" | custom-call | tf_op jit(solution)/shard_map/finish/pallas_call | solution.py:1036
  32.4 6.6 %all-to-all-start.1 = ((f32[8,48,128]{2,1,0:T(8,128)}), f32[8,48,128]{2,1,0:T(8,128)S(1)}, u32[]{:S(2)}, u32[]{:S(2)}) async-start(f32[8,48,128]{2,1,0:T(8,128)} %get-tuple-element.25), calls=%async_computation.1 | async-start | bytes 393216 | tf_op jit(solution)/shard_map/all_to_all | solution.py:949
  39.1 1.3 %collective-permute-start.3 = (f32[16,128]{1,0:T(8,128)S(1)}, f32[16,128]{1,0:T(8,128)S(1)}, u32[]{:S(2)}, u32[]{:S(2)}) collective-permute-start(f32[16,128]{1,0:T(8,128)S(1)} %get-tuple-element.27.ylo_ref), channel_id=1, source_target_pairs={{8,0},{16,8},{24,16},{9,1},{17,9},{25,17},{10,2},{18,10},{26,18},{... | collective-permute-start | bytes 24584 | tf_op jit(solution)/shard_map/ppermute | solution.py:945
  40.3 3.0 %collective-permute-start.2 = (f32[16,128]{1,0:T(8,128)S(1)}, f32[16,128]{1,0:T(8,128)S(1)}, u32[]{:S(2)}, u32[]{:S(2)}) collective-permute-start(f32[16,128]{1,0:T(8,128)S(1)} %get-tuple-element.28.yhi_ref), channel_id=1, source_target_pairs={{0,8},{8,16},{16,24},{1,9},{9,17},{17,25},{2,10},{10,18},{18,26},{... | collective-permute-start | bytes 24584 | tf_op jit(solution)/shard_map/ppermute | solution.py:945
  43.4 0.0 collective-permute-done.3.yr_ref
  43.4 0.8 %collective-permute-done.2.yl_ref = f32[16,128]{1,0:T(8,128)S(1)} collective-permute-done((f32[16,128]{1,0:T(8,128)S(1)}, f32[16,128]{1,0:T(8,128)S(1)}, u32[]{:S(2)}, u32[]{:S(2)}) %collective-permute-start.2) | collective-permute-done | bytes 8224 | tf_op jit(solution)/shard_map/ppermute | solution.py:945
  44.2 1.2 %edges.1.new_ref = f32[384,256]{1,0:T(8,128)S(1)} custom-call(f32[384,256]{1,0:T(8,128)} %get-tuple-element.26.new_hbm, f32[32,256]{1,0:T(8,128)S(1)} %get-tuple-element.18.low_ref.xlo_ref, f32[32,256]{1,0:T(8,128)S(1)} %get-tuple-element.19.high_ref.xhi_ref, f32[16,128]{1,0:T(8,128)S(1)} %get-tuple-element.27.ylo_ref, ...), custom_call_target="tpu_custom_call" | custom-call | tf_op jit(solution)/shard_map/edges/pallas_call | solution.py:1063
  45.4 1.5 %all-to-all-done.1.avg_ref = f32[8,48,128]{2,1,0:T(8,128)S(1)} async-done(((f32[8,48,128]{2,1,0:T(8,128)}), f32[8,48,128]{2,1,0:T(8,128)S(1)}, u32[]{:S(2)}, u32[]{:S(2)}) %all-to-all-start.1) | async-done | bytes 196640 | tf_op jit(solution)/shard_map/all_to_all | solution.py:949
  46.8 1.2 %place.1 = f32[384,256]{1,0:T(8,128)} custom-call(s32[16,256]{1,0:T(8,128)S(1)} %get-tuple-element.16.place_ref, f32[8,48,128]{2,1,0:T(8,128)S(1)} %all-to-all-done.1.avg_ref, f32[384,256]{1,0:T(8,128)S(1)} %edges.1.new_ref), custom_call_target="tpu_custom_call" | custom-call | tf_op jit(solution)/shard_map/place/pallas_call | solution.py:1073
  (1 shorter events, 0.0 us)
Async XLA Ops:
  4.3 19.1 %all-to-all-start = ((f32[8,64,128]{2,1,0:T(8,128)}), f32[8,64,128]{2,1,0:T(8,128)S(1)}, u32[]{:S(2)}, u32[]{:S(2)}) async-start(f32[8,64,128]{2,1,0:T(8,128)} %get-tuple-element.17), calls=%async_computation | async-start | bytes 524288 | tf_op jit(solution)/shard_map/all_to_all | solution.py:949
  11.6 11.8 %collective-permute-start = (f32[32,256]{1,0:T(8,128)S(1)}, f32[32,256]{1,0:T(8,128)S(1)}, u32[]{:S(2)}, u32[]{:S(2)}) collective-permute-start(f32[32,256]{1,0:T(8,128)S(1)} %get-tuple-element.24), channel_id=1, source_target_pairs={{0,1},{1,2},{2,3},{3,4},{4,5},{5,6},{6,7},{8,9},{9,10},{10,11},{11... | collective-permute-start | bytes 98312 | tf_op jit(solution)/shard_map/ppermute | solution.py:945
  15.5 7.9 %collective-permute-start.1 = (f32[32,256]{1,0:T(8,128)S(1)}, f32[32,256]{1,0:T(8,128)S(1)}, u32[]{:S(2)}, u32[]{:S(2)}) collective-permute-start(f32[32,256]{1,0:T(8,128)S(1)} %get-tuple-element.20.after_ref), channel_id=1, source_target_pairs={{1,0},{2,1},{3,2},{4,3},{5,4},{6,5},{7,6},{9,8},{10,9},{11,10},{12... | collective-permute-start | bytes 98312 | tf_op jit(solution)/shard_map/ppermute | solution.py:945
  32.4 14.4 %all-to-all-start.1 = ((f32[8,48,128]{2,1,0:T(8,128)}), f32[8,48,128]{2,1,0:T(8,128)S(1)}, u32[]{:S(2)}, u32[]{:S(2)}) async-start(f32[8,48,128]{2,1,0:T(8,128)} %get-tuple-element.25), calls=%async_computation.1 | async-start | bytes 393216 | tf_op jit(solution)/shard_map/all_to_all | solution.py:949
  39.1 4.3 %collective-permute-start.3 = (f32[16,128]{1,0:T(8,128)S(1)}, f32[16,128]{1,0:T(8,128)S(1)}, u32[]{:S(2)}, u32[]{:S(2)}) collective-permute-start(f32[16,128]{1,0:T(8,128)S(1)} %get-tuple-element.27.ylo_ref), channel_id=1, source_target_pairs={{8,0},{16,8},{24,16},{9,1},{17,9},{25,17},{10,2},{18,10},{26,18},{... | collective-permute-start | bytes 24584 | tf_op jit(solution)/shard_map/ppermute | solution.py:945
  40.3 3.8 %collective-permute-start.2 = (f32[16,128]{1,0:T(8,128)S(1)}, f32[16,128]{1,0:T(8,128)S(1)}, u32[]{:S(2)}, u32[]{:S(2)}) collective-permute-start(f32[16,128]{1,0:T(8,128)S(1)} %get-tuple-element.28.yhi_ref), channel_id=1, source_target_pairs={{0,8},{8,16},{16,24},{1,9},{9,17},{17,25},{2,10},{10,18},{18,26},{... | collective-permute-start | bytes 24584 | tf_op jit(solution)/shard_map/ppermute | solution.py:945

commit v9 on v7

--- a/solution.py
+++ b/solution.py
@@ -504,9 +504,11 @@
     fields_hbm,
     coeffs_hbm,
     upward_hbm,
+    ghost_hbm,
     fields_ref,
     coeffs,
     upward,
+    ghost_ref,
     state_ref,
     kappa_ref,
     rate_ref,
@@ -514,6 +516,7 @@
     conduct,
     sems,
     out_sems,
+    ghost_sem,
     *,
     slots,
 ):
@@ -552,6 +555,10 @@
         (fields_ref, FIELD_ROWS),
     ):
         clear_pads(ref, size)
+    for tile in range(TILES):
+        ghost_ref[:, tile * LANES : (tile + 1) * LANES] = ghost_table(tile)
+    keep_ghost = pltpu.make_async_copy(ghost_ref, ghost_hbm, ghost_sem)
+    keep_ghost.start()
 
     lane = lane_ids((DEPTH, LANES))
     column = lane % EDGE
@@ -580,46 +587,48 @@
                 start = slot * UPWARD_ROWS + padded_at(tile, ztile) + shift
                 return conduct[aligned(start, DEPTH) if shift == 0 else pl.ds(start, DEPTH), :]
 
-            center = here(0, 0)
-            turned = roll_lanes(center, -EDGE)
-            back_before = None
-            for tile in range(TILES):
-                other = turned
+            tiles = range(TILES)
+            centers = [here(tile, 0) for tile in tiles]
+            turned = [roll_lanes(center, -EDGE) for center in centers]
+            total = [FINE_SCALE * side_y * center for center in centers]
+            next_x = []
+            for tile in tiles:
+                other = turned[tile]
                 if tile + 1 < TILES:
-                    center_after = here(tile + 1, 0)
-                    turned_after = roll_lanes(center_after, -EDGE)
-                    other = jnp.where(lane < LANES - EDGE, turned, turned_after)
-                next_x = face(FINE_SCALE, center, other)
+                    other = jnp.where(lane < LANES - EDGE, other, turned[tile + 1])
+                value = face(FINE_SCALE, centers[tile], other)
                 if tile == TILES - 1:
-                    next_x = jnp.where(lane < LANES - EDGE, next_x, 0.0)
-                back = roll_lanes(next_x, EDGE)
-                prev_x = jnp.where(lane >= EDGE, back, 0.0 if tile == 0 else back_before)
-                next_y = jnp.where(
-                    column < EDGE - 1, face(FINE_SCALE, center, roll_lanes(center, -1)), 0.0
-                )
-                prev_y = roll_lanes(next_y, 1)
-                next_z = face(FINE_SCALE, center, here(tile, 1))
+                    value = jnp.where(lane < LANES - EDGE, value, 0.0)
+                next_x.append(value)
+                keep(0, tile, ztile, value)
+            back = [roll_lanes(value, EDGE) for value in next_x]
+            side = [roll_lanes(center, -1) for center in centers]
+            for tile in tiles:
+                prev_x = jnp.where(lane >= EDGE, back[tile], back[tile - 1] if tile else 0.0)
+                keep(1, tile, ztile, prev_x)
+                total[tile] = total[tile] + (next_x[tile] + prev_x)
+            total[0] = total[0] + jnp.where(lane < EDGE, FINE_SCALE * centers[0], 0.0)
+            total[-1] = total[-1] + jnp.where(lane >= LANES - EDGE, FINE_SCALE * centers[-1], 0.0)
+            next_y = []
+            for tile in tiles:
+                value = face(FINE_SCALE, centers[tile], side[tile])
+                next_y.append(jnp.where(column < EDGE - 1, value, 0.0))
+                keep(2, tile, ztile, next_y[tile])
+            prev_y = [roll_lanes(value, 1) for value in next_y]
+            for tile in tiles:
+                total[tile] = total[tile] + (next_y[tile] + prev_y[tile])
+                next_z = face(FINE_SCALE, centers[tile], here(tile, 1))
                 spot = slot * UPWARD_ROWS + padded_at(tile, ztile)
                 upward[aligned(spot, DEPTH), :] = next_z
-                prev_z = upward[pl.ds(spot - 1, DEPTH), :]
-                sides = side_y
-                if tile == 0:
-                    sides = sides + jnp.where(lane < EDGE, 1.0, 0.0)
-                if tile == TILES - 1:
-                    sides = sides + jnp.where(lane >= LANES - EDGE, 1.0, 0.0)
-                scale = FINE_SCALE * center
-                total = (next_x + prev_x) + (next_y + prev_y) + (next_z + prev_z) + sides * scale
-                keep(0, tile, ztile, next_x)
-                keep(1, tile, ztile, prev_x)
-                keep(2, tile, ztile, next_y)
+                total[tile] = total[tile] + next_z
+                keep(7, tile, ztile, FINE_SCALE * centers[tile])
+            for tile in tiles:
+                spot = slot * UPWARD_ROWS + padded_at(tile, ztile)
+                total[tile] = total[tile] + upward[pl.ds(spot - 1, DEPTH), :]
                 rate = rate_ref[slot, pl.ds(DEPTH * ztile, DEPTH), pl.ds(tile * LANES, LANES)]
                 keep(3, tile, ztile, DT_FINE * rate)
                 for field in range(SPECIES):
-                    keep(4 + field, tile, ztile, 1.0 - DIFFUSE[field] * total)
-                keep(7, tile, ztile, scale)
-                back_before = back
-                if tile + 1 < TILES:
-                    center, turned = center_after, turned_after
+                    keep(4 + field, tile, ztile, 1.0 - DIFFUSE[field] * total[tile])
 
         start_all(stores(slot, 1, 3))
         for ztile in range(ZTILES):
@@ -641,6 +650,7 @@
     for slot in range(slots):
         for copy in stores(slot, 0, 3):
             copy.wait()
+    keep_ghost.wait()
 
 
 def finish_kernel(
@@ -648,6 +658,7 @@
     fields_hbm,
     coeffs_hbm,
     upward_hbm,
+    ghost_hbm,
     xl_ref,
     xr_ref,
     out_hbm,
@@ -666,6 +677,7 @@
     sems,
     in_sems,
     avg_sems,
+    ghost_sem,
     *,
     slots,
 ):
@@ -687,10 +699,10 @@
             )
         ]
 
+    take_ghost = pltpu.make_async_copy(ghost_hbm, ghost_ref, ghost_sem)
+    take_ghost.start()
     start_all(loads(0))
     clear_pads(first, FIELD_ROWS)
-    for tile in range(TILES):
-        ghost_ref[:, tile * LANES : (tile + 1) * LANES] = ghost_table(tile)
     plane_ref[...] = plane_table()
     mean_ref[...] = mean_table()
 
@@ -714,6 +726,7 @@
         for slot in range(slots)
     ]
     ghost_rows = 2 * SPECIES * FZ
+    take_ghost.wait()
     for pair in range(TILES // 2):
         cols = slice(2 * pair * LANES, 2 * (pair + 1) * LANES)
         for slot in range(slots):
@@ -1013,13 +1026,15 @@
     kept = [hbm32(slots * size, LANES) for size in (FIELD_ROWS, COEFF_ROWS, UPWARD_ROWS)]
     kept_scratch = [pltpu.VMEM((slots * size, LANES), jnp.float32)
         for size in (FIELD_ROWS, COEFF_ROWS, UPWARD_ROWS)]
-    fields, coeffs, upward = pl.pallas_call(
+    table = (2 * LANES, EDGE * EDGE)
+    fields, coeffs, upward, ghost = pl.pallas_call(
         functools.partial(prepare_kernel, slots=slots),
-        out_shape=kept,
+        out_shape=kept + [pltpu.HBM(table, jnp.bfloat16)],
         in_specs=[VMEM] + [HBM] * 3,
-        out_specs=[HBM] * 3,
+        out_specs=[HBM] * 4,
         scratch_shapes=kept_scratch
         + [
+            pltpu.VMEM(table, jnp.bfloat16),
             pltpu.VMEM(fine_state.shape, jnp.float32),
             pltpu.VMEM(fine_kappa.shape, jnp.float32),
             pltpu.VMEM(fine_rate.shape, jnp.float32),
@@ -1027,6 +1042,7 @@
             pltpu.VMEM((slots * UPWARD_ROWS, LANES), jnp.float32),
             pltpu.SemaphoreType.DMA((3, slots)),
             pltpu.SemaphoreType.DMA((3, slots)),
+            pltpu.SemaphoreType.DMA,
         ],
         compiler_params=PARAMS,
         name="prepare",
@@ -1036,7 +1052,7 @@
     fine_out, averages = pl.pallas_call(
         functools.partial(finish_kernel, slots=slots),
         out_shape=[hbm32(*fine_state.shape), hbm32(af_count, *chunk)],
-        in_specs=[VMEM] + [HBM] * 3 + [VMEM] * 2,
+        in_specs=[VMEM] + [HBM] * 4 + [VMEM] * 2,
         out_specs=[HBM] * 2,
         scratch_shapes=kept_scratch
         + [
@@ -1051,10 +1067,11 @@
             pltpu.SemaphoreType.DMA((slots,)),
             pltpu.SemaphoreType.DMA((3, slots)),
             pltpu.SemaphoreType.DMA((af_count,)),
+            pltpu.SemaphoreType.DMA,
         ],
         compiler_params=PARAMS,
         name="finish",
-    )(strips, *pinned(fields, coeffs, upward), xl, xr)
+    )(strips, *pinned(fields, coeffs, upward, ghost), xl, xr)
 
     arrived = exchange(averages)
 

time: 47.9 us -> 48.5 us (1.013)
  Pallas kernels: 20.9 us -> 21.4 us
    pallas_call x1, Pallas kernels: 8.29 us -> 9.01 us  [per_device(): pl.pallas_call(functools.partial(finish_kernel, slots=slots), out_shape=[...]
where the time goes in v9:
time: 48.5 us; the launch traced here: 47.9 us
  starting transfers between devices  23.5 us (48%)
  Pallas kernels  21.4 us (44%)
  waiting for transfers between devices  2.27 us (5%)
  between operations  0.73 us (2%)
    all_to_all x2, starting transfers between devices, exchange(): return lax.all_to_all(chunks, 'af', split_axis=0, concat_axis=0, tiled=True)  13.9 us
    ppermute x4, starting transfers between devices, shifted(): return lax.ppermute(values, axis, pairs)  9.53 us
    pallas_call x1, Pallas kernels, per_device(): pl.pallas_call(functools.partial(finish_kernel, slots=slots), out_shape=[...  9.01 us
    pallas_call x1, Pallas kernels, per_device(): pl.pallas_call(functools.partial(prepare_kernel, slots=slots), out_shape=...  6.38 us
    pallas_call x1, Pallas kernels, per_device(): pl.pallas_call(functools.partial(strips_kernel, slots=slots, **sizes), ou...  3.63 us
    all_to_all x2, waiting for transfers between devices, exchange(): return lax.all_to_all(chunks, 'af', split_axis=0, concat_axis=0, tiled=True)  1.47 us
    pallas_call x1, Pallas kernels, per_device(): pl.pallas_call(functools.partial(place_kernel, slots=slots, **sizes), out...  1.21 us
    pallas_call x1, Pallas kernels, per_device(): pl.pallas_call(functools.partial(edges_kernel, cells_x=cells_x, cells_y=c...  1.17 us
  transfers between devices with their start and end apart: 6, of which 2 were waited for; matrix products, arithmetic and copies ran while one was open for 0% of the time, Pallas kernels for 16%

profile of v9, /device:TPU:0, one launch (start us, length us, event | category | flops | bytes accessed | tf_op | source)
XLA Modules:
  0.0 47.9 jit_solution(16560134373871844763)
XLA Ops:
  0.6 3.6 %strips.1 = (f32[384,256]{1,0:T(8,128)}, f32[8,64,128]{2,1,0:T(8,128)}, s32[16,256]{1,0:T(8,128)S(1)}, f32[32,256]{1,0:T(8,128)S(1)}, f32[32,256]{1,0:T(8,128)S(...) custom-call(s32[2,128]{1,0:T(2,128)} %bitcast.9, f32[384,256]{1,0:T(8,128)} %bitcast.5, f32[128,256]{1,0:T(8,128)} %bitcast.7, ...), custom_call_target="tpu_custom_call" | custom-call | tf_op jit(solution)/shard_map/strips/pallas_call | solution.py:979
  4.3 7.3 %all-to-all-start = ((f32[8,64,128]{2,1,0:T(8,128)}), f32[8,64,128]{2,1,0:T(8,128)S(1)}, u32[]{:S(2)}, u32[]{:S(2)}) async-start(f32[8,64,128]{2,1,0:T(8,128)} %get-tuple-element.18), calls=%async_computation | async-start | bytes 524288 | tf_op jit(solution)/shard_map/all_to_all | solution.py:962
  11.6 3.9 %collective-permute-start = (f32[32,256]{1,0:T(8,128)S(1)}, f32[32,256]{1,0:T(8,128)S(1)}, u32[]{:S(2)}, u32[]{:S(2)}) collective-permute-start(f32[32,256]{1,0:T(8,128)S(1)} %get-tuple-element.26), channel_id=1, source_target_pairs={{0,1},{1,2},{2,3},{3,4},{4,5},{5,6},{6,7},{8,9},{9,10},{10,11},{11... | collective-permute-start | bytes 98312 | tf_op jit(solution)/shard_map/ppermute | solution.py:958
  15.5 1.3 %collective-permute-start.1 = (f32[32,256]{1,0:T(8,128)S(1)}, f32[32,256]{1,0:T(8,128)S(1)}, u32[]{:S(2)}, u32[]{:S(2)}) collective-permute-start(f32[32,256]{1,0:T(8,128)S(1)} %get-tuple-element.21.after_ref), channel_id=1, source_target_pairs={{1,0},{2,1},{3,2},{4,3},{5,4},{6,5},{7,6},{9,8},{10,9},{11,10},{12... | collective-permute-start | bytes 98312 | tf_op jit(solution)/shard_map/ppermute | solution.py:958
  16.8 6.4 %prepare.1 = (f32[3872,128]{1,0:T(8,128)}, f32[8192,128]{1,0:T(8,128)}, f32[1312,128]{1,0:T(8,128)}, bf16[256,1024]{1,0:T(8,128)(2,1)}) custom-call(f32[32,256]{1,0:T(8,128)S(1)} %get-tuple-element.21.after_ref, f32[4,3,32,1024]{3,2,1,0:T(8,128)} %state_hbm.1, f32[4,32,1024]{2,1,0:T(8,128)} %kappa_hbm.1, f32[4,32,1024]{2,1,0:T(8,128)} %rate_hbm.1), custom_call_target="tpu_custom_call" | custom-call | tf_op jit(solution)/shard_map/prepare/pallas_call | solution.py:1030
  23.2 0.0 collective-permute-done.xl_ref
  23.2 0.0 collective-permute-done.1.xr_ref
  23.2 0.0 all-to-all-done.strips_ref
  23.2 9.0 %finish.1 = (f32[4,3,32,1024]{3,2,1,0:T(8,128)}, f32[8,48,128]{2,1,0:T(8,128)}) custom-call(f32[8,64,128]{2,1,0:T(8,128)S(1)} %all-to-all-done.strips_ref, f32[3872,128]{1,0:T(8,128)} %get-tuple-element.22.fields_hbm, f32[8192,128]{1,0:T(8,128)} %get-tuple-element.23.coeffs_hbm, f32[1312,128]{1,0:T(8,128)} %get-tuple-element.24.upward_hbm, ...), custom_call_target="tpu_custom_call" | custom-call | tf_op jit(solution)/shard_map/finish/pallas_call | solution.py:1052
  32.2 6.6 %all-to-all-start.1 = ((f32[8,48,128]{2,1,0:T(8,128)}), f32[8,48,128]{2,1,0:T(8,128)S(1)}, u32[]{:S(2)}, u32[]{:S(2)}) async-start(f32[8,48,128]{2,1,0:T(8,128)} %get-tuple-element.27), calls=%async_computation.1 | async-start | bytes 393216 | tf_op jit(solution)/shard_map/all_to_all | solution.py:962
  38.9 1.3 %collective-permute-start.3 = (f32[16,128]{1,0:T(8,128)S(1)}, f32[16,128]{1,0:T(8,128)S(1)}, u32[]{:S(2)}, u32[]{:S(2)}) collective-permute-start(f32[16,128]{1,0:T(8,128)S(1)} %get-tuple-element.29.ylo_ref), channel_id=1, source_target_pairs={{8,0},{16,8},{24,16},{9,1},{17,9},{25,17},{10,2},{18,10},{26,18},{... | collective-permute-start | bytes 24584 | tf_op jit(solution)/shard_map/ppermute | solution.py:958
  40.2 3.0 %collective-permute-start.2 = (f32[16,128]{1,0:T(8,128)S(1)}, f32[16,128]{1,0:T(8,128)S(1)}, u32[]{:S(2)}, u32[]{:S(2)}) collective-permute-start(f32[16,128]{1,0:T(8,128)S(1)} %get-tuple-element.30.yhi_ref), channel_id=1, source_target_pairs={{0,8},{8,16},{16,24},{1,9},{9,17},{17,25},{2,10},{10,18},{18,26},{... | collective-permute-start | bytes 24584 | tf_op jit(solution)/shard_map/ppermute | solution.py:958
  43.2 0.0 collective-permute-done.3.yr_ref
  43.2 0.8 %collective-permute-done.2.yl_ref = f32[16,128]{1,0:T(8,128)S(1)} collective-permute-done((f32[16,128]{1,0:T(8,128)S(1)}, f32[16,128]{1,0:T(8,128)S(1)}, u32[]{:S(2)}, u32[]{:S(2)}) %collective-permute-start.2) | collective-permute-done | bytes 8224 | tf_op jit(solution)/shard_map/ppermute | solution.py:958
  44.0 1.2 %edges.1.new_ref = f32[384,256]{1,0:T(8,128)S(1)} custom-call(f32[384,256]{1,0:T(8,128)} %get-tuple-element.28.new_hbm, f32[32,256]{1,0:T(8,128)S(1)} %get-tuple-element.19.low_ref.xlo_ref, f32[32,256]{1,0:T(8,128)S(1)} %get-tuple-element.20.high_ref.xhi_ref, f32[16,128]{1,0:T(8,128)S(1)} %get-tuple-element.29.ylo_ref, ...), custom_call_target="tpu_custom_call" | custom-call | tf_op jit(solution)/shard_map/edges/pallas_call | solution.py:1080
  45.2 1.5 %all-to-all-done.1.avg_ref = f32[8,48,128]{2,1,0:T(8,128)S(1)} async-done(((f32[8,48,128]{2,1,0:T(8,128)}), f32[8,48,128]{2,1,0:T(8,128)S(1)}, u32[]{:S(2)}, u32[]{:S(2)}) %all-to-all-start.1) | async-done | bytes 196640 | tf_op jit(solution)/shard_map/all_to_all | solution.py:962
  46.7 1.2 %place.1 = f32[384,256]{1,0:T(8,128)} custom-call(s32[16,256]{1,0:T(8,128)S(1)} %get-tuple-element.17.place_ref, f32[8,48,128]{2,1,0:T(8,128)S(1)} %all-to-all-done.1.avg_ref, f32[384,256]{1,0:T(8,128)S(1)} %edges.1.new_ref), custom_call_target="tpu_custom_call" | custom-call | tf_op jit(solution)/shard_map/place/pallas_call | solution.py:1090
  (1 shorter events, 0.0 us)
Async XLA Ops:
  4.3 18.9 %all-to-all-start = ((f32[8,64,128]{2,1,0:T(8,128)}), f32[8,64,128]{2,1,0:T(8,128)S(1)}, u32[]{:S(2)}, u32[]{:S(2)}) async-start(f32[8,64,128]{2,1,0:T(8,128)} %get-tuple-element.18), calls=%async_computation | async-start | bytes 524288 | tf_op jit(solution)/shard_map/all_to_all | solution.py:962
  11.6 11.6 %collective-permute-start = (f32[32,256]{1,0:T(8,128)S(1)}, f32[32,256]{1,0:T(8,128)S(1)}, u32[]{:S(2)}, u32[]{:S(2)}) collective-permute-start(f32[32,256]{1,0:T(8,128)S(1)} %get-tuple-element.26), channel_id=1, source_target_pairs={{0,1},{1,2},{2,3},{3,4},{4,5},{5,6},{6,7},{8,9},{9,10},{10,11},{11... | collective-permute-start | bytes 98312 | tf_op jit(solution)/shard_map/ppermute | solution.py:958
  15.5 7.7 %collective-permute-start.1 = (f32[32,256]{1,0:T(8,128)S(1)}, f32[32,256]{1,0:T(8,128)S(1)}, u32[]{:S(2)}, u32[]{:S(2)}) collective-permute-start(f32[32,256]{1,0:T(8,128)S(1)} %get-tuple-element.21.after_ref), channel_id=1, source_target_pairs={{1,0},{2,1},{3,2},{4,3},{5,4},{6,5},{7,6},{9,8},{10,9},{11,10},{12... | collective-permute-start | bytes 98312 | tf_op jit(solution)/shard_map/ppermute | solution.py:958
  32.2 14.4 %all-to-all-start.1 = ((f32[8,48,128]{2,1,0:T(8,128)}), f32[8,48,128]{2,1,0:T(8,128)S(1)}, u32[]{:S(2)}, u32[]{:S(2)}) async-start(f32[8,48,128]{2,1,0:T(8,128)} %get-tuple-element.27), calls=%async_computation.1 | async-start | bytes 393216 | tf_op jit(solution)/shard_map/all_to_all | solution.py:962
  38.9 4.3 %collective-permute-start.3 = (f32[16,128]{1,0:T(8,128)S(1)}, f32[16,128]{1,0:T(8,128)S(1)}, u32[]{:S(2)}, u32[]{:S(2)}) collective-permute-start(f32[16,128]{1,0:T(8,128)S(1)} %get-tuple-element.29.ylo_ref), channel_id=1, source_target_pairs={{8,0},{16,8},{24,16},{9,1},{17,9},{25,17},{10,2},{18,10},{26,18},{... | collective-permute-start | bytes 24584 | tf_op jit(solution)/shard_map/ppermute | solution.py:958
  40.2 3.8 %collective-permute-start.2 = (f32[16,128]{1,0:T(8,128)S(1)}, f32[16,128]{1,0:T(8,128)S(1)}, u32[]{:S(2)}, u32[]{:S(2)}) collective-permute-start(f32[16,128]{1,0:T(8,128)S(1)} %get-tuple-element.30.yhi_ref), channel_id=1, source_target_pairs={{0,8},{8,16},{16,24},{1,9},{9,17},{17,25},{2,10},{10,18},{18,26},{... | collective-permute-start | bytes 24584 | tf_op jit(solution)/shard_map/ppermute | solution.py:958
